TPU v7x, 512 devices: a whole 4x4x16 slice. The times are simulated.
512 devices in a mesh: gx: 32 (over z, core), gy: 4 (over x), gz: 4 (over y).
Axes of the slice: x: 4, y: 4, z: 16, core: 2. Of those that a mesh axis runs over, the one named last changes fastest.
Arguments:
- fluid_temp: float32 [512, 256, 512], P('gx', 'gy', 'gz'), may hold values from -6 to 6
- liquid: int32 [512, 256, 512], P('gx', 'gy', 'gz'), may hold values 0 or 1
- face_src: int32 [1024, 4, 4, 128], P('gx', 'gy', 'gz'), may hold values from -1 to 131071, as said below
- face_dst: int32 [1024, 4, 4, 128], P('gx', 'gy', 'gz'), may hold values from -1 to 1023, as said below
- solid_old: float32 [16, 256, 128], P(('gy', 'gz'), 'gx'), may hold values from -6 to 6
- solid_diag: float32 [16, 256, 128], P(('gy', 'gz'), 'gx'), may hold values from 4 to 16
- blocks: float32 [16, 256, 5, 128, 128], P(('gy', 'gz'), 'gx'), may hold values from -0.25 to 0.25
- pattern: int32 [16, 256, 5], P(('gy', 'gz'), 'gx'), may hold values 0 or 1
Outputs:
- fluid_new: float32 [512, 256, 512], P('gx', 'gy', 'gz')
- solid_temp: float32 [16, 256, 128], P(('gy', 'gz'), 'gx')
Inputs may be any that keep to these rules, and one draw needn't show every extreme that they name: `face_src`: entry q * 32 + r of slab (a, b) lists in its first c slots local cells of brick (q, a, b) whose temperatures go to run r, c from 1 to 128 and 128 in some blocks of every draw; the other slots hold -1; cells may repeat. `face_dst`: entry r * 32 + q of slab (a, b) names, slot by slot, the local solid cell of run r that receives the matching slot of face_src entry q * 32 + r, and -1 exactly where that slot of face_src is -1; cells may repeat.
All inputs are finite; a program needn't handle non-finite values. No bound on the sum of `liquid` or of `pattern` on one device may be relied on, other than what follows from the above.
Results may differ from a plain program's by a relative error of at most 0.00014.
Values sent between devices are 32-bit elements; how exact they have to be, the bound alone decides.
No kernel may reach another device: no remote copies, remote signals or barrier semaphores. Data moves between devices by JAX's collectives and lax.ppermute only.
A program may use at most 64 MiB of HBM per device.

v0:
```python
import math

import jax
import jax.numpy as jnp
from jax import lax
from jax.sharding import PartitionSpec as P

REACH = 2
SWEEPS = 4
NB = 5


DIFFUSION = 0.12
EVAPORATION = 0.5
SATURATION = 0.25
WALL_COUPLING = 0.2


def padded_2(shard, sides, width, wrap):
    for axis, dim in sides:
        peers, length = (lax.axis_size(axis), shard.shape[dim])
        up = [(i, (i + 1) % peers) for i in range(peers if wrap else peers - 1)]
        down = [(j, i) for i, j in up]
        last = lax.slice_in_dim(shard, length - width, length, axis=dim)
        leading = lax.slice_in_dim(shard, 0, width, axis=dim)
        before = lax.ppermute(last, axis, up)
        after = lax.ppermute(leading, axis, down)
        shard = jnp.concatenate([before, shard, after], axis=dim)
    return shard


def apply_tiles(values, blocks_run, pattern_run, diagonal):
    tile_count = values.shape[0]
    padded = padded_2(values, (("gx", 0),), REACH, False)
    neighbours = jnp.stack([padded[offset : offset + tile_count] for offset in range(NB)], axis=1)
    neighbours = neighbours * pattern_run[:, :, None]
    coupled = jnp.einsum("tjab,tjb->ta", blocks_run, neighbours, precision=lax.Precision.HIGHEST)
    return diagonal * values + coupled


def chebyshev(right_side, blocks_run, pattern_run, diagonal):
    inverse = 1.0 / diagonal
    iterate = inverse * right_side
    residual = right_side - apply_tiles(iterate, blocks_run, pattern_run, diagonal)
    update = inverse * residual
    iterate = iterate + update
    rho_old = 0.5
    for sweep in range(1, SWEEPS):
        rho_next = 1.0 / (4.0 - rho_old)
        residual = right_side - apply_tiles(iterate, blocks_run, pattern_run, diagonal)
        update = rho_next * rho_old * update + 4.0 * rho_next * inverse * residual
        iterate = iterate + update
        rho_old = rho_next
    return iterate


def slot_hots(block_ids, row_count, width):
    valid = block_ids >= 0
    row_id = jnp.where(valid, block_ids // width, -1)
    depth = jnp.where(valid, block_ids % width, -1)
    row_hot = (row_id[:, None] == jnp.arange(row_count, dtype=jnp.int32)[None, :]).astype(
        jnp.float32
    )
    depth_hot = depth[:, None] == jnp.arange(width, dtype=jnp.int32)[None, :]
    return (row_hot, depth_hot)


def block_size(total):
    return math.gcd(total, 512)


def pick_cells(table, slot_ids):
    row_count, width = table.shape
    size = block_size(slot_ids.shape[0])

    def pick_one_block(block_ids):
        row_hot, depth_hot = slot_hots(block_ids, row_count, width)
        picked = jnp.dot(
            row_hot, table, precision=lax.Precision.HIGHEST, preferred_element_type=jnp.float32
        )
        return jnp.sum(jnp.where(depth_hot, picked, 0.0), axis=1)

    return lax.map(pick_one_block, slot_ids.reshape(-1, size)).reshape(-1)


def spread_cells(values, slot_ids, row_count, width):
    size = block_size(slot_ids.shape[0])

    def spread_one_block(total, operands):
        block_ids, block_values = operands
        row_hot, depth_hot = slot_hots(block_ids, row_count, width)
        placed = jnp.where(depth_hot, block_values[:, None], 0.0)
        added = jnp.dot(
            row_hot.T, placed, precision=lax.Precision.HIGHEST, preferred_element_type=jnp.float32
        )
        return (total + added, None)

    start = jnp.zeros((row_count, width), jnp.float32)
    total, unused = lax.scan(
        spread_one_block, start, (slot_ids.reshape(-1, size), values.reshape(-1, size))
    )
    return total


def per_device(fluid_temp, liquid, face_src, face_dst, solid_old, solid_diag, blocks, pattern):
    senders = lax.axis_size("gx")
    depth_count = fluid_temp.shape[2]
    row_count = fluid_temp.shape[0] * fluid_temp.shape[1]
    padded = padded_2(fluid_temp, (("gx", 0), ("gy", 1), ("gz", 2)), 1, True)
    source_ids = face_src.reshape(-1)
    fluid_table = fluid_temp.reshape(row_count, depth_count)
    outgoing = pick_cells(fluid_table, source_ids).reshape(senders, -1)
    arriving = lax.all_to_all(outgoing, "gx", split_axis=0, concat_axis=0, tiled=True)
    target_ids = face_dst.reshape(-1)
    tile_count = solid_old.shape[1]
    tile_width = solid_old.shape[2]
    gathered = spread_cells(arriving.reshape(-1), target_ids, tile_count, tile_width)
    diagonal = solid_diag[0]
    right_side = diagonal * solid_old[0] + gathered
    iterate = chebyshev(right_side, blocks[0], pattern[0].astype(jnp.float32), diagonal)
    sent_back = pick_cells(iterate, target_ids).reshape(senders, -1)
    returned = lax.all_to_all(sent_back, "gx", split_axis=0, concat_axis=0, tiled=True)
    centre = padded[1:-1, 1:-1, 1:-1]
    laplacian = padded[2:, 1:-1, 1:-1] + padded[:-2, 1:-1, 1:-1]
    laplacian = laplacian + padded[1:-1, 2:, 1:-1] + padded[1:-1, :-2, 1:-1]
    laplacian = laplacian + padded[1:-1, 1:-1, 2:] + padded[1:-1, 1:-1, :-2] - 6.0 * centre
    wall_sum = spread_cells((returned - outgoing).reshape(-1), source_ids, row_count, depth_count)
    wall_sum = wall_sum.reshape(fluid_temp.shape)
    liquid_share = liquid.astype(jnp.float32)
    fluid_new = (
        fluid_temp
        + DIFFUSION * laplacian
        - EVAPORATION * liquid_share * jnp.maximum(fluid_temp - SATURATION, 0.0)
        + WALL_COUPLING * wall_sum
    )
    return (fluid_new, iterate[None])


def solution(mesh):
    return jax.shard_map(
        per_device,
        mesh=mesh,
        in_specs=(
            P("gx", "gy", "gz"),
            P("gx", "gy", "gz"),
            P("gx", "gy", "gz", None),
            P("gx", "gy", "gz", None),
            P(("gy", "gz"), "gx", None),
            P(("gy", "gz"), "gx", None),
            P(("gy", "gz"), "gx", None, None, None),
            P(("gy", "gz"), "gx", None),
        ),
        out_specs=(P("gx", "gy", "gz"), P(("gy", "gz"), "gx", None)),
        check_vma=False,
    )
```

profile of v0, /device:TPU:1, one launch (start us, length us, event | category | flops | bytes accessed | tf_op | source)
XLA Modules:
  0.0 173.6 jit_solution(7902732795825720715)
XLA Ops:
  2.9 20.0 %while.50 = (s32[]{:T(128)}, f32[8,512]{1,0:T(8,128)S(1)}, s32[8,512]{1,0:T(8,128)S(1)}, f32[1024,128]{1,0:T(8,128)}, s32[]{:T(128)}, /*index=5*/s32[]{:T(128)}) while((s32[]{:T(128)}, f32[8,512]{1,0:T(8,128)S(1)}, s32[8,512]{1,0:T(8,128)S(1)}, f32[1024,128]{1,0:T(8,128)}, s32[]{:T(128)}, /*index=5*/s32[]{:T(128)}) %tuple.135), condition=%wide.region_2.3_spmd, body=%wide.region_0.2_spmd.sunk | while | flops 806038016 | bytes 544853 | solution.py:83
  23.6 16.8 %all-to-all-start = ((f32[32,1,128]{2,1,0:T(1,128)}), f32[32,1,128]{2,1,0:T(1,128)S(1)}, u32[]{:S(2)}, u32[]{:S(2)}) async-start(f32[32,1,128]{2,1,0:T(1,128)} %all_to_all.14), calls=%async_computation | async-start | bytes 32768 | tf_op jit(solution)/shard_map/all_to_all | solution.py:113
  44.9 7.2 %all-to-all-done = f32[32,1,128]{2,1,0:T(1,128)S(1)} async-done(((f32[32,1,128]{2,1,0:T(1,128)}), f32[32,1,128]{2,1,0:T(1,128)S(1)}, u32[]{:S(2)}, u32[]{:S(2)}) %all-to-all-start) | async-done | bytes 16416 | tf_op jit(solution)/shard_map/all_to_all | solution.py:113
  53.2 5.5 %while.52 = (s32[]{:T(128)}, f32[8,128]{1,0:T(8,128)S(1)}, s32[8,512]{1,0:T(8,128)S(1)}, f32[8,512]{1,0:T(8,128)S(1)}, s32[]{:T(128)}, /*index=5*/s32[]{:T(128)}) while((s32[]{:T(128)}, f32[8,128]{1,0:T(8,128)S(1)}, s32[8,512]{1,0:T(8,128)S(1)}, f32[8,512]{1,0:T(8,128)S(1)}, s32[]{:T(128)}, /*index=5*/s32[]{:T(128)}) %tuple.126), condition=%wide.region_4.5_spmd.clone, body=%wide.region_3.4_spmd.clone.sunk | while | flops 6439939 | bytes 28767 | solution.py:99
  58.7 3.0 %collective-permute-start.6 = (f32[2,128]{1,0:T(2,128)S(1)}, f32[2,128]{1,0:T(2,128)S(1)}, u32[]{:S(2)}, u32[]{:S(2)}) collective-permute-start(f32[2,128]{1,0:T(2,128)S(1)} %get-tuple-element.319), channel_id=1, source_target_pairs={{0,16},{16,32},{32,48},{48,64},{64,80},{80,96},{96,112},{112,128},... | collective-permute-start | bytes 3080 | tf_op jit(solution)/shard_map/ppermute | solution.py:26
  64.8 2.9 %collective-permute-done.7 = f32[2,128]{1,0:T(2,128)S(1)} collective-permute-done((f32[2,128]{1,0:T(2,128)S(1)}, f32[2,128]{1,0:T(2,128)S(1)}, u32[]{:S(2)}, u32[]{:S(2)}) %collective-permute-start.7) | collective-permute-done | bytes 1056 | tf_op jit(solution)/shard_map/ppermute | solution.py:27
  82.0 3.1 %collective-permute-start.3 = (f32[18,1,128]{2,1,0:T(1,128)S(1)}, f32[18,1,128]{2,1,0:T(1,128)S(1)}, u32[]{:S(2)}, u32[]{:S(2)}) collective-permute-start(f32[18,1,128]{2,1,0:T(1,128)S(1)} %get-tuple-element.308), channel_id=1, source_target_pairs={{0,4},{4,8},{8,12},{12,0},{1,5},{5,9},{9,13},{13,1},{2,6},{6,10},{... | collective-permute-start | bytes 27656 | tf_op jit(solution)/shard_map/ppermute | solution.py:26
  85.1 3.4 %collective-permute-start.2 = (f32[18,1,128]{2,1,0:T(1,128)S(1)}, f32[18,1,128]{2,1,0:T(1,128)S(1)}, u32[]{:S(2)}, u32[]{:S(2)}) collective-permute-start(f32[18,1,128]{2,1,0:T(1,128)S(1)} %get-tuple-element.309), channel_id=1, source_target_pairs={{4,0},{8,4},{12,8},{0,12},{5,1},{9,5},{13,9},{1,13},{6,2},{10,6},{... | collective-permute-start | bytes 27656 | tf_op jit(solution)/shard_map/ppermute | solution.py:27
  88.5 2.9 %collective-permute-start.11 = (f32[2,128]{1,0:T(2,128)S(1)}, f32[2,128]{1,0:T(2,128)S(1)}, u32[]{:S(2)}, u32[]{:S(2)}) collective-permute-start(f32[2,128]{1,0:T(2,128)S(1)} %get-tuple-element.314), channel_id=1, source_target_pairs={{16,0},{32,16},{48,32},{64,48},{80,64},{96,80},{112,96},{128,112},... | collective-permute-start | bytes 3080 | tf_op jit(solution)/shard_map/ppermute | solution.py:27
  104.3 2.6 %fusion.32 = f32[8,1,128,1]{2,1,3,0:T(1,128)S(1)} fusion(f32[1,8,5,128,128]{4,3,2,1,0:T(8,128)S(1)} %copy-done, f32[8,5,128,1]{2,0,1,3:T(8,128)S(1)} %multiply_bitcast_fusion), kind=kOutput, calls=%fused_computation.80 | convolution fusion | flops 7864320 | bytes 2646016 | tf_op jit(solution)/shard_map/tjab,tjb->ta/dot_general | solution.py:37
  106.9 4.3 %while.51 = (s32[]{:T(128)}, f32[8,512]{1,0:T(8,128)S(1)}, s32[8,512]{1,0:T(8,128)S(1)}, f32[8,128]{1,0:T(8,128)S(1)}, s32[]{:T(128)}, /*index=5*/s32[]{:T(128)}) while((s32[]{:T(128)}, f32[8,512]{1,0:T(8,128)S(1)}, s32[8,512]{1,0:T(8,128)S(1)}, f32[8,128]{1,0:T(8,128)S(1)}, s32[]{:T(128)}, /*index=5*/s32[]{:T(128)}) %tuple.137), condition=%wide.region_7.8_spmd, body=%wide.region_5.7_spmd.sunk | while | flops 6502914 | bytes 24661 | solution.py:83
  111.9 10.2 %all-to-all-start.1 = ((f32[32,1,128]{2,1,0:T(1,128)}), f32[32,1,128]{2,1,0:T(1,128)S(1)}, u32[]{:S(2)}, u32[]{:S(2)}) async-start(f32[32,1,128]{2,1,0:T(1,128)} %all_to_all.16), calls=%async_computation.1 | async-start | bytes 32768 | tf_op jit(solution)/shard_map/all_to_all | solution.py:122
  124.8 4.7 %collective-permute-start.4 = (f32[18,66,1]{1,0,2:T(8,128)S(1)}, f32[18,66,1]{1,0,2:T(8,128)S(1)}, u32[]{:S(2)}, u32[]{:S(2)}) collective-permute-start(f32[18,66,1]{1,0,2:T(8,128)S(1)} %copy.25), channel_id=1, source_target_pairs={{1,0},{2,1},{3,2},{0,3},{5,4},{6,5},{7,6},{4,7},{9,8},{10,9},{11,1... | collective-permute-start | bytes 14264 | tf_op jit(solution)/shard_map/ppermute | solution.py:27
  133.1 3.4 %collective-permute-done.5 = f32[18,66,1]{1,0,2:T(8,128)S(1)} collective-permute-done((f32[18,66,1]{1,0,2:T(8,128)S(1)}, f32[18,66,1]{1,0,2:T(8,128)S(1)}, u32[]{:S(2)}, u32[]{:S(2)}) %collective-permute-start.5) | collective-permute-done | bytes 4784 | tf_op jit(solution)/shard_map/ppermute | solution.py:26
  138.3 30.3 %while.53 = (s32[]{:T(128)}, f32[1024,128]{1,0:T(8,128)}, s32[8,512]{1,0:T(8,128)S(1)}, f32[8,512]{1,0:T(8,128)S(1)}, s32[]{:T(128)}, /*index=5*/s32[]{:T(128)}) while((s32[]{:T(128)}, f32[1024,128]{1,0:T(8,128)}, s32[8,512]{1,0:T(8,128)S(1)}, f32[8,512]{1,0:T(8,128)S(1)}, s32[]{:T(128)}, /*index=5*/s32[]{:T(128)}) %tuple.136), condition=%wide.region_9.10_spmd.clone, body=%wide.region_8.9_spmd.clone.sunk | while | flops 806235136 | bytes 1069151 | solution.py:99
  138.4 2.8 %fusion.131 = f32[1024,128]{1,0:T(8,128)} fusion(s32[512]{0:T(512)S(1)} %get-tuple-element.434, f32[1024,128]{1,0:T(8,128)} %get-tuple-element.497, pred[]{:T(512)S(6)} %compare.55, f32[512]{0:T(512)S(1)} %bitcast.216, s32[512]{0:T(512)S(1)} %get-tuple-element.435), kind=kOutput, calls=%fused_computation.59.clone.1 | convolution fusion | flops 806223872 | bytes 1054721 | tf_op jit(solution)/shard_map/while/body/eval_jaxpr/dot_general | solution.py:93
  141.3 3.9 %fusion.131 = f32[1024,128]{1,0:T(8,128)} fusion(s32[512]{0:T(512)S(1)} %get-tuple-element.434, f32[1024,128]{1,0:T(8,128)} %get-tuple-element.497, pred[]{:T(512)S(6)} %compare.55, f32[512]{0:T(512)S(1)} %bitcast.216, s32[512]{0:T(512)S(1)} %get-tuple-element.435), kind=kOutput, calls=%fused_computation.59.clone.1 | convolution fusion | flops 806223872 | bytes 1054721 | tf_op jit(solution)/shard_map/while/body/eval_jaxpr/dot_general | solution.py:93
  145.2 3.9 %fusion.131 = f32[1024,128]{1,0:T(8,128)} fusion(s32[512]{0:T(512)S(1)} %get-tuple-element.434, f32[1024,128]{1,0:T(8,128)} %get-tuple-element.497, pred[]{:T(512)S(6)} %compare.55, f32[512]{0:T(512)S(1)} %bitcast.216, s32[512]{0:T(512)S(1)} %get-tuple-element.435), kind=kOutput, calls=%fused_computation.59.clone.1 | convolution fusion | flops 806223872 | bytes 1054721 | tf_op jit(solution)/shard_map/while/body/eval_jaxpr/dot_general | solution.py:93
  149.1 3.9 %fusion.131 = f32[1024,128]{1,0:T(8,128)} fusion(s32[512]{0:T(512)S(1)} %get-tuple-element.434, f32[1024,128]{1,0:T(8,128)} %get-tuple-element.497, pred[]{:T(512)S(6)} %compare.55, f32[512]{0:T(512)S(1)} %bitcast.216, s32[512]{0:T(512)S(1)} %get-tuple-element.435), kind=kOutput, calls=%fused_computation.59.clone.1 | convolution fusion | flops 806223872 | bytes 1054721 | tf_op jit(solution)/shard_map/while/body/eval_jaxpr/dot_general | solution.py:93
  153.0 3.9 %fusion.131 = f32[1024,128]{1,0:T(8,128)} fusion(s32[512]{0:T(512)S(1)} %get-tuple-element.434, f32[1024,128]{1,0:T(8,128)} %get-tuple-element.497, pred[]{:T(512)S(6)} %compare.55, f32[512]{0:T(512)S(1)} %bitcast.216, s32[512]{0:T(512)S(1)} %get-tuple-element.435), kind=kOutput, calls=%fused_computation.59.clone.1 | convolution fusion | flops 806223872 | bytes 1054721 | tf_op jit(solution)/shard_map/while/body/eval_jaxpr/dot_general | solution.py:93
  156.9 3.9 %fusion.131 = f32[1024,128]{1,0:T(8,128)} fusion(s32[512]{0:T(512)S(1)} %get-tuple-element.434, f32[1024,128]{1,0:T(8,128)} %get-tuple-element.497, pred[]{:T(512)S(6)} %compare.55, f32[512]{0:T(512)S(1)} %bitcast.216, s32[512]{0:T(512)S(1)} %get-tuple-element.435), kind=kOutput, calls=%fused_computation.59.clone.1 | convolution fusion | flops 806223872 | bytes 1054721 | tf_op jit(solution)/shard_map/while/body/eval_jaxpr/dot_general | solution.py:93
  160.8 3.9 %fusion.131 = f32[1024,128]{1,0:T(8,128)} fusion(s32[512]{0:T(512)S(1)} %get-tuple-element.434, f32[1024,128]{1,0:T(8,128)} %get-tuple-element.497, pred[]{:T(512)S(6)} %compare.55, f32[512]{0:T(512)S(1)} %bitcast.216, s32[512]{0:T(512)S(1)} %get-tuple-element.435), kind=kOutput, calls=%fused_computation.59.clone.1 | convolution fusion | flops 806223872 | bytes 1054721 | tf_op jit(solution)/shard_map/while/body/eval_jaxpr/dot_general | solution.py:93
  164.7 3.9 %fusion.131 = f32[1024,128]{1,0:T(8,128)} fusion(s32[512]{0:T(512)S(1)} %get-tuple-element.434, f32[1024,128]{1,0:T(8,128)} %get-tuple-element.497, pred[]{:T(512)S(6)} %compare.55, f32[512]{0:T(512)S(1)} %bitcast.216, s32[512]{0:T(512)S(1)} %get-tuple-element.435), kind=kOutput, calls=%fused_computation.59.clone.1 | convolution fusion | flops 806223872 | bytes 1054721 | tf_op jit(solution)/shard_map/while/body/eval_jaxpr/dot_general | solution.py:93
  169.7 4.0 %fusion.45 = f32[16,64,128]{2,1,0:T(8,128)} fusion(f32[16,64,128]{2,1,0:T(8,128)S(1)} %bitcast.210, f32[16,64,128]{2,1,0:T(8,128)} %bitcast.209, f32[18,66,1]{2,1,0:T(8,128)} %copy.28, f32[18,1,128]{2,1,0:T(1,128)S(1)} %collective-permute-done.2, f32[18,64,128]{2,1,0:T(8,128)} %copy-done.1, f32[18,1,128]{2,1,0:T(1,128)S(1)} %collective-permute-done.3, ...), kind=kLoop, calls=%fused_computation.95 | loop fusion | flops 3407872 | bytes 2780448 | tf_op jit(solution)/shard_map/add | solution.py:131
  (224 shorter events, 77.7 us)
Async XLA Ops:
  0.6 67.1 %copy-start = (f32[1,8,5,128,128]{4,3,2,1,0:T(8,128)S(1)}, f32[1,8,5,128,128]{4,3,2,1,0:T(8,128)}, u32[]{:S(2)}) copy-start(f32[1,8,5,128,128]{4,3,2,1,0:T(8,128)} %param.22) | copy-start | bytes 7864324
  2.9 40.0 %copy-start.6 = (s32[1,8,5]{1,0,2:T(1,128)S(1)}, s32[1,8,5]{1,0,2:T(1,128)}, u32[]{:S(2)}) copy-start(s32[1,8,5]{1,0,2:T(1,128)} %param.23) | copy-start | bytes 484
  2.9 40.1 %copy-start.3 = (s32[32,1,1,128]{3,2,1,0:T(1,128)S(1)}, s32[32,1,1,128]{3,2,1,0:T(1,128)}, u32[]{:S(2)}) copy-start(s32[32,1,1,128]{3,2,1,0:T(1,128)} %param.19) | copy-start | bytes 49156
  2.9 55.7 %copy-start.2 = (f32[1,8,128]{2,1,0:T(8,128)S(1)}, f32[1,8,128]{2,1,0:T(8,128)}, u32[]{:S(2)}) copy-start(f32[1,8,128]{2,1,0:T(8,128)} %param.21) | copy-start | bytes 12292
  2.9 55.7 %copy-start.4 = (f32[1,8,128]{2,1,0:T(8,128)S(1)}, f32[1,8,128]{2,1,0:T(8,128)}, u32[]{:S(2)}) copy-start(f32[1,8,128]{2,1,0:T(8,128)} %param.20) | copy-start | bytes 12292
  23.6 28.5 %all-to-all-start = ((f32[32,1,128]{2,1,0:T(1,128)}), f32[32,1,128]{2,1,0:T(1,128)S(1)}, u32[]{:S(2)}, u32[]{:S(2)}) async-start(f32[32,1,128]{2,1,0:T(1,128)} %all_to_all.14), calls=%async_computation | async-start | bytes 32768 | tf_op jit(solution)/shard_map/all_to_all | solution.py:113
  41.1 31.2 %collective-permute-start = (f32[1,64,128]{2,1,0:T(8,128)S(1)}, f32[1,64,128]{2,1,0:T(8,128)S(1)}, u32[]{:S(2)}, u32[]{:S(2)}) collective-permute-start(f32[1,64,128]{2,1,0:T(8,128)S(1)} %get-tuple-element.310), channel_id=1, source_target_pairs={{16,0},{32,16},{48,32},{64,48},{80,64},{96,80},{112,96},{128,112},... | collective-permute-start | bytes 98312 | tf_op jit(solution)/shard_map/ppermute | solution.py:27
  41.4 3.5 %collective-permute-start.1 = (f32[1,64,128]{2,1,0:T(8,128)S(1)}, f32[1,64,128]{2,1,0:T(8,128)S(1)}, u32[]{:S(2)}, u32[]{:S(2)}) collective-permute-start(f32[1,64,128]{2,1,0:T(8,128)S(1)} %get-tuple-element.311), channel_id=1, source_target_pairs={{0,16},{16,32},{32,48},{48,64},{64,80},{80,96},{96,112},{112,128},... | collective-permute-start | bytes 98312 | tf_op jit(solution)/shard_map/ppermute | solution.py:26
  58.7 6.0 %collective-permute-start.6 = (f32[2,128]{1,0:T(2,128)S(1)}, f32[2,128]{1,0:T(2,128)S(1)}, u32[]{:S(2)}, u32[]{:S(2)}) collective-permute-start(f32[2,128]{1,0:T(2,128)S(1)} %get-tuple-element.319), channel_id=1, source_target_pairs={{0,16},{16,32},{32,48},{48,64},{64,80},{80,96},{96,112},{112,128},... | collective-permute-start | bytes 3080 | tf_op jit(solution)/shard_map/ppermute | solution.py:26
  62.8 4.9 %collective-permute-start.7 = (f32[2,128]{1,0:T(2,128)S(1)}, f32[2,128]{1,0:T(2,128)S(1)}, u32[]{:S(2)}, u32[]{:S(2)}) collective-permute-start(f32[2,128]{1,0:T(2,128)S(1)} %get-tuple-element.318), channel_id=1, source_target_pairs={{16,0},{32,16},{48,32},{64,48},{80,64},{96,80},{112,96},{128,112},... | collective-permute-start | bytes 3080 | tf_op jit(solution)/shard_map/ppermute | solution.py:27
  70.4 4.4 %collective-permute-start.8 = (f32[2,128]{1,0:T(2,128)S(1)}, f32[2,128]{1,0:T(2,128)S(1)}, u32[]{:S(2)}, u32[]{:S(2)}) collective-permute-start(f32[2,128]{1,0:T(2,128)S(1)} %get-tuple-element.317), channel_id=1, source_target_pairs={{0,16},{16,32},{32,48},{48,64},{64,80},{80,96},{96,112},{112,128},... | collective-permute-start | bytes 3080 | tf_op jit(solution)/shard_map/ppermute | solution.py:26
  72.4 23.7 %copy-start.1 = (f32[18,64,128]{2,1,0:T(8,128)}, f32[18,64,128]{2,1,0:T(8,128)S(1)}, u32[]{:S(2)}) copy-start(f32[18,64,128]{2,1,0:T(8,128)S(1)} %constant_dynamic-update-slice_fusion) | copy-start | bytes 1769476
  72.4 4.9 %collective-permute-start.9 = (f32[2,128]{1,0:T(2,128)S(1)}, f32[2,128]{1,0:T(2,128)S(1)}, u32[]{:S(2)}, u32[]{:S(2)}) collective-permute-start(f32[2,128]{1,0:T(2,128)S(1)} %get-tuple-element.316), channel_id=1, source_target_pairs={{16,0},{32,16},{48,32},{64,48},{80,64},{96,80},{112,96},{128,112},... | collective-permute-start | bytes 3080 | tf_op jit(solution)/shard_map/ppermute | solution.py:27
  80.0 11.4 %collective-permute-start.10 = (f32[2,128]{1,0:T(2,128)S(1)}, f32[2,128]{1,0:T(2,128)S(1)}, u32[]{:S(2)}, u32[]{:S(2)}) collective-permute-start(f32[2,128]{1,0:T(2,128)S(1)} %get-tuple-element.315), channel_id=1, source_target_pairs={{0,16},{16,32},{32,48},{48,64},{64,80},{80,96},{96,112},{112,128},... | collective-permute-start | bytes 3080 | tf_op jit(solution)/shard_map/ppermute | solution.py:26
  82.0 16.1 %collective-permute-start.3 = (f32[18,1,128]{2,1,0:T(1,128)S(1)}, f32[18,1,128]{2,1,0:T(1,128)S(1)}, u32[]{:S(2)}, u32[]{:S(2)}) collective-permute-start(f32[18,1,128]{2,1,0:T(1,128)S(1)} %get-tuple-element.308), channel_id=1, source_target_pairs={{0,4},{4,8},{8,12},{12,0},{1,5},{5,9},{9,13},{13,1},{2,6},{6,10},{... | collective-permute-start | bytes 27656 | tf_op jit(solution)/shard_map/ppermute | solution.py:26
  85.1 13.0 %collective-permute-start.2 = (f32[18,1,128]{2,1,0:T(1,128)S(1)}, f32[18,1,128]{2,1,0:T(1,128)S(1)}, u32[]{:S(2)}, u32[]{:S(2)}) collective-permute-start(f32[18,1,128]{2,1,0:T(1,128)S(1)} %get-tuple-element.309), channel_id=1, source_target_pairs={{4,0},{8,4},{12,8},{0,12},{5,1},{9,5},{13,9},{1,13},{6,2},{10,6},{... | collective-permute-start | bytes 27656 | tf_op jit(solution)/shard_map/ppermute | solution.py:27
  88.5 4.9 %collective-permute-start.11 = (f32[2,128]{1,0:T(2,128)S(1)}, f32[2,128]{1,0:T(2,128)S(1)}, u32[]{:S(2)}, u32[]{:S(2)}) collective-permute-start(f32[2,128]{1,0:T(2,128)S(1)} %get-tuple-element.314), channel_id=1, source_target_pairs={{16,0},{32,16},{48,32},{64,48},{80,64},{96,80},{112,96},{128,112},... | collective-permute-start | bytes 3080 | tf_op jit(solution)/shard_map/ppermute | solution.py:27
  96.2 5.7 %collective-permute-start.12 = (f32[2,128]{1,0:T(2,128)S(1)}, f32[2,128]{1,0:T(2,128)S(1)}, u32[]{:S(2)}, u32[]{:S(2)}) collective-permute-start(f32[2,128]{1,0:T(2,128)S(1)} %get-tuple-element.313), channel_id=1, source_target_pairs={{0,16},{16,32},{32,48},{48,64},{64,80},{80,96},{96,112},{112,128},... | collective-permute-start | bytes 3080 | tf_op jit(solution)/shard_map/ppermute | solution.py:26
  99.3 4.9 %collective-permute-start.13 = (f32[2,128]{1,0:T(2,128)S(1)}, f32[2,128]{1,0:T(2,128)S(1)}, u32[]{:S(2)}, u32[]{:S(2)}) collective-permute-start(f32[2,128]{1,0:T(2,128)S(1)} %get-tuple-element.312), channel_id=1, source_target_pairs={{16,0},{32,16},{48,32},{64,48},{80,64},{96,80},{112,96},{128,112},... | collective-permute-start | bytes 3080 | tf_op jit(solution)/shard_map/ppermute | solution.py:27
  111.3 26.4 %copy-start.5 = (f32[8,128]{1,0:T(8,128)}, f32[8,128]{1,0:T(8,128)S(1)}, u32[]{:S(2)}) copy-start(f32[8,128]{1,0:T(8,128)S(1)} %get-tuple-element.533) | copy-start | bytes 12292
  111.9 25.8 %all-to-all-start.1 = ((f32[32,1,128]{2,1,0:T(1,128)}), f32[32,1,128]{2,1,0:T(1,128)S(1)}, u32[]{:S(2)}, u32[]{:S(2)}) async-start(f32[32,1,128]{2,1,0:T(1,128)} %all_to_all.16), calls=%async_computation.1 | async-start | bytes 32768 | tf_op jit(solution)/shard_map/all_to_all | solution.py:122
  124.8 8.0 %collective-permute-start.4 = (f32[18,66,1]{1,0,2:T(8,128)S(1)}, f32[18,66,1]{1,0,2:T(8,128)S(1)}, u32[]{:S(2)}, u32[]{:S(2)}) collective-permute-start(f32[18,66,1]{1,0,2:T(8,128)S(1)} %copy.25), channel_id=1, source_target_pairs={{1,0},{2,1},{3,2},{0,3},{5,4},{6,5},{7,6},{4,7},{9,8},{10,9},{11,1... | collective-permute-start | bytes 14264 | tf_op jit(solution)/shard_map/ppermute | solution.py:27
  130.8 5.7 %collective-permute-start.5 = (f32[18,66,1]{1,0,2:T(8,128)S(1)}, f32[18,66,1]{1,0,2:T(8,128)S(1)}, u32[]{:S(2)}, u32[]{:S(2)}) collective-permute-start(f32[18,66,1]{1,0,2:T(8,128)S(1)} %copy.27), channel_id=1, source_target_pairs={{0,1},{1,2},{2,3},{3,0},{4,5},{5,6},{6,7},{7,4},{8,9},{9,10},{10,1... | collective-permute-start | bytes 14264 | tf_op jit(solution)/shard_map/ppermute | solution.py:26
where the time goes:
time: 175 us; the launch traced here: 174 us
  matrix products  67.9 us (39%)
  starting transfers between devices  60.4 us (35%)
  waiting for transfers between devices  21.2 us (12%)
  local copies, waits for them, and re-layouts  11.5 us (7%)
  other arithmetic  10.6 us (6%)
    dot_general x16, matrix products, spread_one_block(): jnp.dot(row_hot.T, placed, precision=lax.Precision.HIGHEST, preferred_ele...  35 us
    dot_general x16, matrix products, pick_one_block(): jnp.dot(row_hot, table, precision=lax.Precision.HIGHEST, preferred_elemen...  22.4 us
    ppermute x7, starting transfers between devices, padded_2(): after = lax.ppermute(leading, axis, down)  18 us
    all_to_all x1, starting transfers between devices, per_device(): lax.all_to_all(outgoing, 'gx', split_axis=0, concat_axis=0, tiled=True)  16.8 us
    ppermute x7, starting transfers between devices, padded_2(): before = lax.ppermute(last, axis, up)  15.4 us
    dot_general x4, matrix products, apply_tiles(): jnp.einsum('tjab,tjb->ta', blocks_run, neighbours, precision=lax.Precisio...  10.4 us
    all_to_all x1, starting transfers between devices, per_device(): lax.all_to_all(sent_back, 'gx', split_axis=0, concat_axis=0, tiled=True)  10.2 us
    ppermute x7, waiting for transfers between devices, padded_2(): after = lax.ppermute(leading, axis, down)  9.58 us
  transfers between devices with their start and end apart: 16, of which 7 were waited for; matrix products, arithmetic and copies ran while one was open for 12% of the time, Pallas kernels for 0%

commit v1 on v0

v1 whole, which is shorter than its diff:
```python
import functools

import jax
import jax.numpy as jnp
from jax import lax
from jax.experimental import pallas as pl
from jax.experimental.pallas import tpu as pltpu
from jax.sharding import PartitionSpec as P

F32 = jnp.float32
BF16 = jnp.bfloat16
I32 = jnp.int32
RUNS = 32
WIDTH = 128
ROWS = 1024
TILES = 8
NB = 5
WIN = 24

DIFFUSION = 0.12
EVAPORATION = 0.5
SATURATION = 0.25
WALL_COUPLING = 0.2

VMEM = pl.BlockSpec(memory_space=pltpu.VMEM)


def params(mib):
    return pltpu.CompilerParams(vmem_limit_bytes=mib << 20)


def two_parts(values):
    high = values.astype(BF16)
    return high, (values - high.astype(F32)).astype(BF16)


def lanes(rows):
    return jnp.concatenate(rows, axis=1)


def row_hots(row, count):
    width = row.shape[1]
    part = min(count, 256)
    level = lax.broadcasted_iota(I32, (part, width), 0).astype(F32).astype(BF16)
    one, zero = jnp.ones((), BF16), jnp.zeros((), BF16)
    parts = []
    for index in range(count // part):
        here = jnp.where((row >= index * part) & (row < (index + 1) * part), row - index * part, -1)
        parts.append(jnp.where(level == here.astype(F32).astype(BF16), one, zero))
    return parts[0] if len(parts) == 1 else jnp.concatenate(parts, axis=0)


def placed_parts(column, count, values):
    width = column.shape[1]
    mask = lax.broadcasted_iota(I32, (count, width), 0) == column
    high = values.astype(BF16).astype(F32)
    low = values - high
    both = [jnp.where(mask, part, 0.0) for part in (high, low)]
    return jnp.concatenate(both, axis=0).astype(BF16)


CONTRACT_LAST = (((1,), (1,)), ((), ()))


def pick_kernel(fluid, src, dst, old, diag, pattern, sent, outgoing, on_chip, across, y_faces, z_faces, table):
    parity = lax.rem(lax.axis_index("gx"), 2)
    for block in range(8):
        turned = fluid[128 * block : 128 * block + 128, :].T
        z_faces[0, block : block + 1, :] = turned[0:1, :]
        z_faces[1, block : block + 1, :] = turned[127:128, :]
        high, low = two_parts(turned)
        table[0:128, 128 * block : 128 * block + 128] = high
        table[128:256, 128 * block : 128 * block + 128] = low
    for slab in range(16):
        y_faces[0, slab : slab + 1, :] = fluid[64 * slab : 64 * slab + 1, :]
        y_faces[1, slab : slab + 1, :] = fluid[64 * slab + 63 : 64 * slab + 64, :]
    first, last = fluid[0:64, :], fluid[960:1024, :]
    for packed, face in ((on_chip, jnp.where(parity == 0, last, first)), (across, jnp.where(parity == 0, first, last))):
        packed[0:32, :] = dst[...].astype(F32)
        packed[32:40, :] = old[...]
        packed[40:48, :] = diag[...]
        packed[48:56, :] = jnp.zeros((8, WIDTH), F32)
        packed[48:56, 0:NB] = pattern[...].astype(F32)
        packed[56:120, :] = face
    group = 4
    for start in range(0, RUNS, group):
        ids = lanes([src[r : r + 1, :] for r in range(start, start + group)])
        picked = jnp.dot(table[...], row_hots(ids >> 7, ROWS), preferred_element_type=F32)
        both = picked[0:128] + picked[128:256]
        mask = lax.broadcasted_iota(I32, (WIDTH, group * WIDTH), 0) == (ids & 127)
        value = jnp.sum(jnp.where(mask, both, 0.0), axis=0, keepdims=True)
        for r in range(start, start + group):
            mine = value[:, (r - start) * WIDTH : (r - start + 1) * WIDTH]
            outgoing[r : r + 1, :] = mine
            sent[r, :, 0:128] = mine
            sent[r ^ 1, :, 128:256] = mine
            beside = (r + 1) % RUNS if r % 2 else (r - 1) % RUNS
            sent[beside, :, 256:384] = mine


def spread_run(ids_of, values_of):
    group = 8
    total = None
    for start in range(0, RUNS, group):
        cell = lanes([ids_of(r) for r in range(start, start + group)])
        value = lanes([values_of(r) for r in range(start, start + group)])
        row = jnp.where(cell >= 0, ((cell >> 5) & 3) * 8 + (cell >> 7), -1)
        hots = row_hots(row, 32)
        placed = placed_parts(cell & 31, 32, value)
        added = lax.dot_general(hots, placed, CONTRACT_LAST, preferred_element_type=F32)
        total = added if total is None else total + added
    total = total[:, 0:32] + total[:, 32:64]
    return lanes([total[8 * u : 8 * u + 8, :] for u in range(4)])


def window(parity, own, partner, beside):
    pad = jnp.zeros((4, WIDTH), F32)
    low = jnp.concatenate([beside[4:8], own, partner, pad], axis=0)
    high = jnp.concatenate([partner, own, beside[0:4], pad], axis=0)
    return jnp.where(parity == 0, low, high)


def neighbours(iterate, pats, first, count, shifted):
    for offset in range(NB):
        values = iterate[first - 2 + offset : first - 2 + offset + count, :]
        shifted[offset, first : first + count, :] = values * pats[offset, first : first + count, :]


def apply_tile(blocks, tile, shifted, place, coupled):
    total = None
    for offset in range(NB):
        term = blocks[tile, offset] * shifted[offset, pl.ds(place, 1), :]
        total = term if total is None else total + term
    coupled[pl.ds(place, 1), :] = jnp.sum(total.T, axis=0, keepdims=True)


RHO = [0.5]
for _ in range(3):
    RHO.append(1.0 / (4.0 - RHO[-1]))


def wall_first_kernel(
    arrived, dst, old, diag, pattern, on_chip, across, own_blocks, partner_blocks, beside_blocks,
    state, pats, swap, iterate, shifted, coupled,
):
    me = lax.axis_index("gx")
    parity = lax.rem(me, 2)
    at_edge = (me == 0) | (me == RUNS - 1)
    keep = jnp.where(at_edge, 0.0, 1.0)
    added = [
        spread_run(lambda r: dst[r : r + 1, :], lambda r: arrived[r, :, 0:128]),
        spread_run(lambda r: on_chip[r : r + 1, :].astype(I32), lambda r: arrived[r, :, 128:256]),
        spread_run(lambda r: across[r : r + 1, :].astype(I32), lambda r: arrived[r, :, 256:384]),
    ]
    diagonals = [diag[...], on_chip[40:48, :], across[40:48, :]]
    olds = [old[...], on_chip[32:40, :], across[32:40, :]]
    rights = [d * o + a for d, o, a in zip(diagonals, olds, added)]
    inverses = [1.0 / d for d in diagonals]
    rights[2], inverses[2] = rights[2] * keep, inverses[2] * keep
    own_pattern = jnp.concatenate([pattern[...].astype(F32), jnp.zeros((TILES, WIDTH - NB), F32)], axis=1)
    present = window(parity, own_pattern, on_chip[48:56, :], across[48:56, :])
    for offset in range(NB):
        pats[offset] = jnp.broadcast_to(present[:, offset : offset + 1], (WIN, WIDTH))
    right = window(parity, *rights)
    inverse = window(parity, *inverses)
    diagonal = window(parity, *diagonals)
    value = inverse * right
    iterate[...] = value
    shifted[...] = jnp.zeros((NB, WIN, WIDTH), F32)
    coupled[...] = jnp.zeros((WIN, WIDTH), F32)
    own_at, partner_at, beside_at = 4 + 4 * parity, 12 - 12 * parity, 2 + 14 * parity

    neighbours(iterate, pats, 2, 16, shifted)
    for tile in range(TILES):
        apply_tile(own_blocks, tile, shifted, own_at + tile, coupled)
    for tile in range(6):
        apply_tile(partner_blocks, tile + 2 * parity, shifted, partner_at + tile + 2 * parity, coupled)
    for tile in range(2):
        apply_tile(beside_blocks, tile, shifted, beside_at + tile, coupled)
    update = inverse * (right - (diagonal * value + coupled[...]))
    value = value + update
    iterate[...] = value

    neighbours(iterate, pats, 4, 12, shifted)
    for tile in range(TILES):
        apply_tile(own_blocks, tile, shifted, own_at + tile, coupled)
    for tile in range(4):
        apply_tile(partner_blocks, tile + 4 * parity, shifted, partner_at + tile + 4 * parity, coupled)
    update = RHO[1] * RHO[0] * update + 4.0 * RHO[1] * inverse * (right - (diagonal * value + coupled[...]))
    value = value + update
    state[0], state[1], state[2], state[3], state[4] = value, update, right, inverse, diagonal
    swap[0:4, :] = jnp.where(parity == 0, value[4:8], value[12:16])
    swap[4:8, :] = jnp.where(parity == 0, update[4:8], update[12:16])


def wall_second_kernel(
    state, pats, swapped, dst, own_blocks, partner_blocks, beside_blocks,
    solid, returned, iterate, shifted, coupled,
):
    me = lax.axis_index("gx")
    parity = lax.rem(me, 2)
    at_edge = (me == 0) | (me == RUNS - 1)
    keep = jnp.where(at_edge, 0.0, 1.0)
    value, update, right, inverse, diagonal = (state[i] for i in range(5))

    def with_swapped(inside, outside):
        low = jnp.concatenate([outside, inside[4:24]], axis=0)
        high = jnp.concatenate([inside[0:16], outside, inside[20:24]], axis=0)
        return jnp.where(parity == 0, low, high)

    value = with_swapped(value, swapped[0:4, :] * keep)
    update = with_swapped(update, swapped[4:8, :] * keep)
    own_at, partner_at, beside_at = 4 + 4 * parity, 12 - 12 * parity, 2 + 14 * parity
    iterate[...] = value
    shifted[...] = jnp.zeros((NB, WIN, WIDTH), F32)
    coupled[...] = jnp.zeros((WIN, WIDTH), F32)

    neighbours(iterate, pats, 2, 16, shifted)
    for tile in range(TILES):
        apply_tile(own_blocks, tile, shifted, own_at + tile, coupled)
    for tile in range(2):
        apply_tile(partner_blocks, tile + 6 * parity, shifted, partner_at + tile + 6 * parity, coupled)
    for tile in range(2):
        apply_tile(beside_blocks, tile, shifted, beside_at + tile, coupled)
    update = RHO[2] * RHO[1] * update + 4.0 * RHO[2] * inverse * (right - (diagonal * value + coupled[...]))
    value = value + update
    iterate[...] = value

    neighbours(iterate, pats, 4, 12, shifted)
    for tile in range(TILES):
        apply_tile(own_blocks, tile, shifted, own_at + tile, coupled)
    update = RHO[3] * RHO[2] * update + 4.0 * RHO[3] * inverse * (right - (diagonal * value + coupled[...]))
    value = value + update
    mine = jnp.where(parity == 0, value[4:12], value[8:16])
    solid[...] = mine
    for block in range(4):
        cell = dst[8 * block : 8 * block + 8, :]
        tile, lane = cell >> 7, cell & 127
        found = jnp.zeros((8, WIDTH), F32)
        for index in range(TILES):
            row = jnp.broadcast_to(mine[index : index + 1, :], (8, WIDTH))
            found = jnp.where(tile == index, jnp.take_along_axis(row, lane, axis=1, mode="promise_in_bounds"), found)
        for r in range(8):
            returned[8 * block + r] = found[r : r + 1, :]


def stencil_kernel(fluid, liquid, on_chip, across, y_before, y_after, z_before, z_after, base):
    parity = lax.rem(lax.axis_index("gx"), 2)
    near, far = on_chip[56:120, :], across[56:120, :]
    x_before = jnp.where(parity == 0, far, near)
    x_after = jnp.where(parity == 0, near, far)
    row = lax.broadcasted_iota(I32, (64, WIDTH), 0)
    lane = lax.broadcasted_iota(I32, (64, WIDTH), 1)
    for slab in range(16):
        start = 64 * slab
        here = fluid[start : start + 64, :]
        total = (fluid[start - 64 : start, :] if slab else x_before) + (
            fluid[start + 64 : start + 128, :] if slab < 15 else x_after
        )
        total = total + jnp.where(row == 0, y_before[slab : slab + 1, :], pltpu.roll(here, 1, 0))
        total = total + jnp.where(row == 63, y_after[slab : slab + 1, :], pltpu.roll(here, 63, 0))
        half = 64 * (slab % 2)
        left = jnp.broadcast_to(z_before[slab // 2 : slab // 2 + 1, :], (WIDTH, WIDTH)).T[half : half + 64, :]
        right = jnp.broadcast_to(z_after[slab // 2 : slab // 2 + 1, :], (WIDTH, WIDTH)).T[half : half + 64, :]
        total = total + jnp.where(lane == 0, left, pltpu.roll(here, 1, 1))
        total = total + jnp.where(lane == 127, right, pltpu.roll(here, 127, 1))
        total = total - 6.0 * here
        share = liquid[start : start + 64, :].astype(F32)
        base[start : start + 64, :] = (
            here + DIFFUSION * total - EVAPORATION * share * jnp.maximum(here - SATURATION, 0.0)
        )


def final_kernel(base, src, outgoing, returned, fluid_new):
    group = 4
    total = None
    for start in range(0, RUNS, group):
        rows = range(start, start + group)
        ids = lanes([src[r : r + 1, :] for r in rows])
        value = lanes([returned[r] - outgoing[r : r + 1, :] for r in rows])
        placed = placed_parts(ids & 127, WIDTH, value)
        added = lax.dot_general(row_hots(ids >> 7, ROWS), placed, CONTRACT_LAST, preferred_element_type=F32)
        total = added if total is None else total + added
    fluid_new[...] = base[...] + WALL_COUPLING * (total[:, 0:128] + total[:, 128:256])


def shape(*dims):
    return jax.ShapeDtypeStruct(dims, F32)


def call(kernel, outs, scratch, mib, flops, moved):
    return pl.pallas_call(
        kernel,
        out_shape=outs,
        scratch_shapes=scratch,
        compiler_params=params(mib),
        cost_estimate=pl.CostEstimate(flops=flops, bytes_accessed=moved, transcendentals=0),
    )


def per_device(fluid_temp, liquid, face_src, face_dst, solid_old, solid_diag, blocks, pattern):
    parity = lax.rem(lax.axis_index("gx"), 2)
    inside = [(i, i ^ 1) for i in range(RUNS)]
    outside = [(i, (i - 1) % RUNS if i % 2 == 0 else (i + 1) % RUNS) for i in range(RUNS)]
    up = [(i, (i + 1) % 4) for i in range(4)]
    down = [(i, (i - 1) % 4) for i in range(4)]
    fluid = fluid_temp.reshape(ROWS, WIDTH)
    src = face_src.reshape(RUNS, WIDTH)
    dst = face_dst.reshape(RUNS, WIDTH)
    old, diag, own_blocks, present = solid_old[0], solid_diag[0], blocks[0], pattern[0]

    sent, outgoing, on_chip, across, y_faces, z_faces = call(
        pick_kernel,
        (shape(RUNS, 1, 384), shape(RUNS, WIDTH), shape(120, WIDTH), shape(120, WIDTH), shape(2, 16, WIDTH), shape(2, 8, WIDTH)),
        [pltpu.VMEM((256, ROWS), BF16)],
        24, 2 * 256 * 1024 * 4096, 1 << 20,
    )(fluid, src, dst, old, diag, present)

    arrived = lax.all_to_all(sent, "gx", split_axis=0, concat_axis=0, tiled=True)
    partner_blocks = lax.ppermute(own_blocks, "gx", inside)
    edge_blocks = lax.dynamic_slice_in_dim(own_blocks, 6 * parity, 2, axis=0)
    beside_blocks = lax.ppermute(edge_blocks, "gx", outside)
    on_chip = lax.ppermute(on_chip, "gx", inside)
    across = lax.ppermute(across, "gx", outside)

    scratch = [pltpu.VMEM((WIN, WIDTH), F32), pltpu.VMEM((NB, WIN, WIDTH), F32), pltpu.VMEM((WIN, WIDTH), F32)]
    state, pats, swap = call(
        wall_first_kernel,
        (shape(5, WIN, WIDTH), shape(NB, WIN, WIDTH), shape(8, WIDTH)),
        scratch, 24, 1 << 24, 6 << 20,
    )(arrived, dst, old, diag, present, on_chip, across, own_blocks, partner_blocks, beside_blocks)
    swapped = lax.ppermute(swap, "gx", outside)
    solid, sent_back = call(
        wall_second_kernel,
        (shape(TILES, WIDTH), shape(RUNS, 1, WIDTH)),
        scratch, 24, 1 << 24, 6 << 20,
    )(state, pats, swapped, dst, own_blocks, partner_blocks, beside_blocks)
    returned = lax.all_to_all(sent_back, "gx", split_axis=0, concat_axis=0, tiled=True)

    y_before = lax.ppermute(y_faces[1], "gy", up)
    y_after = lax.ppermute(y_faces[0], "gy", down)
    z_before = lax.ppermute(z_faces[1], "gz", up)
    z_after = lax.ppermute(z_faces[0], "gz", down)
    base = call(stencil_kernel, shape(ROWS, WIDTH), [], 24, 1 << 22, 1 << 21)(
        fluid, liquid.reshape(ROWS, WIDTH), on_chip, across, y_before, y_after, z_before, z_after
    )
    fluid_new = call(final_kernel, shape(ROWS, WIDTH), [], 24, 2 * 256 * 1024 * 4096, 1 << 20)(
        base, src, outgoing, returned
    )
    return fluid_new.reshape(fluid_temp.shape), solid[None]


def solution(mesh):
    return jax.shard_map(
        per_device,
        mesh=mesh,
        in_specs=(
            P("gx", "gy", "gz"),
            P("gx", "gy", "gz"),
            P("gx", "gy", "gz", None),
            P("gx", "gy", "gz", None),
            P(("gy", "gz"), "gx", None),
            P(("gy", "gz"), "gx", None),
            P(("gy", "gz"), "gx", None, None, None),
            P(("gy", "gz"), "gx", None),
        ),
        out_specs=(P("gx", "gy", "gz"), P(("gy", "gz"), "gx", None)),
        check_vma=False,
    )
```

time: 175 us -> 84.8 us (0.48)
  matrix products: 67.9 us -> 0 us
  Pallas kernels: 0 us -> 13.7 us
  waiting for transfers between devices: 21.2 us -> 8.96 us
  other arithmetic: 10.6 us -> 0 us
  starting transfers between devices: 60.4 us -> 51.7 us
  local copies, waits for them, and re-layouts: 11.5 us -> 8.71 us
    dot_general x36 -> x0, matrix products: 67.9 us -> none  [the longest x16 35 us: spread_one_block(): jnp.dot(row_hot.T, placed, precision=lax.Precision.HIGHEST, preferred_ele...]
    pallas_call x0 -> x5, Pallas kernels: none -> 13.7 us  [the longest x1 3.28 us: per_device(): call(wall_first_kernel, (shape(5, WIN, WIDTH), shape(NB, WIN, WIDTH), sha...]
    ppermute x14 -> x9, waiting for transfers between devices: 14 us -> 4.12 us  [the longest x1 2.84 us: per_device(): across = lax.ppermute(across, 'gx', outside)]
    all_to_all x1, starting transfers between devices: 16.8 us -> 10.6 us  [per_device(): lax.all_to_all(sent, 'gx', split_axis=0, concat_axis=0, tiled=True)]
    slice x9 -> x0, local copies, waits for them, and re-layouts: 4.91 us -> none  [the longest x7 3.48 us: padded_2(): leading = lax.slice_in_dim(shard, 0, width, axis=dim)]
    unnamed x21 -> x27, local copies, waits for them, and re-layouts: 1.81 us -> 6.71 us
    add x5 -> x0, other arithmetic: 4.03 us -> none  [the longest x1 3.95 us: per_device(): fluid_temp + DIFFUSION * laplacian]
    all_to_all x1, waiting for transfers between devices: 7.15 us -> 4.04 us  [per_device(): lax.all_to_all(sent, 'gx', split_axis=0, concat_axis=0, tiled=True)]
  transfers between devices with their start and end apart: 16 -> 11, of which waited for: 7 -> 4; matrix products, arithmetic and copies ran while one was open for 12% -> 3% of each run, Pallas kernels for 0% -> 9%
where the time goes in v1:
time: 84.8 us; the launch traced here: 83.9 us
  starting transfers between devices  51.7 us (61%)
  Pallas kernels  13.7 us (16%)
  waiting for transfers between devices  8.96 us (11%)
  local copies, waits for them, and re-layouts  8.71 us (10%)
    all_to_all x1, starting transfers between devices, per_device(): lax.all_to_all(sent, 'gx', split_axis=0, concat_axis=0, tiled=True)  10.6 us
    ppermute x1, starting transfers between devices, per_device(): partner_blocks = lax.ppermute(own_blocks, 'gx', inside)  8.79 us
    all_to_all x1, starting transfers between devices, per_device(): lax.all_to_all(sent_back, 'gx', split_axis=0, concat_axis=0, tiled=True)  8.17 us
    unnamed x27, local copies, waits for them, and re-layouts  6.71 us
    all_to_all x1, waiting for transfers between devices, per_device(): lax.all_to_all(sent, 'gx', split_axis=0, concat_axis=0, tiled=True)  4.04 us
    ppermute x1, starting transfers between devices, per_device(): swapped = lax.ppermute(swap, 'gx', outside)  3.52 us
    ppermute x1, starting transfers between devices, per_device(): across = lax.ppermute(across, 'gx', outside)  3.45 us
    ppermute x1, starting transfers between devices, per_device(): y_after = lax.ppermute(y_faces[0], 'gy', down)  3.39 us
  transfers between devices with their start and end apart: 11, of which 4 were waited for; matrix products, arithmetic and copies ran while one was open for 3% of the time, Pallas kernels for 9%

profile of v1, /device:TPU:1, one launch (start us, length us, event | category | flops | bytes accessed | tf_op | source)
XLA Modules:
  0.0 83.9 jit_solution(11676964119779223357)
XLA Ops:
  0.6 8.8 %collective-permute-start.6 = (f32[8,5,128,128]{3,2,1,0:T(8,128)}, f32[8,5,128,128]{3,2,1,0:T(8,128)}, u32[]{:S(2)}, u32[]{:S(2)}) collective-permute-start(f32[8,5,128,128]{3,2,1,0:T(8,128)} %bitcast.20), channel_id=1, source_target_pairs={{0,16},{16,0},{32,48},{48,32},{64,80},{80,64},{96,112},{112,96},{1... | collective-permute-start | bytes 7864328 | tf_op jit(solution)/shard_map/ppermute | solution.py:320
  9.4 2.0 %dynamic-slice_bitcast_fusion = f32[2,5,128,128]{3,2,1,0:T(8,128)} fusion(f32[1,8,5,128,128]{4,3,2,1,0:T(8,128)} %param.14, s32[]{:T(128)S(6)} %select_n.3), kind=kLoop, calls=%fused_computation | loop fusion | bytes 1310724 | tf_op jit(solution)/shard_map/dynamic_slice | solution.py:321
  11.4 1.9 %collective-permute-start.7 = (f32[2,5,128,128]{3,2,1,0:T(8,128)}, f32[2,5,128,128]{3,2,1,0:T(8,128)S(1)}, u32[]{:S(2)}, u32[]{:S(2)}) collective-permute-start(f32[2,5,128,128]{3,2,1,0:T(8,128)} %dynamic-slice_bitcast_fusion), channel_id=1, source_target_pairs={{0,496},{16,32},{32,16},{48,64},{64,48},{80,96},{96,80},{112,128},... | collective-permute-start | bytes 1966088 | tf_op jit(solution)/shard_map/ppermute | solution.py:322
  14.1 1.0 %copy-done.1 = f32[16,64,128]{2,1,0:T(8,128)S(1)} copy-done((f32[16,64,128]{2,1,0:T(8,128)S(1)}, f32[16,64,128]{2,1,0:T(8,128)}, u32[]{:S(2)}) %copy-start.1) | copy-done | bytes 524312
  18.0 3.1 %shard_map.95 = (f32[32,1,384]{2,1,0:T(1,128)}, f32[32,128]{1,0:T(8,128)S(1)}, f32[120,128]{1,0:T(8,128)}, f32[120,128]{1,0:T(8,128)S(1)}, f32[2,16,128]{2,1,0:T(8,128)S(1)}, /*index=5*/f32[2,8,128]{2,1,0:T(8,128)S(1)}) custom-call(f32[1024,128]{1,0:T(8,128)S(1)} %bitcast.23, s32[32,128]{1,0:T(8,128)S(1)} %bitcast.35, s32[32,128]{1,0:T(8,128)S(1)} %bitcast.26, ...), custom_call_target="tpu_custom_call" | custom-call | flops 2147483648 | bytes 1048576 | tf_op jit(solution)/shard_map/pallas_call | solution.py:312
  21.1 10.6 %all-to-all-start = ((f32[32,1,384]{2,1,0:T(1,128)}), f32[32,1,384]{2,1,0:T(1,128)S(1)}, u32[]{:S(2)}, u32[]{:S(2)}) async-start(f32[32,1,384]{2,1,0:T(1,128)} %get-tuple-element.18), calls=%async_computation | async-start | bytes 98304 | tf_op jit(solution)/shard_map/all_to_all | solution.py:319
  31.7 2.1 %collective-permute-start = (f32[120,128]{1,0:T(8,128)}, f32[120,128]{1,0:T(8,128)S(1)}, u32[]{:S(2)}, u32[]{:S(2)}) collective-permute-start(f32[120,128]{1,0:T(8,128)} %get-tuple-element.13), channel_id=1, source_target_pairs={{0,16},{16,0},{32,48},{48,32},{64,80},{80,64},{96,112},{112,96},{1... | collective-permute-start | bytes 184328 | tf_op jit(solution)/shard_map/ppermute | solution.py:323
  33.9 3.5 %collective-permute-start.1 = (f32[120,128]{1,0:T(8,128)}, f32[120,128]{1,0:T(8,128)S(1)}, u32[]{:S(2)}, u32[]{:S(2)}) collective-permute-start(f32[120,128]{1,0:T(8,128)} %copy-done.10), channel_id=1, source_target_pairs={{0,496},{16,32},{32,16},{48,64},{64,48},{80,96},{96,80},{112,128},... | collective-permute-start | bytes 184328 | tf_op jit(solution)/shard_map/ppermute | solution.py:324
  37.3 2.8 %collective-permute-done.1.across = f32[120,128]{1,0:T(8,128)S(1)} collective-permute-done((f32[120,128]{1,0:T(8,128)}, f32[120,128]{1,0:T(8,128)S(1)}, u32[]{:S(2)}, u32[]{:S(2)}) %collective-permute-start.1) | collective-permute-done | bytes 61472 | tf_op jit(solution)/shard_map/ppermute | solution.py:324
  40.2 4.0 %all-to-all-done.arrived = f32[32,1,384]{2,1,0:T(1,128)S(1)} async-done(((f32[32,1,384]{2,1,0:T(1,128)}), f32[32,1,384]{2,1,0:T(1,128)S(1)}, u32[]{:S(2)}, u32[]{:S(2)}) %all-to-all-start) | async-done | bytes 49184 | tf_op jit(solution)/shard_map/all_to_all | solution.py:319
  44.2 3.3 %shard_map.97 = (f32[5,24,128]{2,1,0:T(8,128)S(1)}, f32[5,24,128]{2,1,0:T(8,128)S(1)}, f32[8,128]{1,0:T(8,128)S(1)}) custom-call(f32[32,1,384]{2,1,0:T(1,128)S(1)} %all-to-all-done.arrived, s32[32,128]{1,0:T(8,128)S(1)} %bitcast.27, f32[8,128]{1,0:T(8,128)S(1)} %bitcast.32, f32[8,128]{1,0:T(8,128)S(1)} %bitcast.34, s32[8,5]{1,0:T(8,128)S(1)} %bitcast.30, ...), custom_call_target="tpu_custom_call" | custom-call | flops 16777216 | bytes 6291456 | tf_op jit(solution)/shard_map/pallas_call | solution.py:327
  47.5 3.5 %collective-permute-start.8 = (f32[8,128]{1,0:T(8,128)S(1)}, f32[8,128]{1,0:T(8,128)S(1)}, u32[]{:S(2)}, u32[]{:S(2)}) collective-permute-start(f32[8,128]{1,0:T(8,128)S(1)} %get-tuple-element.21), channel_id=1, source_target_pairs={{0,496},{16,32},{32,16},{48,64},{64,48},{80,96},{96,80},{112,128},... | collective-permute-start | bytes 12296 | tf_op jit(solution)/shard_map/ppermute | solution.py:332
  51.1 3.1 %collective-permute-start.2 = (f32[16,128]{1,0:T(8,128)S(1)}, f32[16,128]{1,0:T(8,128)S(1)}, u32[]{:S(2)}, u32[]{:S(2)}) collective-permute-start(f32[16,128]{1,0:T(8,128)S(1)} %get-tuple-element.25), channel_id=1, source_target_pairs={{0,4},{4,8},{8,12},{12,0},{1,5},{5,9},{9,13},{13,1},{2,6},{6,10},{... | collective-permute-start | bytes 24584 | tf_op jit(solution)/shard_map/ppermute | solution.py:340
  54.2 3.4 %collective-permute-start.3 = (f32[16,128]{1,0:T(8,128)S(1)}, f32[16,128]{1,0:T(8,128)S(1)}, u32[]{:S(2)}, u32[]{:S(2)}) collective-permute-start(f32[16,128]{1,0:T(8,128)S(1)} %get-tuple-element.24), channel_id=1, source_target_pairs={{0,12},{4,0},{8,4},{12,8},{1,13},{5,1},{9,5},{13,9},{2,14},{6,2},{... | collective-permute-start | bytes 24584 | tf_op jit(solution)/shard_map/ppermute | solution.py:341
  57.6 3.1 %shard_map.98 = (f32[8,128]{1,0:T(8,128)}, f32[32,1,128]{2,1,0:T(1,128)}) custom-call(f32[5,24,128]{2,1,0:T(8,128)S(1)} %get-tuple-element.19.state, f32[5,24,128]{2,1,0:T(8,128)S(1)} %get-tuple-element.20.pats, f32[8,128]{1,0:T(8,128)S(1)} %collective-permute-done.8.swapped, s32[32,128]{1,0:T(8,128)S(1)} %bitcast.28, f32[8,5,128,128]{3,2,1,0:T(8,128)S(1)} %bitcast.22, ...), custom_call_target="tpu_custom_call" | custom-call | flops 16777216 | bytes 6291456 | tf_op jit(solution)/shard_map/pallas_call | solution.py:333
  60.8 8.2 %all-to-all-start.1 = ((f32[32,1,128]{2,1,0:T(1,128)}), f32[32,1,128]{2,1,0:T(1,128)S(1)}, u32[]{:S(2)}, u32[]{:S(2)}) async-start(f32[32,1,128]{2,1,0:T(1,128)} %get-tuple-element.22), calls=%async_computation.1 | async-start | bytes 32768 | tf_op jit(solution)/shard_map/all_to_all | solution.py:338
  69.0 3.2 %collective-permute-start.4 = (f32[8,128]{1,0:T(8,128)S(1)}, f32[8,128]{1,0:T(8,128)S(1)}, u32[]{:S(2)}, u32[]{:S(2)}) collective-permute-start(f32[8,128]{1,0:T(8,128)S(1)} %get-tuple-element.27), channel_id=1, source_target_pairs={{0,1},{1,2},{2,3},{3,0},{4,5},{5,6},{6,7},{7,4},{8,9},{9,10},{10,1... | collective-permute-start | bytes 12296 | tf_op jit(solution)/shard_map/ppermute | solution.py:342
  72.2 3.4 %collective-permute-start.5 = (f32[8,128]{1,0:T(8,128)S(1)}, f32[8,128]{1,0:T(8,128)S(1)}, u32[]{:S(2)}, u32[]{:S(2)}) collective-permute-start(f32[8,128]{1,0:T(8,128)S(1)} %get-tuple-element.26), channel_id=1, source_target_pairs={{0,3},{1,0},{2,1},{3,2},{4,7},{5,4},{6,5},{7,6},{8,11},{9,8},{10,9... | collective-permute-start | bytes 12296 | tf_op jit(solution)/shard_map/ppermute | solution.py:343
  75.6 1.3 %collective-permute-done.5.z_after = f32[8,128]{1,0:T(8,128)S(1)} collective-permute-done((f32[8,128]{1,0:T(8,128)S(1)}, f32[8,128]{1,0:T(8,128)S(1)}, u32[]{:S(2)}, u32[]{:S(2)}) %collective-permute-start.5) | collective-permute-done | bytes 4128 | tf_op jit(solution)/shard_map/ppermute | solution.py:343
  76.8 1.0 %copy-done.2 = f32[16,64,128]{2,1,0:T(8,128)S(1)} copy-done((f32[16,64,128]{2,1,0:T(8,128)S(1)}, f32[16,64,128]{2,1,0:T(8,128)}, u32[]{:S(2)}) %copy-start.2) | copy-done | bytes 524312
  77.9 1.0 %copy-done.3 = s32[16,64,128]{2,1,0:T(8,128)S(1)} copy-done((s32[16,64,128]{2,1,0:T(8,128)S(1)}, s32[16,64,128]{2,1,0:T(8,128)}, u32[]{:S(2)}) %copy-start.3) | copy-done | bytes 524312
  78.9 0.9 %shard_map.96.base = f32[1024,128]{1,0:T(8,128)S(1)} custom-call(f32[1024,128]{1,0:T(8,128)S(1)} %bitcast.24, s32[1024,128]{1,0:T(8,128)S(1)} %bitcast.25, f32[120,128]{1,0:T(8,128)S(1)} %collective-permute-done.on_chip, f32[120,128]{1,0:T(8,128)S(1)} %collective-permute-done.1.across, f32[16,128]{1,0:T(8,128)S(1)} %collective-permute-done.2.y_before, ...), custom_call_target="tpu_custom_call" | custom-call | flops 4194304 | bytes 2097152 | tf_op jit(solution)/shard_map/pallas_call | solution.py:344
  79.9 0.8 all-to-all-done.1.returned
  80.7 3.2 %shard_map.99 = f32[1024,128]{1,0:T(8,128)} custom-call(f32[1024,128]{1,0:T(8,128)S(1)} %shard_map.96.base, s32[32,128]{1,0:T(8,128)S(1)} %bitcast.36, f32[32,128]{1,0:T(8,128)S(1)} %get-tuple-element.17.outgoing, f32[32,1,128]{2,1,0:T(1,128)S(1)} %all-to-all-done.1.returned), custom_call_target="tpu_custom_call" | custom-call | flops 2147483648 | bytes 1048576 | tf_op jit(solution)/shard_map/pallas_call | solution.py:347
  (33 shorter events, 3.6 us)
Async XLA Ops:
  0.6 43.6 %collective-permute-start.6 = (f32[8,5,128,128]{3,2,1,0:T(8,128)}, f32[8,5,128,128]{3,2,1,0:T(8,128)}, u32[]{:S(2)}, u32[]{:S(2)}) collective-permute-start(f32[8,5,128,128]{3,2,1,0:T(8,128)} %bitcast.20), channel_id=1, source_target_pairs={{0,16},{16,0},{32,48},{48,32},{64,80},{80,64},{96,112},{112,96},{1... | collective-permute-start | bytes 7864328 | tf_op jit(solution)/shard_map/ppermute | solution.py:320
  11.4 32.8 %collective-permute-start.7 = (f32[2,5,128,128]{3,2,1,0:T(8,128)}, f32[2,5,128,128]{3,2,1,0:T(8,128)S(1)}, u32[]{:S(2)}, u32[]{:S(2)}) collective-permute-start(f32[2,5,128,128]{3,2,1,0:T(8,128)} %dynamic-slice_bitcast_fusion), channel_id=1, source_target_pairs={{0,496},{16,32},{32,16},{48,64},{64,48},{80,96},{96,80},{112,128},... | collective-permute-start | bytes 1966088 | tf_op jit(solution)/shard_map/ppermute | solution.py:322
  14.1 1.0 %copy-start.1 = (f32[16,64,128]{2,1,0:T(8,128)S(1)}, f32[16,64,128]{2,1,0:T(8,128)}, u32[]{:S(2)}) copy-start(f32[16,64,128]{2,1,0:T(8,128)} %param.8) | copy-start | bytes 1572868
  15.1 0.7 copy-start.4
  15.9 0.7 copy-start.6
  16.5 0.7 copy-start.8
  17.2 0.7 copy-start.11
  18.0 26.3 %copy-start = (f32[1,8,5,128,128]{4,3,2,1,0:T(8,128)S(1)}, f32[1,8,5,128,128]{4,3,2,1,0:T(8,128)}, u32[]{:S(2)}) copy-start(f32[1,8,5,128,128]{4,3,2,1,0:T(8,128)} %param.14) | copy-start | bytes 7864324
  18.0 26.3 %copy-start.5 = (s32[32,1,1,128]{3,2,1,0:T(1,128)S(1)}, s32[32,1,1,128]{3,2,1,0:T(1,128)}, u32[]{:S(2)}) copy-start(s32[32,1,1,128]{3,2,1,0:T(1,128)} %param.11) | copy-start | bytes 49156
  18.0 26.3 %copy-start.7 = (f32[1,8,128]{2,1,0:T(8,128)S(1)}, f32[1,8,128]{2,1,0:T(8,128)}, u32[]{:S(2)}) copy-start(f32[1,8,128]{2,1,0:T(8,128)} %param.12) | copy-start | bytes 12292
  18.0 26.3 %copy-start.9 = (f32[1,8,128]{2,1,0:T(8,128)S(1)}, f32[1,8,128]{2,1,0:T(8,128)}, u32[]{:S(2)}) copy-start(f32[1,8,128]{2,1,0:T(8,128)} %param.13) | copy-start | bytes 12292
  21.1 10.6 %copy-start.10 = (f32[120,128]{1,0:T(8,128)}, f32[120,128]{1,0:T(8,128)S(1)}, u32[]{:S(2)}) copy-start(f32[120,128]{1,0:T(8,128)S(1)} %get-tuple-element.14) | copy-start | bytes 184324
  21.1 23.1 %all-to-all-start = ((f32[32,1,384]{2,1,0:T(1,128)}), f32[32,1,384]{2,1,0:T(1,128)S(1)}, u32[]{:S(2)}, u32[]{:S(2)}) async-start(f32[32,1,384]{2,1,0:T(1,128)} %get-tuple-element.18), calls=%async_computation | async-start | bytes 98304 | tf_op jit(solution)/shard_map/all_to_all | solution.py:319
  31.7 5.6 %collective-permute-start = (f32[120,128]{1,0:T(8,128)}, f32[120,128]{1,0:T(8,128)S(1)}, u32[]{:S(2)}, u32[]{:S(2)}) collective-permute-start(f32[120,128]{1,0:T(8,128)} %get-tuple-element.13), channel_id=1, source_target_pairs={{0,16},{16,0},{32,48},{48,32},{64,80},{80,64},{96,112},{112,96},{1... | collective-permute-start | bytes 184328 | tf_op jit(solution)/shard_map/ppermute | solution.py:323
  33.9 6.3 %collective-permute-start.1 = (f32[120,128]{1,0:T(8,128)}, f32[120,128]{1,0:T(8,128)S(1)}, u32[]{:S(2)}, u32[]{:S(2)}) collective-permute-start(f32[120,128]{1,0:T(8,128)} %copy-done.10), channel_id=1, source_target_pairs={{0,496},{16,32},{32,16},{48,64},{64,48},{80,96},{96,80},{112,128},... | collective-permute-start | bytes 184328 | tf_op jit(solution)/shard_map/ppermute | solution.py:324
  47.5 10.1 %collective-permute-start.8 = (f32[8,128]{1,0:T(8,128)S(1)}, f32[8,128]{1,0:T(8,128)S(1)}, u32[]{:S(2)}, u32[]{:S(2)}) collective-permute-start(f32[8,128]{1,0:T(8,128)S(1)} %get-tuple-element.21), channel_id=1, source_target_pairs={{0,496},{16,32},{32,16},{48,64},{64,48},{80,96},{96,80},{112,128},... | collective-permute-start | bytes 12296 | tf_op jit(solution)/shard_map/ppermute | solution.py:332
  51.1 25.7 %collective-permute-start.2 = (f32[16,128]{1,0:T(8,128)S(1)}, f32[16,128]{1,0:T(8,128)S(1)}, u32[]{:S(2)}, u32[]{:S(2)}) collective-permute-start(f32[16,128]{1,0:T(8,128)S(1)} %get-tuple-element.25), channel_id=1, source_target_pairs={{0,4},{4,8},{8,12},{12,0},{1,5},{5,9},{9,13},{13,1},{2,6},{6,10},{... | collective-permute-start | bytes 24584 | tf_op jit(solution)/shard_map/ppermute | solution.py:340
  54.2 22.6 %collective-permute-start.3 = (f32[16,128]{1,0:T(8,128)S(1)}, f32[16,128]{1,0:T(8,128)S(1)}, u32[]{:S(2)}, u32[]{:S(2)}) collective-permute-start(f32[16,128]{1,0:T(8,128)S(1)} %get-tuple-element.24), channel_id=1, source_target_pairs={{0,12},{4,0},{8,4},{12,8},{1,13},{5,1},{9,5},{13,9},{2,14},{6,2},{... | collective-permute-start | bytes 24584 | tf_op jit(solution)/shard_map/ppermute | solution.py:341
  57.6 23.0 %copy-start.12 = (s32[32,1,1,128]{3,2,1,0:T(1,128)S(1)}, s32[32,1,1,128]{3,2,1,0:T(1,128)}, u32[]{:S(2)}) copy-start(s32[32,1,1,128]{3,2,1,0:T(1,128)} %param.10) | copy-start | bytes 49156
  60.8 19.9 %all-to-all-start.1 = ((f32[32,1,128]{2,1,0:T(1,128)}), f32[32,1,128]{2,1,0:T(1,128)S(1)}, u32[]{:S(2)}, u32[]{:S(2)}) async-start(f32[32,1,128]{2,1,0:T(1,128)} %get-tuple-element.22), calls=%async_computation.1 | async-start | bytes 32768 | tf_op jit(solution)/shard_map/all_to_all | solution.py:338
  69.0 6.6 %collective-permute-start.4 = (f32[8,128]{1,0:T(8,128)S(1)}, f32[8,128]{1,0:T(8,128)S(1)}, u32[]{:S(2)}, u32[]{:S(2)}) collective-permute-start(f32[8,128]{1,0:T(8,128)S(1)} %get-tuple-element.27), channel_id=1, source_target_pairs={{0,1},{1,2},{2,3},{3,0},{4,5},{5,6},{6,7},{7,4},{8,9},{9,10},{10,1... | collective-permute-start | bytes 12296 | tf_op jit(solution)/shard_map/ppermute | solution.py:342
  72.2 4.6 %collective-permute-start.5 = (f32[8,128]{1,0:T(8,128)S(1)}, f32[8,128]{1,0:T(8,128)S(1)}, u32[]{:S(2)}, u32[]{:S(2)}) collective-permute-start(f32[8,128]{1,0:T(8,128)S(1)} %get-tuple-element.26), channel_id=1, source_target_pairs={{0,3},{1,0},{2,1},{3,2},{4,7},{5,4},{6,5},{7,6},{8,11},{9,8},{10,9... | collective-permute-start | bytes 12296 | tf_op jit(solution)/shard_map/ppermute | solution.py:343
  76.8 1.0 %copy-start.2 = (f32[16,64,128]{2,1,0:T(8,128)S(1)}, f32[16,64,128]{2,1,0:T(8,128)}, u32[]{:S(2)}) copy-start(f32[16,64,128]{2,1,0:T(8,128)} %param.8) | copy-start | bytes 1572868
  77.9 1.0 %copy-start.3 = (s32[16,64,128]{2,1,0:T(8,128)S(1)}, s32[16,64,128]{2,1,0:T(8,128)}, u32[]{:S(2)}) copy-start(s32[16,64,128]{2,1,0:T(8,128)} %param.9) | copy-start | bytes 1572868

commit v2 on v1

v2 whole, which is shorter than its diff:
```python
import jax
import jax.numpy as jnp
from jax import lax
from jax.experimental import pallas as pl
from jax.experimental.pallas import tpu as pltpu
from jax.sharding import PartitionSpec as P

F32 = jnp.float32
BF16 = jnp.bfloat16
I32 = jnp.int32
RUNS = 32
WIDTH = 128
ROWS = 1024
TILES = 8
NB = 5
WIN = 24
TILE_ROWS = NB * WIDTH
SMALL = 120

DIFFUSION = 0.12
EVAPORATION = 0.5
SATURATION = 0.25
WALL_COUPLING = 0.2

VMEM = pl.BlockSpec(memory_space=pltpu.VMEM)
HBM = pl.BlockSpec(memory_space=pltpu.HBM)
ANY = pl.BlockSpec(memory_space=pl.ANY)


def params(mib):
    return pltpu.CompilerParams(vmem_limit_bytes=mib << 20)


def two_parts(values):
    high = values.astype(BF16)
    return high, (values - high.astype(F32)).astype(BF16)


def lanes(rows):
    return jnp.concatenate(rows, axis=1)


def row_hots(row, count):
    width = row.shape[1]
    part = min(count, 256)
    level = lax.broadcasted_iota(I32, (part, width), 0).astype(F32).astype(BF16)
    one, zero = jnp.ones((), BF16), jnp.zeros((), BF16)
    parts = []
    for index in range(count // part):
        here = jnp.where((row >= index * part) & (row < (index + 1) * part), row - index * part, -1)
        parts.append(jnp.where(level == here.astype(F32).astype(BF16), one, zero))
    return parts[0] if len(parts) == 1 else jnp.concatenate(parts, axis=0)


def placed_parts(column, count, values):
    width = column.shape[1]
    mask = lax.broadcasted_iota(I32, (count, width), 0) == column
    high = values.astype(BF16).astype(F32)
    low = values - high
    both = [jnp.where(mask, part, 0.0) for part in (high, low)]
    return jnp.concatenate(both, axis=0).astype(BF16)


CONTRACT_LAST = (((1,), (1,)), ((), ()))


def pick_kernel(
    fluid_hbm, src_hbm, dst_hbm, old_hbm, diag_hbm, pattern_hbm, blocks_hbm,
    sent, outgoing, own, y_faces, z_faces, on_chip_hbm, across_hbm,
    fluid, src, dst, pattern, table, packed, sems,
):
    me = lax.axis_index("gx")
    parity = lax.rem(me, 2)

    def copy(source, target, index):
        started = pltpu.make_async_copy(source, target, sems.at[index])
        started.start()
        return started

    loads = [copy(fluid_hbm.at[128 * i : 128 * i + 128], fluid.at[128 * i : 128 * i + 128], i) for i in range(8)]
    load_src = copy(src_hbm, src, 8)
    small = [
        copy(dst_hbm, dst, 9),
        copy(old_hbm, own.at[32:40], 10),
        copy(diag_hbm, own.at[40:48], 11),
        copy(pattern_hbm, pattern, 16),
    ]
    inside = copy(blocks_hbm.at[pl.ds((1 - parity) * 2 * TILE_ROWS, 6 * TILE_ROWS)], on_chip_hbm.at[0 : 6 * TILE_ROWS], 12)
    outside = copy(blocks_hbm.at[pl.ds(parity * 6 * TILE_ROWS, 2 * TILE_ROWS)], across_hbm.at[0 : 2 * TILE_ROWS], 13)
    for block in range(8):
        loads[block].wait()
        turned = fluid[128 * block : 128 * block + 128, :].T
        high, low = two_parts(turned)
        table[0:128, 128 * block : 128 * block + 128] = high
        table[128:256, 128 * block : 128 * block + 128] = low
        z_faces[0, block : block + 1, :] = turned[0:1, :]
        z_faces[1, block : block + 1, :] = turned[127:128, :]
    load_src.wait()
    group = 4
    for start in range(0, RUNS, group):
        ids = lanes([src[r : r + 1, :] for r in range(start, start + group)])
        picked = jnp.dot(table[...], row_hots(ids >> 7, ROWS), preferred_element_type=F32)
        both = picked[0:128] + picked[128:256]
        mask = lax.broadcasted_iota(I32, (WIDTH, group * WIDTH), 0) == (ids & 127)
        value = jnp.sum(jnp.where(mask, both, 0.0), axis=0, keepdims=True)
        for r in range(start, start + group):
            mine = value[:, (r - start) * WIDTH : (r - start + 1) * WIDTH]
            outgoing[r : r + 1, :] = mine
            sent[r, :, 0:128] = mine
            sent[r ^ 1, :, 128:256] = mine
            beside = (r + 1) % RUNS if r % 2 else (r - 1) % RUNS
            sent[beside, :, 256:384] = mine
    for slab in range(16):
        y_faces[0, slab : slab + 1, :] = fluid[64 * slab : 64 * slab + 1, :]
        y_faces[1, slab : slab + 1, :] = fluid[64 * slab + 63 : 64 * slab + 64, :]
    for each in small:
        each.wait()
    own[0:32, :] = dst[...].astype(F32)
    own[48:56, :] = jnp.zeros((8, WIDTH), F32)
    for offset in range(NB):
        own[48 + offset : 49 + offset, 0:TILES] = pattern[offset].astype(F32)
    first, last = fluid[0:64, :], fluid[960:1024, :]
    for index, face in ((0, jnp.where(parity == 0, last, first)), (1, jnp.where(parity == 0, first, last))):
        packed[index, 0:56, :] = own[...]
        packed[index, 56:120, :] = face
    tail_in = copy(packed.at[0], on_chip_hbm.at[6 * TILE_ROWS : 6 * TILE_ROWS + SMALL], 14)
    tail_out = copy(packed.at[1], across_hbm.at[2 * TILE_ROWS : 2 * TILE_ROWS + SMALL], 15)
    for each in (inside, outside, tail_in, tail_out):
        each.wait()


def spread_run(ids_of, values_of):
    group = 8
    total = None
    for start in range(0, RUNS, group):
        cell = lanes([ids_of(r) for r in range(start, start + group)])
        value = lanes([values_of(r) for r in range(start, start + group)])
        row = jnp.where(cell >= 0, ((cell >> 5) & 3) * 8 + (cell >> 7), -1)
        hots = row_hots(row, 32)
        placed = placed_parts(cell & 31, 32, value)
        added = lax.dot_general(hots, placed, CONTRACT_LAST, preferred_element_type=F32)
        total = added if total is None else total + added
    total = total[:, 0:32] + total[:, 32:64]
    return lanes([total[8 * u : 8 * u + 8, :] for u in range(4)])


def window(parity, own, partner, beside):
    pad = jnp.zeros((4, own.shape[1]), F32)
    low = jnp.concatenate([beside[4:8], own, partner, pad], axis=0)
    high = jnp.concatenate([partner, own, beside[0:4], pad], axis=0)
    return jnp.where(parity == 0, low, high)


def neighbours(iterate, pats, first, count, shifted):
    for offset in range(NB):
        values = iterate[first - 2 + offset : first - 2 + offset + count, :]
        shifted[offset, first : first + count, :] = values * pats[offset, first : first + count, :]


def apply_tile(blocks, tile, shifted, place, coupled):
    total = None
    for offset in range(NB):
        start = pl.multiple_of(tile * TILE_ROWS + offset * WIDTH, WIDTH)
        term = blocks[pl.ds(start, WIDTH), :] * shifted[offset, pl.ds(place, 1), :]
        total = term if total is None else total + term
    coupled[pl.ds(place, 1), :] = jnp.sum(total.T, axis=0, keepdims=True)


RHO = [0.5]
for _ in range(3):
    RHO.append(1.0 / (4.0 - RHO[-1]))


def stepped(sweep, value, update, right, inverse, diagonal, coupled):
    residual = right - (diagonal * value + coupled)
    if sweep == 0:
        update = inverse * residual
    else:
        update = RHO[sweep] * RHO[sweep - 1] * update + 4.0 * RHO[sweep] * inverse * residual
    return value + update, update


def own_run_kernel(arrived, own, added):
    added[...] = spread_run(lambda r: own[r : r + 1, :].astype(I32), lambda r: arrived[r, :, 0:128])


def beside_run_kernel(arrived, across_hbm, added_own, added, small, sem):
    load = pltpu.make_async_copy(across_hbm.at[2 * TILE_ROWS : 2 * TILE_ROWS + SMALL], small, sem)
    load.start()
    added[0:TILES, :] = added_own[...]
    load.wait()
    added[TILES : 2 * TILES, :] = spread_run(
        lambda r: small[r : r + 1, :].astype(I32), lambda r: arrived[r, :, 256:384]
    )


def wall_first_kernel(
    arrived, added_before, beside_small, own, own_blocks, on_chip_hbm, across_hbm, y_before, y_after,
    state, pats, swap, faces, y_faces,
    inner, outer, iterate, shifted, coupled, sems,
):
    me = lax.axis_index("gx")
    parity = lax.rem(me, 2)
    keep = jnp.where((me == 0) | (me == RUNS - 1), 0.0, 1.0)
    loads = []
    at_in = 6 * TILE_ROWS
    for index, (source, target, low, high) in enumerate((
        (on_chip_hbm, inner, at_in, at_in + SMALL),
        (on_chip_hbm, inner, 0, at_in),
        (across_hbm, outer, 0, 2 * TILE_ROWS),
    )):
        loads.append(pltpu.make_async_copy(source.at[low:high], target.at[low:high], sems.at[index]))
        loads[-1].start()
    loads[0].wait()
    partner, beside = inner[at_in : at_in + SMALL, :], beside_small[...]
    added = [
        added_before[0:TILES, :],
        spread_run(lambda r: inner[at_in + r : at_in + r + 1, :].astype(I32), lambda r: arrived[r, :, 128:256]),
        added_before[TILES : 2 * TILES, :],
    ]
    holders = [own[...], partner, beside]
    diagonals = [each[40:48] for each in holders]
    rights = [d * each[32:40] + a for d, each, a in zip(diagonals, holders, added)]
    inverses = [1.0 / d for d in diagonals]
    rights[2], inverses[2] = rights[2] * keep, inverses[2] * keep
    present = window(parity, *[each[48:56].T[0:TILES] for each in holders])
    for offset in range(NB):
        pats[offset] = jnp.broadcast_to(present[:, offset : offset + 1], (WIN, WIDTH))
    right = window(parity, *rights)
    inverse = window(parity, *inverses)
    diagonal = window(parity, *diagonals)
    y_faces[0], y_faces[1] = y_before[...], y_after[...]
    faces[0] = jnp.where(parity == 0, beside[56:120], partner[56:120])
    faces[1] = jnp.where(parity == 0, partner[56:120], beside[56:120])
    value = inverse * right
    iterate[...] = value
    shifted[...] = jnp.zeros((NB, WIN, WIDTH), F32)
    coupled[...] = jnp.zeros((WIN, WIDTH), F32)
    own_at = 4 + 4 * parity

    neighbours(iterate, pats, 2, 16, shifted)
    for tile in range(TILES):
        apply_tile(own_blocks, tile, shifted, own_at + tile, coupled)
    loads[1].wait()
    loads[2].wait()
    for tile in range(6):
        apply_tile(inner, tile, shifted, 12 - 10 * parity + tile, coupled)
    for tile in range(2):
        apply_tile(outer, tile, shifted, 2 + 14 * parity + tile, coupled)
    value, update = stepped(0, value, None, right, inverse, diagonal, coupled[...])
    iterate[...] = value

    neighbours(iterate, pats, 4, 12, shifted)
    for tile in range(TILES):
        apply_tile(own_blocks, tile, shifted, own_at + tile, coupled)
    for tile in range(4):
        apply_tile(inner, tile + 2 * parity, shifted, 12 - 8 * parity + tile, coupled)
    value, update = stepped(1, value, update, right, inverse, diagonal, coupled[...])
    state[0], state[1], state[2], state[3], state[4] = value, update, right, inverse, diagonal
    swap[0:4, :] = jnp.where(parity == 0, value[4:8], value[12:16])
    swap[4:8, :] = jnp.where(parity == 0, update[4:8], update[12:16])


def wall_inner_kernel(state, pats, own_blocks, on_chip_hbm, inside, inner, iterate, shifted, coupled, sem):
    parity = lax.rem(lax.axis_index("gx"), 2)
    load = pltpu.make_async_copy(on_chip_hbm.at[pl.ds(parity * 4 * TILE_ROWS, 2 * TILE_ROWS)], inner, sem)
    load.start()
    value, update, right, inverse, diagonal = (state[i] for i in range(5))
    iterate[...] = value
    shifted[...] = jnp.zeros((NB, WIN, WIDTH), F32)
    coupled[...] = jnp.zeros((WIN, WIDTH), F32)
    own_at = 4 + 4 * parity
    neighbours(iterate, pats, 6, 8, shifted)
    for index in range(6):
        tile = index + 2 - 2 * parity
        apply_tile(own_blocks, tile, shifted, own_at + tile, coupled)
    load.wait()
    for index in range(2):
        apply_tile(inner, index, shifted, 12 - 6 * parity + index, coupled)
    value, update = stepped(2, value, update, right, inverse, diagonal, coupled[...])
    inside[0], inside[1] = value, update
    iterate[...] = value
    neighbours(iterate, pats, 8, 4, shifted)
    for index in range(4):
        tile = index + 4 - 4 * parity
        apply_tile(own_blocks, tile, shifted, own_at + tile, coupled)
    inside[2] = coupled[...]


def wall_last_kernel(
    state, pats, inside, swapped, own, own_blocks, across_hbm,
    solid, returned, outer, iterate, shifted, coupled, sem,
):
    load = pltpu.make_async_copy(across_hbm.at[0 : 2 * TILE_ROWS], outer, sem)
    load.start()
    me = lax.axis_index("gx")
    parity = lax.rem(me, 2)
    keep = jnp.where((me == 0) | (me == RUNS - 1), 0.0, 1.0)
    value, update, right, inverse, diagonal = (state[i] for i in range(5))

    def with_swapped(inside, outside):
        low = jnp.concatenate([outside, inside[4:24]], axis=0)
        high = jnp.concatenate([inside[0:16], outside, inside[20:24]], axis=0)
        return jnp.where(parity == 0, low, high)

    value = with_swapped(value, swapped[0:4, :] * keep)
    update = with_swapped(update, swapped[4:8, :] * keep)
    place = lax.broadcasted_iota(I32, (WIN, WIDTH), 0)
    own_at = 4 + 4 * parity
    iterate[...] = value
    shifted[...] = jnp.zeros((NB, WIN, WIDTH), F32)
    coupled[...] = jnp.zeros((WIN, WIDTH), F32)
    neighbours(iterate, pats, 2, 16, shifted)
    for index in range(2):
        tile = index + 6 * parity
        apply_tile(own_blocks, tile, shifted, own_at + tile, coupled)
    load.wait()
    for index in range(2):
        apply_tile(outer, index, shifted, 2 + 14 * parity + index, coupled)
    value, update = stepped(2, value, update, right, inverse, diagonal, coupled[...])
    known = (place >= 6) & (place < 14)
    value, update = jnp.where(known, inside[0], value), jnp.where(known, inside[1], update)
    iterate[...] = value
    neighbours(iterate, pats, 4, 12, shifted)
    for index in range(4):
        tile = index + 4 * parity
        apply_tile(own_blocks, tile, shifted, own_at + tile, coupled)
    product = jnp.where((place >= 8) & (place < 12), inside[2], coupled[...])
    value, update = stepped(3, value, update, right, inverse, diagonal, product)
    mine = jnp.where(parity == 0, value[4:12], value[8:16])
    solid[...] = mine
    for block in range(4):
        cell = own[8 * block : 8 * block + 8, :].astype(I32)
        tile, lane = cell >> 7, cell & 127
        found = jnp.zeros((8, WIDTH), F32)
        for index in range(TILES):
            row = jnp.broadcast_to(mine[index : index + 1, :], (8, WIDTH))
            found = jnp.where(tile == index, jnp.take_along_axis(row, lane, axis=1, mode="promise_in_bounds"), found)
        for r in range(8):
            returned[8 * block + r] = found[r : r + 1, :]


def stencil_kernel(fluid_hbm, liquid_hbm, x_faces, y_faces, z_before, z_after, base, fluid, liquid, sems):
    loads = [
        pltpu.make_async_copy(fluid_hbm, fluid, sems.at[0]),
        pltpu.make_async_copy(liquid_hbm, liquid, sems.at[1]),
    ]
    for each in loads:
        each.start()
    row = lax.broadcasted_iota(I32, (64, WIDTH), 0)
    lane = lax.broadcasted_iota(I32, (64, WIDTH), 1)
    for each in loads:
        each.wait()
    for slab in range(16):
        start = 64 * slab
        block = slab // 2
        here = fluid[start : start + 64, :]
        total = (fluid[start - 64 : start, :] if slab else x_faces[0]) + (
            fluid[start + 64 : start + 128, :] if slab < 15 else x_faces[1]
        )
        total = total + jnp.where(row == 0, y_faces[0, slab : slab + 1, :], pltpu.roll(here, 1, 0))
        total = total + jnp.where(row == 63, y_faces[1, slab : slab + 1, :], pltpu.roll(here, 63, 0))
        half = 64 * (slab % 2)
        left = jnp.broadcast_to(z_before[block : block + 1, :], (WIDTH, WIDTH)).T[half : half + 64, :]
        right = jnp.broadcast_to(z_after[block : block + 1, :], (WIDTH, WIDTH)).T[half : half + 64, :]
        total = total + jnp.where(lane == 0, left, pltpu.roll(here, 1, 1))
        total = total + jnp.where(lane == 127, right, pltpu.roll(here, 127, 1))
        total = total - 6.0 * here
        share = liquid[start : start + 64, :].astype(F32)
        base[start : start + 64, :] = (
            here + DIFFUSION * total - EVAPORATION * share * jnp.maximum(here - SATURATION, 0.0)
        )


def final_kernel(base, src, outgoing, returned, fluid_new):
    group = 4
    total = None
    for start in range(0, RUNS, group):
        rows = range(start, start + group)
        ids = lanes([src[r : r + 1, :] for r in rows])
        value = lanes([returned[r] - outgoing[r : r + 1, :] for r in rows])
        placed = placed_parts(ids & 127, WIDTH, value)
        added = lax.dot_general(row_hots(ids >> 7, ROWS), placed, CONTRACT_LAST, preferred_element_type=F32)
        total = added if total is None else total + added
    fluid_new[...] = base[...] + WALL_COUPLING * (total[:, 0:128] + total[:, 128:256])


def shape(*dims):
    return jax.ShapeDtypeStruct(dims, F32)


def call(kernel, mib, ins, outs, out_specs, scratch, flops, moved):
    return pl.pallas_call(
        kernel,
        in_specs=ins,
        out_shape=outs,
        out_specs=out_specs,
        scratch_shapes=scratch,
        compiler_params=params(mib),
        cost_estimate=pl.CostEstimate(flops=flops, bytes_accessed=moved, transcendentals=0),
    )


def vmem(*dims, kind=F32):
    return pltpu.VMEM(dims, kind)


def dma(*dims):
    return pltpu.SemaphoreType.DMA(dims) if dims else pltpu.SemaphoreType.DMA


def per_device(fluid_temp, liquid, face_src, face_dst, solid_old, solid_diag, blocks, pattern):
    inside_pairs = [(i, i ^ 1) for i in range(RUNS)]
    outside_pairs = [(i, (i - 1) % RUNS if i % 2 == 0 else (i + 1) % RUNS) for i in range(RUNS)]
    fluid = fluid_temp.reshape(ROWS, WIDTH)
    src = face_src.reshape(RUNS, WIDTH)
    dst = face_dst.reshape(RUNS, WIDTH)
    own_blocks = blocks.reshape(TILES * TILE_ROWS, WIDTH)
    in_rows, out_rows = 6 * TILE_ROWS + SMALL, 2 * TILE_ROWS + SMALL

    sent, outgoing, own, y_faces, z_faces, on_chip, across = call(
        pick_kernel, 60,
        [HBM] * 7,
        (
            shape(RUNS, 1, 384), shape(RUNS, WIDTH), shape(56, WIDTH), shape(2, 16, WIDTH), shape(2, 8, WIDTH),
            shape(in_rows, WIDTH), shape(out_rows, WIDTH),
        ),
        (VMEM, VMEM, VMEM, VMEM, VMEM, HBM, HBM),
        [
            vmem(ROWS, WIDTH), vmem(RUNS, WIDTH, kind=I32), vmem(RUNS, WIDTH, kind=I32), vmem(NB, 1, TILES, kind=I32),
            vmem(256, ROWS, kind=BF16), vmem(2, SMALL, WIDTH), dma(17),
        ],
        2 * 256 * 1024 * 4096, 1 << 22,
    )(fluid, src, dst, solid_old[0], solid_diag[0], jnp.transpose(pattern, (2, 0, 1)), own_blocks)

    arrived = lax.all_to_all(sent, "gx", split_axis=0, concat_axis=0, tiled=True)
    on_chip = lax.ppermute(on_chip, "gx", inside_pairs)
    across = lax.ppermute(across, "gx", outside_pairs)
    up = [(i, (i + 1) % 4) for i in range(4)]
    down = [(i, (i - 1) % 4) for i in range(4)]
    y_before = lax.ppermute(y_faces[1], "gy", up)
    y_after = lax.ppermute(y_faces[0], "gy", down)

    work = [vmem(WIN, WIDTH), vmem(NB, WIN, WIDTH), vmem(WIN, WIDTH)]
    added_own = call(
        own_run_kernel, 12, [VMEM, VMEM], shape(TILES, WIDTH), VMEM, [], 65 * 10**8, 1 << 16
    )(arrived, own)
    added_before, beside_small = call(
        beside_run_kernel, 12, [VMEM, ANY, VMEM], (shape(2 * TILES, WIDTH), shape(SMALL, WIDTH)), (VMEM, VMEM), [dma()],
        14 * 10**9, 1 << 16,
    )(arrived, across, added_own)
    state, pats, swap, x_faces, y_faces = call(
        wall_first_kernel, 16,
        [VMEM, VMEM, VMEM, VMEM, VMEM, ANY, ANY, VMEM, VMEM],
        (shape(5, WIN, WIDTH), shape(NB, WIN, WIDTH), shape(8, WIDTH), shape(2, 64, WIDTH), shape(2, 16, WIDTH)),
        (VMEM,) * 5,
        [vmem(in_rows, WIDTH), vmem(2 * TILE_ROWS, WIDTH)] + work + [dma(3)],
        1 << 24, 6 << 20,
    )(arrived, added_before, beside_small, own, own_blocks, on_chip, across, y_before, y_after)
    swapped = lax.ppermute(swap, "gx", outside_pairs)
    inside = call(
        wall_inner_kernel, 12,
        [VMEM, VMEM, VMEM, ANY],
        shape(3, WIN, WIDTH), VMEM,
        [vmem(2 * TILE_ROWS, WIDTH)] + work + [dma()],
        1 << 22, 3 << 20,
    )(state, pats, own_blocks, on_chip)
    solid, sent_back = call(
        wall_last_kernel, 12,
        [VMEM] * 6 + [ANY],
        (shape(TILES, WIDTH), shape(RUNS, 1, WIDTH)), (VMEM, VMEM),
        [vmem(2 * TILE_ROWS, WIDTH)] + work + [dma()],
        1 << 23, 3 << 20,
    )(state, pats, inside, swapped, own, own_blocks, across)
    sent_back, z_faces = lax.optimization_barrier((sent_back, z_faces))
    z_before = lax.ppermute(z_faces[1], "gz", up)
    z_after = lax.ppermute(z_faces[0], "gz", down)
    returned = lax.all_to_all(sent_back, "gx", split_axis=0, concat_axis=0, tiled=True)

    base = call(
        stencil_kernel, 12,
        [HBM, HBM, VMEM, VMEM, VMEM, VMEM],
        shape(ROWS, WIDTH), VMEM,
        [vmem(ROWS, WIDTH), vmem(ROWS, WIDTH, kind=I32), dma(2)],
        1 << 22, 1 << 21,
    )(fluid, liquid.reshape(ROWS, WIDTH), x_faces, y_faces, z_before, z_after)
    fluid_new = call(
        final_kernel, 16, [VMEM] * 4, shape(ROWS, WIDTH), VMEM, [], 2 * 256 * 1024 * 4096, 1 << 20
    )(base, src, outgoing, returned)
    return fluid_new.reshape(fluid_temp.shape), solid[None]


def solution(mesh):
    return jax.shard_map(
        per_device,
        mesh=mesh,
        in_specs=(
            P("gx", "gy", "gz"),
            P("gx", "gy", "gz"),
            P("gx", "gy", "gz", None),
            P("gx", "gy", "gz", None),
            P(("gy", "gz"), "gx", None),
            P(("gy", "gz"), "gx", None),
            P(("gy", "gz"), "gx", None, None, None),
            P(("gy", "gz"), "gx", None),
        ),
        out_specs=(P("gx", "gy", "gz"), P(("gy", "gz"), "gx", None)),
        check_vma=False,
    )
```

time: 84.8 us -> 153 us (1.80)
  Pallas kernels: 13.7 us -> 90.6 us
  local copies, waits for them, and re-layouts: 8.71 us -> 1.5 us
  waiting for transfers between devices: 8.96 us -> 6.65 us
    pallas_call x5 -> x8, Pallas kernels: 13.7 us -> 90.6 us  [the longest x1 81.3 us: per_device(): call(pick_kernel, 60, [HBM] * 7, (shape(RUNS, 1, 384), shape(RUNS, WIDTH)...]
    ppermute x5 -> x3, starting transfers between devices: 19.8 us -> 10.4 us  [the longest x1 3.54 us: per_device(): across = lax.ppermute(across, 'gx', outside_pairs)]
    all_to_all x1, starting transfers between devices: 10.6 us -> 16.8 us  [per_device(): lax.all_to_all(sent, 'gx', split_axis=0, concat_axis=0, tiled=True)]
    unnamed x27 -> x16, local copies, waits for them, and re-layouts: 6.71 us -> 0.78 us
    all_to_all x1, starting transfers between devices: 8.17 us -> 12.4 us  [per_device(): lax.all_to_all(sent_back, 'gx', split_axis=0, concat_axis=0, tiled=True)]
    all_to_all x1, waiting for transfers between devices: 4.04 us -> 0.01 us  [per_device(): lax.all_to_all(sent, 'gx', split_axis=0, concat_axis=0, tiled=True)]
    ppermute x1, waiting for transfers between devices: 0.01 us -> 3.92 us  [per_device(): z_before = lax.ppermute(z_faces[1], 'gz', up)]
    ppermute x5 -> x3, waiting for transfers between devices: 2.85 us -> 0.64 us  [the longest x1 0.62 us: per_device(): swapped = lax.ppermute(swap, 'gx', outside_pairs)]
  transfers between devices with their start and end apart: 11 -> 9, of which waited for: 4 -> 4; matrix products, arithmetic and copies ran while one was open for 3% -> 0% of each run, Pallas kernels for 9% -> 2%
where the time goes in v2:
time: 153 us; the launch traced here: 152 us
  Pallas kernels  90.6 us (59%)
  starting transfers between devices  52.4 us (34%)
  waiting for transfers between devices  6.65 us (4%)
    pallas_call x1, Pallas kernels, per_device(): call(pick_kernel, 60, [HBM] * 7, (shape(RUNS, 1, 384), shape(RUNS, WIDTH)...  81.3 us
    all_to_all x1, starting transfers between devices, per_device(): lax.all_to_all(sent, 'gx', split_axis=0, concat_axis=0, tiled=True)  16.8 us
    all_to_all x1, starting transfers between devices, per_device(): lax.all_to_all(sent_back, 'gx', split_axis=0, concat_axis=0, tiled=True)  12.4 us
    ppermute x1, starting transfers between devices, per_device(): z_after = lax.ppermute(z_faces[0], 'gz', down)  4.64 us
    ppermute x1, starting transfers between devices, per_device(): y_after = lax.ppermute(y_faces[0], 'gy', down)  4.37 us
    ppermute x1, waiting for transfers between devices, per_device(): z_before = lax.ppermute(z_faces[1], 'gz', up)  3.92 us
    ppermute x1, starting transfers between devices, per_device(): across = lax.ppermute(across, 'gx', outside_pairs)  3.54 us
    ppermute x1, starting transfers between devices, per_device(): swapped = lax.ppermute(swap, 'gx', outside_pairs)  3.47 us
  transfers between devices with their start and end apart: 9, of which 4 were waited for; matrix products, arithmetic and copies ran while one was open for 0% of the time, Pallas kernels for 2%

profile of v2, /device:TPU:1, one launch (start us, length us, event | category | flops | bytes accessed | tf_op | source)
XLA Modules:
  0.0 152.0 jit_solution(16185962762587262078)
XLA Ops:
  0.6 81.3 %shard_map.95 = (f32[32,1,384]{2,1,0:T(1,128)}, f32[32,128]{1,0:T(8,128)}, f32[56,128]{1,0:T(8,128)}, f32[2,16,128]{2,1,0:T(8,128)}, f32[2,8,128]{2,1,0:T(8,128)...) custom-call(f32[1024,128]{1,0:T(8,128)} %bitcast.22, s32[32,128]{1,0:T(8,128)} %bitcast.25, s32[32,128]{1,0:T(8,128)} %bitcast.27, ...), custom_call_target="tpu_custom_call" | custom-call | flops 2147483648 | bytes 4194304 | tf_op jit(solution)/shard_map/pallas_call | solution.py:421
  82.0 16.8 %all-to-all-start = ((f32[32,1,384]{2,1,0:T(1,128)}), f32[32,1,384]{2,1,0:T(1,128)S(1)}, u32[]{:S(2)}, u32[]{:S(2)}) async-start(f32[32,1,384]{2,1,0:T(1,128)} %get-tuple-element.20), calls=%async_computation | async-start | bytes 98304 | tf_op jit(solution)/shard_map/all_to_all | solution.py:436
  98.7 3.5 %collective-permute-start = (f32[1400,128]{1,0:T(8,128)}, f32[1400,128]{1,0:T(8,128)S(1)}, u32[]{:S(2)}, u32[]{:S(2)}) collective-permute-start(f32[1400,128]{1,0:T(8,128)} %get-tuple-element.21), channel_id=1, source_target_pairs={{0,496},{16,32},{32,16},{48,64},{64,48},{80,96},{96,80},{112,128},... | collective-permute-start | bytes 2150408 | tf_op jit(solution)/shard_map/ppermute | solution.py:438
  102.3 3.4 %collective-permute-start.1 = (f32[3960,128]{1,0:T(8,128)}, f32[3960,128]{1,0:T(8,128)S(1)}, u32[]{:S(2)}, u32[]{:S(2)}) collective-permute-start(f32[3960,128]{1,0:T(8,128)} %get-tuple-element.25), channel_id=1, source_target_pairs={{0,16},{16,0},{32,48},{48,32},{64,80},{80,64},{96,112},{112,96},{1... | collective-permute-start | bytes 6082568 | tf_op jit(solution)/shard_map/ppermute | solution.py:437
  105.6 0.7 slice_bitcast_fusion
  106.4 4.4 %collective-permute-start.3 = (f32[16,128]{1,0:T(8,128)S(1)}, f32[16,128]{1,0:T(8,128)S(1)}, u32[]{:S(2)}, u32[]{:S(2)}) collective-permute-start(f32[16,128]{1,0:T(8,128)S(1)} %get-tuple-element.38), channel_id=1, source_target_pairs={{0,12},{4,0},{8,4},{12,8},{1,13},{5,1},{9,5},{13,9},{2,14},{6,2},{... | collective-permute-start | bytes 24584 | tf_op jit(solution)/shard_map/ppermute | solution.py:442
  110.7 1.9 %collective-permute-start.2 = (f32[16,128]{1,0:T(8,128)S(1)}, f32[16,128]{1,0:T(8,128)S(1)}, u32[]{:S(2)}, u32[]{:S(2)}) collective-permute-start(f32[16,128]{1,0:T(8,128)S(1)} %get-tuple-element.39), channel_id=1, source_target_pairs={{0,4},{4,8},{8,12},{12,0},{1,5},{5,9},{9,13},{13,1},{2,6},{6,10},{... | collective-permute-start | bytes 24584 | tf_op jit(solution)/shard_map/ppermute | solution.py:441
  112.7 0.7 copy-done.3
  113.4 0.4 shard_map.96.added_own
  113.8 0.0 collective-permute-done.across_hbm
  113.9 0.5 shard_map.97
  114.4 2.0 %collective-permute-done.2.y_before = f32[16,128]{1,0:T(8,128)S(1)} collective-permute-done((f32[16,128]{1,0:T(8,128)S(1)}, f32[16,128]{1,0:T(8,128)S(1)}, u32[]{:S(2)}, u32[]{:S(2)}) %collective-permute-start.2) | collective-permute-done | bytes 8224 | tf_op jit(solution)/shard_map/ppermute | solution.py:441
  116.4 2.0 %shard_map.98 = (f32[5,24,128]{2,1,0:T(8,128)S(1)}, f32[5,24,128]{2,1,0:T(8,128)S(1)}, f32[8,128]{1,0:T(8,128)S(1)}, f32[2,64,128]{2,1,0:T(8,128)S(1)}, f32[2,16,128]{2,1,0:T(8,128)S(1)}) custom-call(f32[32,1,384]{2,1,0:T(1,128)S(1)} %all-to-all-done.arrived, f32[16,128]{1,0:T(8,128)S(1)} %get-tuple-element.23.added_before, ...), custom_call_target="tpu_custom_call" | custom-call | flops 16777216 | bytes 6291456 | tf_op jit(solution)/shard_map/pallas_call | solution.py:452
  118.3 3.5 %collective-permute-start.4 = (f32[8,128]{1,0:T(8,128)S(1)}, f32[8,128]{1,0:T(8,128)S(1)}, u32[]{:S(2)}, u32[]{:S(2)}) collective-permute-start(f32[8,128]{1,0:T(8,128)S(1)} %get-tuple-element.31), channel_id=1, source_target_pairs={{0,496},{16,32},{32,16},{48,64},{64,48},{80,96},{96,80},{112,128},... | collective-permute-start | bytes 12296 | tf_op jit(solution)/shard_map/ppermute | solution.py:460
  121.8 0.8 shard_map.99.inside
  122.6 0.6 collective-permute-done.4.swapped
  123.3 1.4 shard_map.100
  124.7 12.4 %all-to-all-start.1 = ((f32[32,1,128]{2,1,0:T(1,128)}), f32[32,1,128]{2,1,0:T(1,128)S(1)}, u32[]{:S(2)}, u32[]{:S(2)}) async-start(f32[32,1,128]{2,1,0:T(1,128)} %get-tuple-element.36), calls=%async_computation.1 | async-start | bytes 32768 | tf_op jit(solution)/shard_map/all_to_all | solution.py:478
  137.1 4.6 %collective-permute-start.6 = (f32[8,128]{1,0:T(8,128)S(1)}, f32[8,128]{1,0:T(8,128)S(1)}, u32[]{:S(2)}, u32[]{:S(2)}) collective-permute-start(f32[8,128]{1,0:T(8,128)S(1)} %get-tuple-element.40), channel_id=1, source_target_pairs={{0,3},{1,0},{2,1},{3,2},{4,7},{5,4},{6,5},{7,6},{8,11},{9,8},{10,9... | collective-permute-start | bytes 12296 | tf_op jit(solution)/shard_map/ppermute | solution.py:477
  141.8 1.9 %collective-permute-start.5 = (f32[8,128]{1,0:T(8,128)S(1)}, f32[8,128]{1,0:T(8,128)S(1)}, u32[]{:S(2)}, u32[]{:S(2)}) collective-permute-start(f32[8,128]{1,0:T(8,128)S(1)} %get-tuple-element.41), channel_id=1, source_target_pairs={{0,1},{1,2},{2,3},{3,0},{4,5},{5,6},{6,7},{7,4},{8,9},{9,10},{10,1... | collective-permute-start | bytes 12296 | tf_op jit(solution)/shard_map/ppermute | solution.py:476
  143.7 3.9 %collective-permute-done.5.z_before = f32[8,128]{1,0:T(8,128)S(1)} collective-permute-done((f32[8,128]{1,0:T(8,128)S(1)}, f32[8,128]{1,0:T(8,128)S(1)}, u32[]{:S(2)}, u32[]{:S(2)}) %collective-permute-start.5) | collective-permute-done | bytes 4128 | tf_op jit(solution)/shard_map/ppermute | solution.py:476
  147.6 1.0 shard_map.101.base
  148.7 0.1 all-to-all-done.1.returned
  148.8 3.2 %shard_map.102 = f32[1024,128]{1,0:T(8,128)} custom-call(f32[1024,128]{1,0:T(8,128)S(1)} %shard_map.101.base, s32[32,128]{1,0:T(8,128)S(1)} %bitcast.26, f32[32,128]{1,0:T(8,128)S(1)} %copy-done.6, f32[32,1,128]{2,1,0:T(1,128)S(1)} %all-to-all-done.1.returned), custom_call_target="tpu_custom_call" | custom-call | flops 2147483648 | bytes 1048576 | tf_op jit(solution)/shard_map/pallas_call | solution.py:487
  (20 shorter events, 0.1 us)
Async XLA Ops:
  82.0 30.7 %all-to-all-start = ((f32[32,1,384]{2,1,0:T(1,128)}), f32[32,1,384]{2,1,0:T(1,128)S(1)}, u32[]{:S(2)}, u32[]{:S(2)}) async-start(f32[32,1,384]{2,1,0:T(1,128)} %get-tuple-element.20), calls=%async_computation | async-start | bytes 98304 | tf_op jit(solution)/shard_map/all_to_all | solution.py:436
  98.7 15.1 %collective-permute-start = (f32[1400,128]{1,0:T(8,128)}, f32[1400,128]{1,0:T(8,128)S(1)}, u32[]{:S(2)}, u32[]{:S(2)}) collective-permute-start(f32[1400,128]{1,0:T(8,128)} %get-tuple-element.21), channel_id=1, source_target_pairs={{0,496},{16,32},{32,16},{48,64},{64,48},{80,96},{96,80},{112,128},... | collective-permute-start | bytes 2150408 | tf_op jit(solution)/shard_map/ppermute | solution.py:438
  102.3 14.1 %collective-permute-start.1 = (f32[3960,128]{1,0:T(8,128)}, f32[3960,128]{1,0:T(8,128)S(1)}, u32[]{:S(2)}, u32[]{:S(2)}) collective-permute-start(f32[3960,128]{1,0:T(8,128)} %get-tuple-element.25), channel_id=1, source_target_pairs={{0,16},{16,0},{32,48},{48,32},{64,80},{80,64},{96,112},{112,96},{1... | collective-permute-start | bytes 6082568 | tf_op jit(solution)/shard_map/ppermute | solution.py:437
  106.4 8.0 %collective-permute-start.3 = (f32[16,128]{1,0:T(8,128)S(1)}, f32[16,128]{1,0:T(8,128)S(1)}, u32[]{:S(2)}, u32[]{:S(2)}) collective-permute-start(f32[16,128]{1,0:T(8,128)S(1)} %get-tuple-element.38), channel_id=1, source_target_pairs={{0,12},{4,0},{8,4},{12,8},{1,13},{5,1},{9,5},{13,9},{2,14},{6,2},{... | collective-permute-start | bytes 24584 | tf_op jit(solution)/shard_map/ppermute | solution.py:442
  110.7 5.6 %collective-permute-start.2 = (f32[16,128]{1,0:T(8,128)S(1)}, f32[16,128]{1,0:T(8,128)S(1)}, u32[]{:S(2)}, u32[]{:S(2)}) collective-permute-start(f32[16,128]{1,0:T(8,128)S(1)} %get-tuple-element.39), channel_id=1, source_target_pairs={{0,4},{4,8},{8,12},{12,0},{1,5},{5,9},{9,13},{13,1},{2,6},{6,10},{... | collective-permute-start | bytes 24584 | tf_op jit(solution)/shard_map/ppermute | solution.py:441
  112.7 0.7 copy-start.3
  113.8 2.5 %copy-start = (f32[1,8,5,128,128]{4,3,2,1,0:T(8,128)S(1)}, f32[1,8,5,128,128]{4,3,2,1,0:T(8,128)}, u32[]{:S(2)}) copy-start(f32[1,8,5,128,128]{4,3,2,1,0:T(8,128)} %param.14) | copy-start | bytes 7864324
  113.8 2.5 %copy-start.4 = (f32[56,128]{1,0:T(8,128)S(1)}, f32[56,128]{1,0:T(8,128)}, u32[]{:S(2)}) copy-start(f32[56,128]{1,0:T(8,128)} %get-tuple-element.22.own) | copy-start | bytes 86020
  118.3 4.9 %collective-permute-start.4 = (f32[8,128]{1,0:T(8,128)S(1)}, f32[8,128]{1,0:T(8,128)S(1)}, u32[]{:S(2)}, u32[]{:S(2)}) collective-permute-start(f32[8,128]{1,0:T(8,128)S(1)} %get-tuple-element.31), channel_id=1, source_target_pairs={{0,496},{16,32},{32,16},{48,64},{64,48},{80,96},{96,80},{112,128},... | collective-permute-start | bytes 12296 | tf_op jit(solution)/shard_map/ppermute | solution.py:460
  122.6 14.5 %copy-start.7 = (f32[2,8,128]{2,1,0:T(8,128)S(1)}, f32[2,8,128]{2,1,0:T(8,128)}, u32[]{:S(2)}) copy-start(f32[2,8,128]{2,1,0:T(8,128)} %get-tuple-element.34) | copy-start | bytes 24580
  122.6 25.1 %copy-start.1 = (f32[16,64,128]{2,1,0:T(8,128)S(1)}, f32[16,64,128]{2,1,0:T(8,128)}, u32[]{:S(2)}) copy-start(f32[16,64,128]{2,1,0:T(8,128)} %param.8) | copy-start | bytes 1572868
  122.6 25.1 %copy-start.2 = (s32[16,64,128]{2,1,0:T(8,128)S(1)}, s32[16,64,128]{2,1,0:T(8,128)}, u32[]{:S(2)}) copy-start(s32[16,64,128]{2,1,0:T(8,128)} %param.9) | copy-start | bytes 1572868
  122.6 26.2 %copy-start.5 = (s32[32,1,1,128]{3,2,1,0:T(1,128)S(1)}, s32[32,1,1,128]{3,2,1,0:T(1,128)}, u32[]{:S(2)}) copy-start(s32[32,1,1,128]{3,2,1,0:T(1,128)} %param.10) | copy-start | bytes 49156
  122.6 26.2 %copy-start.6 = (f32[32,128]{1,0:T(8,128)S(1)}, f32[32,128]{1,0:T(8,128)}, u32[]{:S(2)}) copy-start(f32[32,128]{1,0:T(8,128)} %get-tuple-element.35.outgoing) | copy-start | bytes 49156
  124.7 24.2 %all-to-all-start.1 = ((f32[32,1,128]{2,1,0:T(1,128)}), f32[32,1,128]{2,1,0:T(1,128)S(1)}, u32[]{:S(2)}, u32[]{:S(2)}) async-start(f32[32,1,128]{2,1,0:T(1,128)} %get-tuple-element.36), calls=%async_computation.1 | async-start | bytes 32768 | tf_op jit(solution)/shard_map/all_to_all | solution.py:478
  137.1 6.6 %collective-permute-start.6 = (f32[8,128]{1,0:T(8,128)S(1)}, f32[8,128]{1,0:T(8,128)S(1)}, u32[]{:S(2)}, u32[]{:S(2)}) collective-permute-start(f32[8,128]{1,0:T(8,128)S(1)} %get-tuple-element.40), channel_id=1, source_target_pairs={{0,3},{1,0},{2,1},{3,2},{4,7},{5,4},{6,5},{7,6},{8,11},{9,8},{10,9... | collective-permute-start | bytes 12296 | tf_op jit(solution)/shard_map/ppermute | solution.py:477
  141.8 5.9 %collective-permute-start.5 = (f32[8,128]{1,0:T(8,128)S(1)}, f32[8,128]{1,0:T(8,128)S(1)}, u32[]{:S(2)}, u32[]{:S(2)}) collective-permute-start(f32[8,128]{1,0:T(8,128)S(1)} %get-tuple-element.41), channel_id=1, source_target_pairs={{0,1},{1,2},{2,3},{3,0},{4,5},{5,6},{6,7},{7,4},{8,9},{9,10},{10,1... | collective-permute-start | bytes 12296 | tf_op jit(solution)/shard_map/ppermute | solution.py:476

commit v3 on v2

--- a/solution.py
+++ b/solution.py
@@ -67,7 +67,7 @@
 def pick_kernel(
     fluid_hbm, src_hbm, dst_hbm, old_hbm, diag_hbm, pattern_hbm, blocks_hbm,
     sent, outgoing, own, y_faces, z_faces, on_chip_hbm, across_hbm,
-    fluid, src, dst, pattern, table, packed, sems,
+    fluid, src, dst, pattern, table, packed, staged_in, staged_out, sems,
 ):
     me = lax.axis_index("gx")
     parity = lax.rem(me, 2)
@@ -85,8 +85,8 @@
         copy(diag_hbm, own.at[40:48], 11),
         copy(pattern_hbm, pattern, 16),
     ]
-    inside = copy(blocks_hbm.at[pl.ds((1 - parity) * 2 * TILE_ROWS, 6 * TILE_ROWS)], on_chip_hbm.at[0 : 6 * TILE_ROWS], 12)
-    outside = copy(blocks_hbm.at[pl.ds(parity * 6 * TILE_ROWS, 2 * TILE_ROWS)], across_hbm.at[0 : 2 * TILE_ROWS], 13)
+    inside = copy(blocks_hbm.at[pl.ds((1 - parity) * 2 * TILE_ROWS, 6 * TILE_ROWS)], staged_in, 12)
+    outside = copy(blocks_hbm.at[pl.ds(parity * 6 * TILE_ROWS, 2 * TILE_ROWS)], staged_out, 13)
     for block in range(8):
         loads[block].wait()
         turned = fluid[128 * block : 128 * block + 128, :].T
@@ -98,6 +98,11 @@
     load_src.wait()
     group = 4
     for start in range(0, RUNS, group):
+        if start == RUNS // 2:
+            inside.wait()
+            outside.wait()
+            inside = copy(staged_in, on_chip_hbm.at[0 : 6 * TILE_ROWS], 17)
+            outside = copy(staged_out, across_hbm.at[0 : 2 * TILE_ROWS], 18)
         ids = lanes([src[r : r + 1, :] for r in range(start, start + group)])
         picked = jnp.dot(table[...], row_hots(ids >> 7, ROWS), preferred_element_type=F32)
         both = picked[0:128] + picked[128:256]
@@ -428,7 +433,7 @@
         (VMEM, VMEM, VMEM, VMEM, VMEM, HBM, HBM),
         [
             vmem(ROWS, WIDTH), vmem(RUNS, WIDTH, kind=I32), vmem(RUNS, WIDTH, kind=I32), vmem(NB, 1, TILES, kind=I32),
-            vmem(256, ROWS, kind=BF16), vmem(2, SMALL, WIDTH), dma(17),
+            vmem(256, ROWS, kind=BF16), vmem(2, SMALL, WIDTH), vmem(6 * TILE_ROWS, WIDTH), vmem(2 * TILE_ROWS, WIDTH), dma(19),
         ],
         2 * 256 * 1024 * 4096, 1 << 22,
     )(fluid, src, dst, solid_old[0], solid_diag[0], jnp.transpose(pattern, (2, 0, 1)), own_blocks)

time: 153 us -> 77 us (0.50)
  Pallas kernels: 90.6 us -> 15.1 us
    pallas_call x1, Pallas kernels: 81.3 us -> 5.8 us  [per_device(): call(pick_kernel, 60, [HBM] * 7, (shape(RUNS, 1, 384), shape(RUNS, WIDTH)...]
  transfers between devices with their start and end apart: 9 -> 9, of which waited for: 4 -> 4; matrix products, arithmetic and copies ran while one was open for 0% -> 1% of each run, Pallas kernels for 2% -> 4%
where the time goes in v3:
time: 77 us; the launch traced here: 76.5 us
  starting transfers between devices  52.4 us (68%)
  Pallas kernels  15.1 us (20%)
  waiting for transfers between devices  6.66 us (9%)
  local copies, waits for them, and re-layouts  1.5 us (2%)
  between operations  0.86 us (1%)
    all_to_all x1, starting transfers between devices, per_device(): lax.all_to_all(sent, 'gx', split_axis=0, concat_axis=0, tiled=True)  16.8 us
    all_to_all x1, starting transfers between devices, per_device(): lax.all_to_all(sent_back, 'gx', split_axis=0, concat_axis=0, tiled=True)  12.4 us
    pallas_call x1, Pallas kernels, per_device(): call(pick_kernel, 60, [HBM] * 7, (shape(RUNS, 1, 384), shape(RUNS, WIDTH)...  5.8 us
    ppermute x1, starting transfers between devices, per_device(): z_after = lax.ppermute(z_faces[0], 'gz', down)  4.63 us
    ppermute x1, starting transfers between devices, per_device(): y_after = lax.ppermute(y_faces[0], 'gy', down)  4.38 us
    ppermute x1, waiting for transfers between devices, per_device(): z_before = lax.ppermute(z_faces[1], 'gz', up)  3.92 us
    ppermute x1, starting transfers between devices, per_device(): across = lax.ppermute(across, 'gx', outside_pairs)  3.54 us
    ppermute x1, starting transfers between devices, per_device(): swapped = lax.ppermute(swap, 'gx', outside_pairs)  3.47 us
  transfers between devices with their start and end apart: 9, of which 4 were waited for; matrix products, arithmetic and copies ran while one was open for 1% of the time, Pallas kernels for 4%

profile of v3, /device:TPU:1, one launch (start us, length us, event | category | flops | bytes accessed | tf_op | source)
XLA Modules:
  0.0 76.5 jit_solution(11290096869459209554)
XLA Ops:
  0.6 5.8 %shard_map.95 = (f32[32,1,384]{2,1,0:T(1,128)}, f32[32,128]{1,0:T(8,128)}, f32[56,128]{1,0:T(8,128)}, f32[2,16,128]{2,1,0:T(8,128)}, f32[2,8,128]{2,1,0:T(8,128)...) custom-call(f32[1024,128]{1,0:T(8,128)} %bitcast.22, s32[32,128]{1,0:T(8,128)} %bitcast.25, s32[32,128]{1,0:T(8,128)} %bitcast.27, ...), custom_call_target="tpu_custom_call" | custom-call | flops 2147483648 | bytes 4194304 | tf_op jit(solution)/shard_map/pallas_call | solution.py:426
  6.4 16.8 %all-to-all-start = ((f32[32,1,384]{2,1,0:T(1,128)}), f32[32,1,384]{2,1,0:T(1,128)S(1)}, u32[]{:S(2)}, u32[]{:S(2)}) async-start(f32[32,1,384]{2,1,0:T(1,128)} %get-tuple-element.20), calls=%async_computation | async-start | bytes 98304 | tf_op jit(solution)/shard_map/all_to_all | solution.py:441
  23.2 3.5 %collective-permute-start = (f32[1400,128]{1,0:T(8,128)}, f32[1400,128]{1,0:T(8,128)S(1)}, u32[]{:S(2)}, u32[]{:S(2)}) collective-permute-start(f32[1400,128]{1,0:T(8,128)} %get-tuple-element.21), channel_id=1, source_target_pairs={{0,496},{16,32},{32,16},{48,64},{64,48},{80,96},{96,80},{112,128},... | collective-permute-start | bytes 2150408 | tf_op jit(solution)/shard_map/ppermute | solution.py:443
  26.8 3.4 %collective-permute-start.1 = (f32[3960,128]{1,0:T(8,128)}, f32[3960,128]{1,0:T(8,128)S(1)}, u32[]{:S(2)}, u32[]{:S(2)}) collective-permute-start(f32[3960,128]{1,0:T(8,128)} %get-tuple-element.25), channel_id=1, source_target_pairs={{0,16},{16,0},{32,48},{48,32},{64,80},{80,64},{96,112},{112,96},{1... | collective-permute-start | bytes 6082568 | tf_op jit(solution)/shard_map/ppermute | solution.py:442
  30.1 0.7 slice_bitcast_fusion
  30.8 4.4 %collective-permute-start.3 = (f32[16,128]{1,0:T(8,128)S(1)}, f32[16,128]{1,0:T(8,128)S(1)}, u32[]{:S(2)}, u32[]{:S(2)}) collective-permute-start(f32[16,128]{1,0:T(8,128)S(1)} %get-tuple-element.38), channel_id=1, source_target_pairs={{0,12},{4,0},{8,4},{12,8},{1,13},{5,1},{9,5},{13,9},{2,14},{6,2},{... | collective-permute-start | bytes 24584 | tf_op jit(solution)/shard_map/ppermute | solution.py:447
  35.2 1.9 %collective-permute-start.2 = (f32[16,128]{1,0:T(8,128)S(1)}, f32[16,128]{1,0:T(8,128)S(1)}, u32[]{:S(2)}, u32[]{:S(2)}) collective-permute-start(f32[16,128]{1,0:T(8,128)S(1)} %get-tuple-element.39), channel_id=1, source_target_pairs={{0,4},{4,8},{8,12},{12,0},{1,5},{5,9},{9,13},{13,1},{2,6},{6,10},{... | collective-permute-start | bytes 24584 | tf_op jit(solution)/shard_map/ppermute | solution.py:446
  37.2 0.7 copy-done.3
  37.9 0.4 shard_map.96.added_own
  38.3 0.0 collective-permute-done.across_hbm
  38.3 0.5 shard_map.97
  38.9 2.0 %collective-permute-done.2.y_before = f32[16,128]{1,0:T(8,128)S(1)} collective-permute-done((f32[16,128]{1,0:T(8,128)S(1)}, f32[16,128]{1,0:T(8,128)S(1)}, u32[]{:S(2)}, u32[]{:S(2)}) %collective-permute-start.2) | collective-permute-done | bytes 8224 | tf_op jit(solution)/shard_map/ppermute | solution.py:446
  40.8 2.0 %shard_map.98 = (f32[5,24,128]{2,1,0:T(8,128)S(1)}, f32[5,24,128]{2,1,0:T(8,128)S(1)}, f32[8,128]{1,0:T(8,128)S(1)}, f32[2,64,128]{2,1,0:T(8,128)S(1)}, f32[2,16,128]{2,1,0:T(8,128)S(1)}) custom-call(f32[32,1,384]{2,1,0:T(1,128)S(1)} %all-to-all-done.arrived, f32[16,128]{1,0:T(8,128)S(1)} %get-tuple-element.23.added_before, ...), custom_call_target="tpu_custom_call" | custom-call | flops 16777216 | bytes 6291456 | tf_op jit(solution)/shard_map/pallas_call | solution.py:457
  42.8 3.5 %collective-permute-start.4 = (f32[8,128]{1,0:T(8,128)S(1)}, f32[8,128]{1,0:T(8,128)S(1)}, u32[]{:S(2)}, u32[]{:S(2)}) collective-permute-start(f32[8,128]{1,0:T(8,128)S(1)} %get-tuple-element.31), channel_id=1, source_target_pairs={{0,496},{16,32},{32,16},{48,64},{64,48},{80,96},{96,80},{112,128},... | collective-permute-start | bytes 12296 | tf_op jit(solution)/shard_map/ppermute | solution.py:465
  46.3 0.8 shard_map.99.inside
  47.1 0.6 collective-permute-done.4.swapped
  47.7 1.4 %shard_map.100 = (f32[8,128]{1,0:T(8,128)}, f32[32,1,128]{2,1,0:T(1,128)}) custom-call(f32[5,24,128]{2,1,0:T(8,128)S(1)} %get-tuple-element.29.state, f32[5,24,128]{2,1,0:T(8,128)S(1)} %get-tuple-element.30.pats, f32[3,24,128]{2,1,0:T(8,128)S(1)} %shard_map.99.inside, f32[8,128]{1,0:T(8,128)S(1)} %collective-permute-done.4.swapped, f32[56,128]{1,0:T(8,128)S(1)} %copy-done.4, ...), custom_call_target="tpu_custom_call" | custom-call | flops 8388608 | bytes 3145728 | tf_op jit(solution)/shard_map/pallas_call | solution.py:473
  49.2 12.4 %all-to-all-start.1 = ((f32[32,1,128]{2,1,0:T(1,128)}), f32[32,1,128]{2,1,0:T(1,128)S(1)}, u32[]{:S(2)}, u32[]{:S(2)}) async-start(f32[32,1,128]{2,1,0:T(1,128)} %get-tuple-element.36), calls=%async_computation.1 | async-start | bytes 32768 | tf_op jit(solution)/shard_map/all_to_all | solution.py:483
  61.6 4.6 %collective-permute-start.6 = (f32[8,128]{1,0:T(8,128)S(1)}, f32[8,128]{1,0:T(8,128)S(1)}, u32[]{:S(2)}, u32[]{:S(2)}) collective-permute-start(f32[8,128]{1,0:T(8,128)S(1)} %get-tuple-element.40), channel_id=1, source_target_pairs={{0,3},{1,0},{2,1},{3,2},{4,7},{5,4},{6,5},{7,6},{8,11},{9,8},{10,9... | collective-permute-start | bytes 12296 | tf_op jit(solution)/shard_map/ppermute | solution.py:482
  66.3 1.9 %collective-permute-start.5 = (f32[8,128]{1,0:T(8,128)S(1)}, f32[8,128]{1,0:T(8,128)S(1)}, u32[]{:S(2)}, u32[]{:S(2)}) collective-permute-start(f32[8,128]{1,0:T(8,128)S(1)} %get-tuple-element.41), channel_id=1, source_target_pairs={{0,1},{1,2},{2,3},{3,0},{4,5},{5,6},{6,7},{7,4},{8,9},{9,10},{10,1... | collective-permute-start | bytes 12296 | tf_op jit(solution)/shard_map/ppermute | solution.py:481
  68.2 3.9 %collective-permute-done.5.z_before = f32[8,128]{1,0:T(8,128)S(1)} collective-permute-done((f32[8,128]{1,0:T(8,128)S(1)}, f32[8,128]{1,0:T(8,128)S(1)}, u32[]{:S(2)}, u32[]{:S(2)}) %collective-permute-start.5) | collective-permute-done | bytes 4128 | tf_op jit(solution)/shard_map/ppermute | solution.py:481
  72.1 1.0 %shard_map.101.base = f32[1024,128]{1,0:T(8,128)S(1)} custom-call(f32[1024,128]{1,0:T(8,128)S(1)} %bitcast.23, s32[1024,128]{1,0:T(8,128)S(1)} %bitcast.24, f32[2,64,128]{2,1,0:T(8,128)S(1)} %get-tuple-element.27.x_faces, f32[2,16,128]{2,1,0:T(8,128)S(1)} %get-tuple-element.28.y_faces, f32[8,128]{1,0:T(8,128)S(1)} %collective-permute-done.5.z_before, ...), custom_call_target="tpu_custom_call" | custom-call | flops 4194304 | bytes 2097152 | tf_op jit(solution)/shard_map/pallas_call | solution.py:485
  73.2 0.1 all-to-all-done.1.returned
  73.3 3.2 %shard_map.102 = f32[1024,128]{1,0:T(8,128)} custom-call(f32[1024,128]{1,0:T(8,128)S(1)} %shard_map.101.base, s32[32,128]{1,0:T(8,128)S(1)} %bitcast.26, f32[32,128]{1,0:T(8,128)S(1)} %copy-done.6, f32[32,1,128]{2,1,0:T(1,128)S(1)} %all-to-all-done.1.returned), custom_call_target="tpu_custom_call" | custom-call | flops 2147483648 | bytes 1048576 | tf_op jit(solution)/shard_map/pallas_call | solution.py:492
  (20 shorter events, 0.1 us)
Async XLA Ops:
  6.4 30.7 %all-to-all-start = ((f32[32,1,384]{2,1,0:T(1,128)}), f32[32,1,384]{2,1,0:T(1,128)S(1)}, u32[]{:S(2)}, u32[]{:S(2)}) async-start(f32[32,1,384]{2,1,0:T(1,128)} %get-tuple-element.20), calls=%async_computation | async-start | bytes 98304 | tf_op jit(solution)/shard_map/all_to_all | solution.py:441
  23.2 15.1 %collective-permute-start = (f32[1400,128]{1,0:T(8,128)}, f32[1400,128]{1,0:T(8,128)S(1)}, u32[]{:S(2)}, u32[]{:S(2)}) collective-permute-start(f32[1400,128]{1,0:T(8,128)} %get-tuple-element.21), channel_id=1, source_target_pairs={{0,496},{16,32},{32,16},{48,64},{64,48},{80,96},{96,80},{112,128},... | collective-permute-start | bytes 2150408 | tf_op jit(solution)/shard_map/ppermute | solution.py:443
  26.8 14.1 %collective-permute-start.1 = (f32[3960,128]{1,0:T(8,128)}, f32[3960,128]{1,0:T(8,128)S(1)}, u32[]{:S(2)}, u32[]{:S(2)}) collective-permute-start(f32[3960,128]{1,0:T(8,128)} %get-tuple-element.25), channel_id=1, source_target_pairs={{0,16},{16,0},{32,48},{48,32},{64,80},{80,64},{96,112},{112,96},{1... | collective-permute-start | bytes 6082568 | tf_op jit(solution)/shard_map/ppermute | solution.py:442
  30.8 8.0 %collective-permute-start.3 = (f32[16,128]{1,0:T(8,128)S(1)}, f32[16,128]{1,0:T(8,128)S(1)}, u32[]{:S(2)}, u32[]{:S(2)}) collective-permute-start(f32[16,128]{1,0:T(8,128)S(1)} %get-tuple-element.38), channel_id=1, source_target_pairs={{0,12},{4,0},{8,4},{12,8},{1,13},{5,1},{9,5},{13,9},{2,14},{6,2},{... | collective-permute-start | bytes 24584 | tf_op jit(solution)/shard_map/ppermute | solution.py:447
  35.2 5.6 %collective-permute-start.2 = (f32[16,128]{1,0:T(8,128)S(1)}, f32[16,128]{1,0:T(8,128)S(1)}, u32[]{:S(2)}, u32[]{:S(2)}) collective-permute-start(f32[16,128]{1,0:T(8,128)S(1)} %get-tuple-element.39), channel_id=1, source_target_pairs={{0,4},{4,8},{8,12},{12,0},{1,5},{5,9},{9,13},{13,1},{2,6},{6,10},{... | collective-permute-start | bytes 24584 | tf_op jit(solution)/shard_map/ppermute | solution.py:446
  37.2 0.7 copy-start.3
  38.3 2.5 %copy-start = (f32[1,8,5,128,128]{4,3,2,1,0:T(8,128)S(1)}, f32[1,8,5,128,128]{4,3,2,1,0:T(8,128)}, u32[]{:S(2)}) copy-start(f32[1,8,5,128,128]{4,3,2,1,0:T(8,128)} %param.14) | copy-start | bytes 7864324
  38.3 2.5 %copy-start.4 = (f32[56,128]{1,0:T(8,128)S(1)}, f32[56,128]{1,0:T(8,128)}, u32[]{:S(2)}) copy-start(f32[56,128]{1,0:T(8,128)} %get-tuple-element.22.own) | copy-start | bytes 86020
  42.8 4.9 %collective-permute-start.4 = (f32[8,128]{1,0:T(8,128)S(1)}, f32[8,128]{1,0:T(8,128)S(1)}, u32[]{:S(2)}, u32[]{:S(2)}) collective-permute-start(f32[8,128]{1,0:T(8,128)S(1)} %get-tuple-element.31), channel_id=1, source_target_pairs={{0,496},{16,32},{32,16},{48,64},{64,48},{80,96},{96,80},{112,128},... | collective-permute-start | bytes 12296 | tf_op jit(solution)/shard_map/ppermute | solution.py:465
  47.0 14.5 %copy-start.7 = (f32[2,8,128]{2,1,0:T(8,128)S(1)}, f32[2,8,128]{2,1,0:T(8,128)}, u32[]{:S(2)}) copy-start(f32[2,8,128]{2,1,0:T(8,128)} %get-tuple-element.34) | copy-start | bytes 24580
  47.1 25.1 %copy-start.1 = (f32[16,64,128]{2,1,0:T(8,128)S(1)}, f32[16,64,128]{2,1,0:T(8,128)}, u32[]{:S(2)}) copy-start(f32[16,64,128]{2,1,0:T(8,128)} %param.8) | copy-start | bytes 1572868
  47.1 25.0 %copy-start.2 = (s32[16,64,128]{2,1,0:T(8,128)S(1)}, s32[16,64,128]{2,1,0:T(8,128)}, u32[]{:S(2)}) copy-start(s32[16,64,128]{2,1,0:T(8,128)} %param.9) | copy-start | bytes 1572868
  47.1 26.2 %copy-start.5 = (s32[32,1,1,128]{3,2,1,0:T(1,128)S(1)}, s32[32,1,1,128]{3,2,1,0:T(1,128)}, u32[]{:S(2)}) copy-start(s32[32,1,1,128]{3,2,1,0:T(1,128)} %param.10) | copy-start | bytes 49156
  47.1 26.2 %copy-start.6 = (f32[32,128]{1,0:T(8,128)S(1)}, f32[32,128]{1,0:T(8,128)}, u32[]{:S(2)}) copy-start(f32[32,128]{1,0:T(8,128)} %get-tuple-element.35.outgoing) | copy-start | bytes 49156
  49.2 24.2 %all-to-all-start.1 = ((f32[32,1,128]{2,1,0:T(1,128)}), f32[32,1,128]{2,1,0:T(1,128)S(1)}, u32[]{:S(2)}, u32[]{:S(2)}) async-start(f32[32,1,128]{2,1,0:T(1,128)} %get-tuple-element.36), calls=%async_computation.1 | async-start | bytes 32768 | tf_op jit(solution)/shard_map/all_to_all | solution.py:483
  61.6 6.6 %collective-permute-start.6 = (f32[8,128]{1,0:T(8,128)S(1)}, f32[8,128]{1,0:T(8,128)S(1)}, u32[]{:S(2)}, u32[]{:S(2)}) collective-permute-start(f32[8,128]{1,0:T(8,128)S(1)} %get-tuple-element.40), channel_id=1, source_target_pairs={{0,3},{1,0},{2,1},{3,2},{4,7},{5,4},{6,5},{7,6},{8,11},{9,8},{10,9... | collective-permute-start | bytes 12296 | tf_op jit(solution)/shard_map/ppermute | solution.py:482
  66.3 5.9 %collective-permute-start.5 = (f32[8,128]{1,0:T(8,128)S(1)}, f32[8,128]{1,0:T(8,128)S(1)}, u32[]{:S(2)}, u32[]{:S(2)}) collective-permute-start(f32[8,128]{1,0:T(8,128)S(1)} %get-tuple-element.41), channel_id=1, source_target_pairs={{0,1},{1,2},{2,3},{3,0},{4,5},{5,6},{6,7},{7,4},{8,9},{9,10},{10,1... | collective-permute-start | bytes 12296 | tf_op jit(solution)/shard_map/ppermute | solution.py:481

commit v4 on v2

--- a/solution.py
+++ b/solution.py
@@ -16,6 +16,7 @@
 WIN = 24
 TILE_ROWS = NB * WIDTH
 SMALL = 120
+FACE_ROWS = 128
 
 DIFFUSION = 0.12
 EVAPORATION = 0.5
@@ -66,8 +67,8 @@
 
 def pick_kernel(
     fluid_hbm, src_hbm, dst_hbm, old_hbm, diag_hbm, pattern_hbm, blocks_hbm,
-    sent, outgoing, own, y_faces, z_faces, on_chip_hbm, across_hbm,
-    fluid, src, dst, pattern, table, packed, sems,
+    sent, outgoing, own, faces_hbm, on_chip_hbm, across_hbm,
+    fluid, src, dst, pattern, table, packed, staged_in, staged_out, faces, sems,
 ):
     me = lax.axis_index("gx")
     parity = lax.rem(me, 2)
@@ -83,18 +84,29 @@
         copy(dst_hbm, dst, 9),
         copy(old_hbm, own.at[32:40], 10),
         copy(diag_hbm, own.at[40:48], 11),
-        copy(pattern_hbm, pattern, 16),
+        copy(pattern_hbm, pattern, 12),
     ]
-    inside = copy(blocks_hbm.at[pl.ds((1 - parity) * 2 * TILE_ROWS, 6 * TILE_ROWS)], on_chip_hbm.at[0 : 6 * TILE_ROWS], 12)
-    outside = copy(blocks_hbm.at[pl.ds(parity * 6 * TILE_ROWS, 2 * TILE_ROWS)], across_hbm.at[0 : 2 * TILE_ROWS], 13)
+    pieces = []
+    for count, first, staged, target in (
+        (2, parity * 6, staged_out, across_hbm),
+        (6, (1 - parity) * 2, staged_in, on_chip_hbm),
+    ):
+        for tile in range(count):
+            at = slice(tile * TILE_ROWS, (tile + 1) * TILE_ROWS)
+            load = copy(blocks_hbm.at[pl.ds((first + tile) * TILE_ROWS, TILE_ROWS)], staged.at[at], 16 + len(pieces))
+            pieces.append((load, staged.at[at], target.at[at]))
     for block in range(8):
         loads[block].wait()
         turned = fluid[128 * block : 128 * block + 128, :].T
         high, low = two_parts(turned)
         table[0:128, 128 * block : 128 * block + 128] = high
         table[128:256, 128 * block : 128 * block + 128] = low
-        z_faces[0, block : block + 1, :] = turned[0:1, :]
-        z_faces[1, block : block + 1, :] = turned[127:128, :]
+        faces[32 + block : 33 + block, :] = turned[0:1, :]
+        faces[40 + block : 41 + block, :] = turned[127:128, :]
+    for slab in range(16):
+        faces[slab : slab + 1, :] = fluid[64 * slab : 64 * slab + 1, :]
+        faces[16 + slab : 17 + slab, :] = fluid[64 * slab + 63 : 64 * slab + 64, :]
+    save_faces = copy(faces, faces_hbm.at[0:48], 13)
     load_src.wait()
     group = 4
     for start in range(0, RUNS, group):
@@ -110,9 +122,10 @@
             sent[r ^ 1, :, 128:256] = mine
             beside = (r + 1) % RUNS if r % 2 else (r - 1) % RUNS
             sent[beside, :, 256:384] = mine
-    for slab in range(16):
-        y_faces[0, slab : slab + 1, :] = fluid[64 * slab : 64 * slab + 1, :]
-        y_faces[1, slab : slab + 1, :] = fluid[64 * slab + 63 : 64 * slab + 64, :]
+        index = start // group
+        load, staged, target = pieces[index]
+        load.wait()
+        pieces[index] = copy(staged, target, 24 + index)
     for each in small:
         each.wait()
     own[0:32, :] = dst[...].astype(F32)
@@ -125,7 +138,7 @@
         packed[index, 56:120, :] = face
     tail_in = copy(packed.at[0], on_chip_hbm.at[6 * TILE_ROWS : 6 * TILE_ROWS + SMALL], 14)
     tail_out = copy(packed.at[1], across_hbm.at[2 * TILE_ROWS : 2 * TILE_ROWS + SMALL], 15)
-    for each in (inside, outside, tail_in, tail_out):
+    for each in (*pieces, tail_in, tail_out, save_faces):
         each.wait()
 
 
@@ -195,8 +208,8 @@
 
 
 def wall_first_kernel(
-    arrived, added_before, beside_small, own, own_blocks, on_chip_hbm, across_hbm, y_before, y_after,
-    state, pats, swap, faces, y_faces,
+    arrived, added_before, beside_small, own, own_blocks, on_chip_hbm, across_hbm,
+    state, pats, swap, faces,
     inner, outer, iterate, shifted, coupled, sems,
 ):
     me = lax.axis_index("gx")
@@ -229,7 +242,6 @@
     right = window(parity, *rights)
     inverse = window(parity, *inverses)
     diagonal = window(parity, *diagonals)
-    y_faces[0], y_faces[1] = y_before[...], y_after[...]
     faces[0] = jnp.where(parity == 0, beside[56:120], partner[56:120])
     faces[1] = jnp.where(parity == 0, partner[56:120], beside[56:120])
     value = inverse * right
@@ -340,11 +352,19 @@
             returned[8 * block + r] = found[r : r + 1, :]
 
 
-def stencil_kernel(fluid_hbm, liquid_hbm, x_faces, y_faces, z_before, z_after, base, fluid, liquid, sems):
+def stencil_kernel(fluid_hbm, liquid_hbm, x_faces, faces_hbm, base, fluid, liquid, faces, sems):
     loads = [
         pltpu.make_async_copy(fluid_hbm, fluid, sems.at[0]),
         pltpu.make_async_copy(liquid_hbm, liquid, sems.at[1]),
     ]
+    y, z = lax.axis_index("gy"), lax.axis_index("gz")
+    before_y, after_y = lax.rem(y + 3, 4) * 4 + z, lax.rem(y + 1, 4) * 4 + z
+    before_z, after_z = y * 4 + lax.rem(z + 3, 4), y * 4 + lax.rem(z + 1, 4)
+    for index, (holder, first, count) in enumerate((
+        (before_y, 16, 16), (after_y, 0, 16), (before_z, 40, 8), (after_z, 32, 8),
+    )):
+        target = faces.at[16 * index : 16 * index + count]
+        loads.append(pltpu.make_async_copy(faces_hbm.at[holder, first : first + count], target, sems.at[2 + index]))
     for each in loads:
         each.start()
     row = lax.broadcasted_iota(I32, (64, WIDTH), 0)
@@ -358,11 +378,11 @@
         total = (fluid[start - 64 : start, :] if slab else x_faces[0]) + (
             fluid[start + 64 : start + 128, :] if slab < 15 else x_faces[1]
         )
-        total = total + jnp.where(row == 0, y_faces[0, slab : slab + 1, :], pltpu.roll(here, 1, 0))
-        total = total + jnp.where(row == 63, y_faces[1, slab : slab + 1, :], pltpu.roll(here, 63, 0))
+        total = total + jnp.where(row == 0, faces[slab : slab + 1, :], pltpu.roll(here, 1, 0))
+        total = total + jnp.where(row == 63, faces[16 + slab : 17 + slab, :], pltpu.roll(here, 63, 0))
         half = 64 * (slab % 2)
-        left = jnp.broadcast_to(z_before[block : block + 1, :], (WIDTH, WIDTH)).T[half : half + 64, :]
-        right = jnp.broadcast_to(z_after[block : block + 1, :], (WIDTH, WIDTH)).T[half : half + 64, :]
+        left = jnp.broadcast_to(faces[32 + block : 33 + block, :], (WIDTH, WIDTH)).T[half : half + 64, :]
+        right = jnp.broadcast_to(faces[48 + block : 49 + block, :], (WIDTH, WIDTH)).T[half : half + 64, :]
         total = total + jnp.where(lane == 0, left, pltpu.roll(here, 1, 1))
         total = total + jnp.where(lane == 127, right, pltpu.roll(here, 127, 1))
         total = total - 6.0 * here
@@ -418,17 +438,17 @@
     own_blocks = blocks.reshape(TILES * TILE_ROWS, WIDTH)
     in_rows, out_rows = 6 * TILE_ROWS + SMALL, 2 * TILE_ROWS + SMALL
 
-    sent, outgoing, own, y_faces, z_faces, on_chip, across = call(
+    sent, outgoing, own, faces, on_chip, across = call(
         pick_kernel, 60,
         [HBM] * 7,
         (
-            shape(RUNS, 1, 384), shape(RUNS, WIDTH), shape(56, WIDTH), shape(2, 16, WIDTH), shape(2, 8, WIDTH),
+            shape(RUNS, 1, 384), shape(RUNS, WIDTH), shape(56, WIDTH), shape(FACE_ROWS, WIDTH),
             shape(in_rows, WIDTH), shape(out_rows, WIDTH),
         ),
-        (VMEM, VMEM, VMEM, VMEM, VMEM, HBM, HBM),
+        (VMEM, VMEM, VMEM, HBM, HBM, HBM),
         [
             vmem(ROWS, WIDTH), vmem(RUNS, WIDTH, kind=I32), vmem(RUNS, WIDTH, kind=I32), vmem(NB, 1, TILES, kind=I32),
-            vmem(256, ROWS, kind=BF16), vmem(2, SMALL, WIDTH), dma(17),
+            vmem(256, ROWS, kind=BF16), vmem(2, SMALL, WIDTH), vmem(6 * TILE_ROWS, WIDTH), vmem(2 * TILE_ROWS, WIDTH), vmem(48, WIDTH), dma(32),
         ],
         2 * 256 * 1024 * 4096, 1 << 22,
     )(fluid, src, dst, solid_old[0], solid_diag[0], jnp.transpose(pattern, (2, 0, 1)), own_blocks)
@@ -436,10 +456,7 @@
     arrived = lax.all_to_all(sent, "gx", split_axis=0, concat_axis=0, tiled=True)
     on_chip = lax.ppermute(on_chip, "gx", inside_pairs)
     across = lax.ppermute(across, "gx", outside_pairs)
-    up = [(i, (i + 1) % 4) for i in range(4)]
-    down = [(i, (i - 1) % 4) for i in range(4)]
-    y_before = lax.ppermute(y_faces[1], "gy", up)
-    y_after = lax.ppermute(y_faces[0], "gy", down)
+    faces = lax.all_gather(faces, ("gy", "gz"), axis=0, tiled=False)
 
     work = [vmem(WIN, WIDTH), vmem(NB, WIN, WIDTH), vmem(WIN, WIDTH)]
     added_own = call(
@@ -449,14 +466,14 @@
         beside_run_kernel, 12, [VMEM, ANY, VMEM], (shape(2 * TILES, WIDTH), shape(SMALL, WIDTH)), (VMEM, VMEM), [dma()],
         14 * 10**9, 1 << 16,
     )(arrived, across, added_own)
-    state, pats, swap, x_faces, y_faces = call(
+    state, pats, swap, x_faces = call(
         wall_first_kernel, 16,
-        [VMEM, VMEM, VMEM, VMEM, VMEM, ANY, ANY, VMEM, VMEM],
-        (shape(5, WIN, WIDTH), shape(NB, WIN, WIDTH), shape(8, WIDTH), shape(2, 64, WIDTH), shape(2, 16, WIDTH)),
-        (VMEM,) * 5,
+        [VMEM, VMEM, VMEM, VMEM, VMEM, ANY, ANY],
+        (shape(5, WIN, WIDTH), shape(NB, WIN, WIDTH), shape(8, WIDTH), shape(2, 64, WIDTH)),
+        (VMEM,) * 4,
         [vmem(in_rows, WIDTH), vmem(2 * TILE_ROWS, WIDTH)] + work + [dma(3)],
         1 << 24, 6 << 20,
-    )(arrived, added_before, beside_small, own, own_blocks, on_chip, across, y_before, y_after)
+    )(arrived, added_before, beside_small, own, own_blocks, on_chip, across)
     swapped = lax.ppermute(swap, "gx", outside_pairs)
     inside = call(
         wall_inner_kernel, 12,
@@ -472,18 +489,15 @@
         [vmem(2 * TILE_ROWS, WIDTH)] + work + [dma()],
         1 << 23, 3 << 20,
     )(state, pats, inside, swapped, own, own_blocks, across)
-    sent_back, z_faces = lax.optimization_barrier((sent_back, z_faces))
-    z_before = lax.ppermute(z_faces[1], "gz", up)
-    z_after = lax.ppermute(z_faces[0], "gz", down)
     returned = lax.all_to_all(sent_back, "gx", split_axis=0, concat_axis=0, tiled=True)
 
     base = call(
         stencil_kernel, 12,
-        [HBM, HBM, VMEM, VMEM, VMEM, VMEM],
+        [HBM, HBM, VMEM, ANY],
         shape(ROWS, WIDTH), VMEM,
-        [vmem(ROWS, WIDTH), vmem(ROWS, WIDTH, kind=I32), dma(2)],
+        [vmem(ROWS, WIDTH), vmem(ROWS, WIDTH, kind=I32), vmem(64, WIDTH), dma(6)],
         1 << 22, 1 << 21,
-    )(fluid, liquid.reshape(ROWS, WIDTH), x_faces, y_faces, z_before, z_after)
+    )(fluid, liquid.reshape(ROWS, WIDTH), x_faces, faces)
     fluid_new = call(
         final_kernel, 16, [VMEM] * 4, shape(ROWS, WIDTH), VMEM, [], 2 * 256 * 1024 * 4096, 1 << 20
     )(base, src, outgoing, returned)

time: 153 us -> 106 us (0.69)
  Pallas kernels: 90.6 us -> 16.4 us
  waiting for transfers between devices: 6.65 us -> 32 us
  between operations: 0.86 us -> 14.2 us
  starting transfers between devices: 52.4 us -> 39.9 us
  local copies, waits for them, and re-layouts: 1.5 us -> 3.04 us
    pallas_call x1, Pallas kernels: 81.3 us -> 7.08 us  [per_device(): call(pick_kernel, 60, [HBM] * 7, (shape(RUNS, 1, 384), shape(RUNS, WIDTH)...]
    all_gather x0 -> x1, waiting for transfers between devices: none -> 25.6 us  [per_device(): faces = lax.all_gather(faces, ('gy', 'gz'), axis=0, tiled=False)]
    ppermute x4 -> x0, starting transfers between devices: 12.9 us -> none  [the longest x1 4.64 us: per_device(): z_after = lax.ppermute(z_faces[0], 'gz', down)]
    ppermute x4 -> x0, waiting for transfers between devices: 5.88 us -> none  [the longest x1 3.92 us: per_device(): z_before = lax.ppermute(z_faces[1], 'gz', up)]
    all_to_all x1, waiting for transfers between devices: 0.01 us -> 5.55 us  [per_device(): lax.all_to_all(sent, 'gx', split_axis=0, concat_axis=0, tiled=True)]
    unnamed x16, local copies, waits for them, and re-layouts: 0.78 us -> 3.04 us
  transfers between devices with their start and end apart: 9 -> 6, of which waited for: 4 -> 4; matrix products, arithmetic and copies ran while one was open for 0% -> 0% of each run, Pallas kernels for 2% -> 6%
where the time goes in v4:
time: 106 us; the launch traced here: 105 us
  starting transfers between devices  39.9 us (38%)
  waiting for transfers between devices  32 us (30%)
  Pallas kernels  16.4 us (15%)
  between operations  14.2 us (13%)
  local copies, waits for them, and re-layouts  3.04 us (3%)
    all_gather x1, waiting for transfers between devices, per_device(): faces = lax.all_gather(faces, ('gy', 'gz'), axis=0, tiled=False)  25.6 us
    all_to_all x1, starting transfers between devices, per_device(): lax.all_to_all(sent, 'gx', split_axis=0, concat_axis=0, tiled=True)  16.8 us
    all_to_all x1, starting transfers between devices, per_device(): lax.all_to_all(sent_back, 'gx', split_axis=0, concat_axis=0, tiled=True)  12.7 us
    pallas_call x1, Pallas kernels, per_device(): call(pick_kernel, 60, [HBM] * 7, (shape(RUNS, 1, 384), shape(RUNS, WIDTH)...  7.08 us
    all_to_all x1, waiting for transfers between devices, per_device(): lax.all_to_all(sent, 'gx', split_axis=0, concat_axis=0, tiled=True)  5.55 us
    ppermute x1, starting transfers between devices, per_device(): across = lax.ppermute(across, 'gx', outside_pairs)  3.54 us
    ppermute x1, starting transfers between devices, per_device(): swapped = lax.ppermute(swap, 'gx', outside_pairs)  3.51 us
    ppermute x1, starting transfers between devices, per_device(): on_chip = lax.ppermute(on_chip, 'gx', inside_pairs)  3.35 us
  transfers between devices with their start and end apart: 6, of which 4 were waited for; matrix products, arithmetic and copies ran while one was open for 0% of the time, Pallas kernels for 6%

profile of v4, /device:TPU:1, one launch (start us, length us, event | category | flops | bytes accessed | tf_op | source)
XLA Modules:
  0.0 105.5 jit_solution(15573983172835752654)
XLA Ops:
  7.2 7.1 %shard_map.95 = (f32[32,1,384]{2,1,0:T(1,128)}, f32[32,128]{1,0:T(8,128)}, f32[56,128]{1,0:T(8,128)}, f32[128,128]{1,0:T(8,128)}, f32[3960,128]{1,0:T(8,128)}, /*index=5*/f32[1400,128]{1,0:T(8,128)}) custom-call(f32[1024,128]{1,0:T(8,128)} %bitcast.16, s32[32,128]{1,0:T(8,128)} %bitcast.19, s32[32,128]{1,0:T(8,128)} %bitcast.21, f32[8,128]{1,0:T(8,128)} %bitcast.22, ...), custom_call_target="tpu_custom_call" | custom-call | flops 2147483648 | bytes 4194304 | tf_op jit(solution)/shard_map/pallas_call | solution.py:441
  14.3 16.8 %all-to-all-start = ((f32[32,1,384]{2,1,0:T(1,128)}), f32[32,1,384]{2,1,0:T(1,128)S(1)}, u32[]{:S(2)}, u32[]{:S(2)}) async-start(f32[32,1,384]{2,1,0:T(1,128)} %get-tuple-element.16), calls=%async_computation | async-start | bytes 98304 | tf_op jit(solution)/shard_map/all_to_all | solution.py:456
  31.0 0.0 all-gather.3.cloned.1.call-start
  31.1 3.5 %collective-permute-start = (f32[1400,128]{1,0:T(8,128)}, f32[1400,128]{1,0:T(8,128)S(1)}, u32[]{:S(2)}, u32[]{:S(2)}) collective-permute-start(f32[1400,128]{1,0:T(8,128)} %get-tuple-element.17), channel_id=1, source_target_pairs={{0,496},{16,32},{32,16},{48,64},{64,48},{80,96},{96,80},{112,128},... | collective-permute-start | bytes 2150408 | tf_op jit(solution)/shard_map/ppermute | solution.py:458
  34.6 3.4 %collective-permute-start.1 = (f32[3960,128]{1,0:T(8,128)}, f32[3960,128]{1,0:T(8,128)S(1)}, u32[]{:S(2)}, u32[]{:S(2)}) collective-permute-start(f32[3960,128]{1,0:T(8,128)} %get-tuple-element.21), channel_id=1, source_target_pairs={{0,16},{16,0},{32,48},{48,32},{64,80},{80,64},{96,112},{112,96},{1... | collective-permute-start | bytes 6082568 | tf_op jit(solution)/shard_map/ppermute | solution.py:457
  38.0 0.0 all-gather.3.cloned.1.call-update
  38.0 5.5 %all-to-all-done.arrived = f32[32,1,384]{2,1,0:T(1,128)S(1)} async-done(((f32[32,1,384]{2,1,0:T(1,128)}), f32[32,1,384]{2,1,0:T(1,128)S(1)}, u32[]{:S(2)}, u32[]{:S(2)}) %all-to-all-start) | async-done | bytes 49184 | tf_op jit(solution)/shard_map/all_to_all | solution.py:456
  43.6 0.7 copy-done.4
  44.3 0.4 shard_map.96.added_own
  44.7 0.2 collective-permute-done.across_hbm
  44.9 0.5 shard_map.97
  45.4 1.0 copy-done
  46.5 1.9 %shard_map.98 = (f32[5,24,128]{2,1,0:T(8,128)S(1)}, f32[5,24,128]{2,1,0:T(8,128)S(1)}, f32[8,128]{1,0:T(8,128)S(1)}, f32[2,64,128]{2,1,0:T(8,128)S(1)}) custom-call(f32[32,1,384]{2,1,0:T(1,128)S(1)} %all-to-all-done.arrived, f32[16,128]{1,0:T(8,128)S(1)} %get-tuple-element.19.added_before, f32[120,128]{1,0:T(8,128)S(1)} %get-tuple-element.20.beside_small, ...), custom_call_target="tpu_custom_call" | custom-call | flops 16777216 | bytes 6291456 | tf_op jit(solution)/shard_map/pallas_call | solution.py:469
  48.4 3.5 %collective-permute-start.2 = (f32[8,128]{1,0:T(8,128)S(1)}, f32[8,128]{1,0:T(8,128)S(1)}, u32[]{:S(2)}, u32[]{:S(2)}) collective-permute-start(f32[8,128]{1,0:T(8,128)S(1)} %get-tuple-element.27), channel_id=1, source_target_pairs={{0,496},{16,32},{32,16},{48,64},{64,48},{80,96},{96,80},{112,128},... | collective-permute-start | bytes 12296 | tf_op jit(solution)/shard_map/ppermute | solution.py:477
  51.9 0.8 shard_map.100.inside
  52.7 0.0 copy-start.2
  52.7 0.0 copy-start.3
  52.7 0.6 collective-permute-done.2.swapped
  53.3 1.4 %shard_map.101 = (f32[8,128]{1,0:T(8,128)}, f32[32,1,128]{2,1,0:T(1,128)}) custom-call(f32[5,24,128]{2,1,0:T(8,128)S(1)} %get-tuple-element.25.state, f32[5,24,128]{2,1,0:T(8,128)S(1)} %get-tuple-element.26.pats, f32[3,24,128]{2,1,0:T(8,128)S(1)} %shard_map.100.inside, f32[8,128]{1,0:T(8,128)S(1)} %collective-permute-done.2.swapped, ...), custom_call_target="tpu_custom_call" | custom-call | flops 8388608 | bytes 3145728 | tf_op jit(solution)/shard_map/pallas_call | solution.py:485
  54.8 12.7 %all-to-all-start.1 = ((f32[32,1,128]{2,1,0:T(1,128)}), f32[32,1,128]{2,1,0:T(1,128)S(1)}, u32[]{:S(2)}, u32[]{:S(2)}) async-start(f32[32,1,128]{2,1,0:T(1,128)} %get-tuple-element.28), calls=%async_computation.1 | async-start | bytes 32768 | tf_op jit(solution)/shard_map/all_to_all | solution.py:492
  67.4 25.6 %all-gather.3.cloned.1.call-done = f32[2048,128]{1,0:T(8,128)} async-done(((f32[128,128]{1,0:T(8,128)}), f32[2048,128]{1,0:T(8,128)}) %all-gather.3.cloned.1.call-update) | async-done | bytes 1048592 | tf_op jit(solution)/shard_map/all_gather | solution.py:459
  93.1 1.2 %copy-done.1 = f32[2048,128]{1,0:T(8,128)S(1)} copy-done((f32[2048,128]{1,0:T(8,128)S(1)}, f32[2048,128]{1,0:T(8,128)}, u32[]{:S(2)}) %copy-start.1) | copy-done | bytes 1048600
  94.3 1.1 %shard_map.99.base = f32[1024,128]{1,0:T(8,128)S(1)} custom-call(f32[1024,128]{1,0:T(8,128)S(1)} %bitcast.17, s32[1024,128]{1,0:T(8,128)S(1)} %bitcast.18, f32[2,64,128]{2,1,0:T(8,128)S(1)} %get-tuple-element.22.x_faces, f32[16,128,128]{2,1,0:T(8,128)S(1)} %bitcast.15), custom_call_target="tpu_custom_call" | custom-call | flops 4194304 | bytes 2097152 | tf_op jit(solution)/shard_map/pallas_call | solution.py:494
  95.5 3.2 %shard_map.102 = f32[1024,128]{1,0:T(8,128)} custom-call(f32[1024,128]{1,0:T(8,128)S(1)} %shard_map.99.base, s32[32,128]{1,0:T(8,128)S(1)} %bitcast.20, f32[32,128]{1,0:T(8,128)S(1)} %copy-done.7, f32[32,1,128]{2,1,0:T(1,128)S(1)} %all-to-all-done.1.returned), custom_call_target="tpu_custom_call" | custom-call | flops 2147483648 | bytes 1048576 | tf_op jit(solution)/shard_map/pallas_call | solution.py:501
  (13 shorter events, 0.0 us)
Async XLA Ops:
  14.3 29.3 %all-to-all-start = ((f32[32,1,384]{2,1,0:T(1,128)}), f32[32,1,384]{2,1,0:T(1,128)S(1)}, u32[]{:S(2)}, u32[]{:S(2)}) async-start(f32[32,1,384]{2,1,0:T(1,128)} %get-tuple-element.16), calls=%async_computation | async-start | bytes 98304 | tf_op jit(solution)/shard_map/all_to_all | solution.py:456
  31.0 62.0 %all-gather.3.cloned.1.call-start = ((), (), s32[]{:S(2)}) async-start(), calls=%async_computation.2 | async-start | bytes 1114112 | tf_op jit(solution)/shard_map/all_gather | solution.py:459
  31.1 13.9 %collective-permute-start = (f32[1400,128]{1,0:T(8,128)}, f32[1400,128]{1,0:T(8,128)S(1)}, u32[]{:S(2)}, u32[]{:S(2)}) collective-permute-start(f32[1400,128]{1,0:T(8,128)} %get-tuple-element.17), channel_id=1, source_target_pairs={{0,496},{16,32},{32,16},{48,64},{64,48},{80,96},{96,80},{112,128},... | collective-permute-start | bytes 2150408 | tf_op jit(solution)/shard_map/ppermute | solution.py:458
  34.6 10.8 %collective-permute-start.1 = (f32[3960,128]{1,0:T(8,128)}, f32[3960,128]{1,0:T(8,128)S(1)}, u32[]{:S(2)}, u32[]{:S(2)}) collective-permute-start(f32[3960,128]{1,0:T(8,128)} %get-tuple-element.21), channel_id=1, source_target_pairs={{0,16},{16,0},{32,48},{48,32},{64,80},{80,64},{96,112},{112,96},{1... | collective-permute-start | bytes 6082568 | tf_op jit(solution)/shard_map/ppermute | solution.py:457
  43.6 0.7 copy-start.4
  44.7 1.8 %copy-start = (f32[1,8,5,128,128]{4,3,2,1,0:T(8,128)S(1)}, f32[1,8,5,128,128]{4,3,2,1,0:T(8,128)}, u32[]{:S(2)}) copy-start(f32[1,8,5,128,128]{4,3,2,1,0:T(8,128)} %param.14) | copy-start | bytes 7864324
  44.7 1.8 %copy-start.5 = (f32[56,128]{1,0:T(8,128)S(1)}, f32[56,128]{1,0:T(8,128)}, u32[]{:S(2)}) copy-start(f32[56,128]{1,0:T(8,128)} %get-tuple-element.18.own) | copy-start | bytes 86020
  48.4 4.9 %collective-permute-start.2 = (f32[8,128]{1,0:T(8,128)S(1)}, f32[8,128]{1,0:T(8,128)S(1)}, u32[]{:S(2)}, u32[]{:S(2)}) collective-permute-start(f32[8,128]{1,0:T(8,128)S(1)} %get-tuple-element.27), channel_id=1, source_target_pairs={{0,496},{16,32},{32,16},{48,64},{64,48},{80,96},{96,80},{112,128},... | collective-permute-start | bytes 12296 | tf_op jit(solution)/shard_map/ppermute | solution.py:477
  52.7 40.4 %copy-start.2 = (f32[16,64,128]{2,1,0:T(8,128)S(1)}, f32[16,64,128]{2,1,0:T(8,128)}, u32[]{:S(2)}) copy-start(f32[16,64,128]{2,1,0:T(8,128)} %param.8) | copy-start | bytes 1572868
  52.7 40.4 %copy-start.3 = (s32[16,64,128]{2,1,0:T(8,128)S(1)}, s32[16,64,128]{2,1,0:T(8,128)}, u32[]{:S(2)}) copy-start(s32[16,64,128]{2,1,0:T(8,128)} %param.9) | copy-start | bytes 1572868
  54.7 40.7 %copy-start.6 = (s32[32,1,1,128]{3,2,1,0:T(1,128)S(1)}, s32[32,1,1,128]{3,2,1,0:T(1,128)}, u32[]{:S(2)}) copy-start(s32[32,1,1,128]{3,2,1,0:T(1,128)} %param.10) | copy-start | bytes 49156
  54.7 40.7 %copy-start.7 = (f32[32,128]{1,0:T(8,128)S(1)}, f32[32,128]{1,0:T(8,128)}, u32[]{:S(2)}) copy-start(f32[32,128]{1,0:T(8,128)} %get-tuple-element.24.outgoing) | copy-start | bytes 49156
  54.8 40.7 %all-to-all-start.1 = ((f32[32,1,128]{2,1,0:T(1,128)}), f32[32,1,128]{2,1,0:T(1,128)S(1)}, u32[]{:S(2)}, u32[]{:S(2)}) async-start(f32[32,1,128]{2,1,0:T(1,128)} %get-tuple-element.28), calls=%async_computation.1 | async-start | bytes 32768 | tf_op jit(solution)/shard_map/all_to_all | solution.py:492
  93.1 1.2 %copy-start.1 = (f32[2048,128]{1,0:T(8,128)S(1)}, f32[2048,128]{1,0:T(8,128)}, u32[]{:S(2)}) copy-start(f32[2048,128]{1,0:T(8,128)} %all-gather.3.cloned.1.call-done) | copy-start | bytes 3145732
Sparse Core Ops, SparseCore 0:
  38.1 54.8 all-gather.2

commit v5 on v3

--- a/solution.py
+++ b/solution.py
@@ -66,7 +66,7 @@
 
 def pick_kernel(
     fluid_hbm, src_hbm, dst_hbm, old_hbm, diag_hbm, pattern_hbm, blocks_hbm,
-    sent, outgoing, own, y_faces, z_faces, on_chip_hbm, across_hbm,
+    sent, outgoing, own, faces, on_chip_hbm, across_hbm,
     fluid, src, dst, pattern, table, packed, staged_in, staged_out, sems,
 ):
     me = lax.axis_index("gx")
@@ -87,14 +87,35 @@
     ]
     inside = copy(blocks_hbm.at[pl.ds((1 - parity) * 2 * TILE_ROWS, 6 * TILE_ROWS)], staged_in, 12)
     outside = copy(blocks_hbm.at[pl.ds(parity * 6 * TILE_ROWS, 2 * TILE_ROWS)], staged_out, 13)
+    before_z = lax.axis_index("gy") * 4 + lax.rem(lax.axis_index("gz") + 3, 4)
+    after_z = lax.axis_index("gy") * 4 + lax.rem(lax.axis_index("gz") + 1, 4)
     for block in range(8):
         loads[block].wait()
         turned = fluid[128 * block : 128 * block + 128, :].T
         high, low = two_parts(turned)
         table[0:128, 128 * block : 128 * block + 128] = high
         table[128:256, 128 * block : 128 * block + 128] = low
-        z_faces[0, block : block + 1, :] = turned[0:1, :]
-        z_faces[1, block : block + 1, :] = turned[127:128, :]
+        at = slice(128 * block, 128 * block + 128)
+        faces[before_z, :, at] = turned[0:1, :]
+        faces[after_z, :, at] = turned[127:128, :]
+    for each in small:
+        each.wait()
+    own[0:32, :] = dst[...].astype(F32)
+    own[48:56, :] = jnp.zeros((8, WIDTH), F32)
+    for offset in range(NB):
+        own[48 + offset : 49 + offset, 0:TILES] = pattern[offset].astype(F32)
+    first, last = fluid[0:64, :], fluid[960:1024, :]
+    for index, face in ((0, jnp.where(parity == 0, last, first)), (1, jnp.where(parity == 0, first, last))):
+        packed[index, 0:56, :] = own[...]
+        packed[index, 56:120, :] = face
+    tail_in = copy(packed.at[0], on_chip_hbm.at[6 * TILE_ROWS : 6 * TILE_ROWS + SMALL], 14)
+    tail_out = copy(packed.at[1], across_hbm.at[2 * TILE_ROWS : 2 * TILE_ROWS + SMALL], 15)
+    y, z = lax.axis_index("gy"), lax.axis_index("gz")
+    after_y, before_y = lax.rem(y + 1, 4) * 4 + z, lax.rem(y + 3, 4) * 4 + z
+    for slab in range(16):
+        at = slice(128 * slab, 128 * slab + 128)
+        faces[before_y, :, at] = fluid[64 * slab : 64 * slab + 1, :]
+        faces[after_y, :, at] = fluid[64 * slab + 63 : 64 * slab + 64, :]
     load_src.wait()
     group = 4
     for start in range(0, RUNS, group):
@@ -115,21 +136,6 @@
             sent[r ^ 1, :, 128:256] = mine
             beside = (r + 1) % RUNS if r % 2 else (r - 1) % RUNS
             sent[beside, :, 256:384] = mine
-    for slab in range(16):
-        y_faces[0, slab : slab + 1, :] = fluid[64 * slab : 64 * slab + 1, :]
-        y_faces[1, slab : slab + 1, :] = fluid[64 * slab + 63 : 64 * slab + 64, :]
-    for each in small:
-        each.wait()
-    own[0:32, :] = dst[...].astype(F32)
-    own[48:56, :] = jnp.zeros((8, WIDTH), F32)
-    for offset in range(NB):
-        own[48 + offset : 49 + offset, 0:TILES] = pattern[offset].astype(F32)
-    first, last = fluid[0:64, :], fluid[960:1024, :]
-    for index, face in ((0, jnp.where(parity == 0, last, first)), (1, jnp.where(parity == 0, first, last))):
-        packed[index, 0:56, :] = own[...]
-        packed[index, 56:120, :] = face
-    tail_in = copy(packed.at[0], on_chip_hbm.at[6 * TILE_ROWS : 6 * TILE_ROWS + SMALL], 14)
-    tail_out = copy(packed.at[1], across_hbm.at[2 * TILE_ROWS : 2 * TILE_ROWS + SMALL], 15)
     for each in (inside, outside, tail_in, tail_out):
         each.wait()
 
@@ -185,8 +191,8 @@
     return value + update, update
 
 
-def own_run_kernel(arrived, own, added):
-    added[...] = spread_run(lambda r: own[r : r + 1, :].astype(I32), lambda r: arrived[r, :, 0:128])
+def own_run_kernel(arrived, dst, added):
+    added[...] = spread_run(lambda r: dst[r : r + 1, :], lambda r: arrived[r, :, 0:128])
 
 
 def beside_run_kernel(arrived, across_hbm, added_own, added, small, sem):
@@ -200,8 +206,8 @@
 
 
 def wall_first_kernel(
-    arrived, added_before, beside_small, own, own_blocks, on_chip_hbm, across_hbm, y_before, y_after,
-    state, pats, swap, faces, y_faces,
+    arrived, added_before, beside_small, own, own_blocks, on_chip_hbm, across_hbm,
+    state, pats, swap, faces,
     inner, outer, iterate, shifted, coupled, sems,
 ):
     me = lax.axis_index("gx")
@@ -234,7 +240,6 @@
     right = window(parity, *rights)
     inverse = window(parity, *inverses)
     diagonal = window(parity, *diagonals)
-    y_faces[0], y_faces[1] = y_before[...], y_after[...]
     faces[0] = jnp.where(parity == 0, beside[56:120], partner[56:120])
     faces[1] = jnp.where(parity == 0, partner[56:120], beside[56:120])
     value = inverse * right
@@ -345,39 +350,7 @@
             returned[8 * block + r] = found[r : r + 1, :]
 
 
-def stencil_kernel(fluid_hbm, liquid_hbm, x_faces, y_faces, z_before, z_after, base, fluid, liquid, sems):
-    loads = [
-        pltpu.make_async_copy(fluid_hbm, fluid, sems.at[0]),
-        pltpu.make_async_copy(liquid_hbm, liquid, sems.at[1]),
-    ]
-    for each in loads:
-        each.start()
-    row = lax.broadcasted_iota(I32, (64, WIDTH), 0)
-    lane = lax.broadcasted_iota(I32, (64, WIDTH), 1)
-    for each in loads:
-        each.wait()
-    for slab in range(16):
-        start = 64 * slab
-        block = slab // 2
-        here = fluid[start : start + 64, :]
-        total = (fluid[start - 64 : start, :] if slab else x_faces[0]) + (
-            fluid[start + 64 : start + 128, :] if slab < 15 else x_faces[1]
-        )
-        total = total + jnp.where(row == 0, y_faces[0, slab : slab + 1, :], pltpu.roll(here, 1, 0))
-        total = total + jnp.where(row == 63, y_faces[1, slab : slab + 1, :], pltpu.roll(here, 63, 0))
-        half = 64 * (slab % 2)
-        left = jnp.broadcast_to(z_before[block : block + 1, :], (WIDTH, WIDTH)).T[half : half + 64, :]
-        right = jnp.broadcast_to(z_after[block : block + 1, :], (WIDTH, WIDTH)).T[half : half + 64, :]
-        total = total + jnp.where(lane == 0, left, pltpu.roll(here, 1, 1))
-        total = total + jnp.where(lane == 127, right, pltpu.roll(here, 127, 1))
-        total = total - 6.0 * here
-        share = liquid[start : start + 64, :].astype(F32)
-        base[start : start + 64, :] = (
-            here + DIFFUSION * total - EVAPORATION * share * jnp.maximum(here - SATURATION, 0.0)
-        )
-
-
-def final_kernel(base, src, outgoing, returned, fluid_new):
+def final_kernel(fluid, liquid, x_faces, faces, src, outgoing, returned, fluid_new):
     group = 4
     total = None
     for start in range(0, RUNS, group):
@@ -387,7 +360,34 @@
         placed = placed_parts(ids & 127, WIDTH, value)
         added = lax.dot_general(row_hots(ids >> 7, ROWS), placed, CONTRACT_LAST, preferred_element_type=F32)
         total = added if total is None else total + added
-    fluid_new[...] = base[...] + WALL_COUPLING * (total[:, 0:128] + total[:, 128:256])
+    wall = total[:, 0:128] + total[:, 128:256]
+    y, z = lax.axis_index("gy"), lax.axis_index("gz")
+    after_y, before_y = lax.rem(y + 1, 4) * 4 + z, lax.rem(y + 3, 4) * 4 + z
+    after_z, before_z = y * 4 + lax.rem(z + 1, 4), y * 4 + lax.rem(z + 3, 4)
+    row = lax.broadcasted_iota(I32, (64, WIDTH), 0)
+    lane = lax.broadcasted_iota(I32, (64, WIDTH), 1)
+    for slab in range(16):
+        start = 64 * slab
+        at, at_z = slice(128 * slab, 128 * slab + 128), slice(128 * (slab // 2), 128 * (slab // 2) + 128)
+        here = fluid[start : start + 64, :]
+        total = (fluid[start - 64 : start, :] if slab else x_faces[0]) + (
+            fluid[start + 64 : start + 128, :] if slab < 15 else x_faces[1]
+        )
+        total = total + jnp.where(row == 0, faces[before_y, :, at], pltpu.roll(here, 1, 0))
+        total = total + jnp.where(row == 63, faces[after_y, :, at], pltpu.roll(here, 63, 0))
+        half = 64 * (slab % 2)
+        left = jnp.broadcast_to(faces[before_z, :, at_z], (WIDTH, WIDTH)).T[half : half + 64, :]
+        right = jnp.broadcast_to(faces[after_z, :, at_z], (WIDTH, WIDTH)).T[half : half + 64, :]
+        total = total + jnp.where(lane == 0, left, pltpu.roll(here, 1, 1))
+        total = total + jnp.where(lane == 127, right, pltpu.roll(here, 127, 1))
+        total = total - 6.0 * here
+        share = liquid[start : start + 64, :].astype(F32)
+        fluid_new[start : start + 64, :] = (
+            here
+            + DIFFUSION * total
+            - EVAPORATION * share * jnp.maximum(here - SATURATION, 0.0)
+            + WALL_COUPLING * wall[start : start + 64, :]
+        )
 
 
 def shape(*dims):
@@ -423,14 +423,14 @@
     own_blocks = blocks.reshape(TILES * TILE_ROWS, WIDTH)
     in_rows, out_rows = 6 * TILE_ROWS + SMALL, 2 * TILE_ROWS + SMALL
 
-    sent, outgoing, own, y_faces, z_faces, on_chip, across = call(
+    sent, outgoing, own, faces, on_chip, across = call(
         pick_kernel, 60,
         [HBM] * 7,
         (
-            shape(RUNS, 1, 384), shape(RUNS, WIDTH), shape(56, WIDTH), shape(2, 16, WIDTH), shape(2, 8, WIDTH),
+            shape(RUNS, 1, 384), shape(RUNS, WIDTH), shape(56, WIDTH), shape(16, 1, 2048),
             shape(in_rows, WIDTH), shape(out_rows, WIDTH),
         ),
-        (VMEM, VMEM, VMEM, VMEM, VMEM, HBM, HBM),
+        (VMEM, VMEM, VMEM, VMEM, HBM, HBM),
         [
             vmem(ROWS, WIDTH), vmem(RUNS, WIDTH, kind=I32), vmem(RUNS, WIDTH, kind=I32), vmem(NB, 1, TILES, kind=I32),
             vmem(256, ROWS, kind=BF16), vmem(2, SMALL, WIDTH), vmem(6 * TILE_ROWS, WIDTH), vmem(2 * TILE_ROWS, WIDTH), dma(19),
@@ -441,27 +441,24 @@
     arrived = lax.all_to_all(sent, "gx", split_axis=0, concat_axis=0, tiled=True)
     on_chip = lax.ppermute(on_chip, "gx", inside_pairs)
     across = lax.ppermute(across, "gx", outside_pairs)
-    up = [(i, (i + 1) % 4) for i in range(4)]
-    down = [(i, (i - 1) % 4) for i in range(4)]
-    y_before = lax.ppermute(y_faces[1], "gy", up)
-    y_after = lax.ppermute(y_faces[0], "gy", down)
+    faces = lax.all_to_all(faces, ("gy", "gz"), split_axis=0, concat_axis=0, tiled=True)
 
     work = [vmem(WIN, WIDTH), vmem(NB, WIN, WIDTH), vmem(WIN, WIDTH)]
     added_own = call(
         own_run_kernel, 12, [VMEM, VMEM], shape(TILES, WIDTH), VMEM, [], 65 * 10**8, 1 << 16
-    )(arrived, own)
+    )(arrived, dst)
     added_before, beside_small = call(
         beside_run_kernel, 12, [VMEM, ANY, VMEM], (shape(2 * TILES, WIDTH), shape(SMALL, WIDTH)), (VMEM, VMEM), [dma()],
         14 * 10**9, 1 << 16,
     )(arrived, across, added_own)
-    state, pats, swap, x_faces, y_faces = call(
+    state, pats, swap, x_faces = call(
         wall_first_kernel, 16,
-        [VMEM, VMEM, VMEM, VMEM, VMEM, ANY, ANY, VMEM, VMEM],
-        (shape(5, WIN, WIDTH), shape(NB, WIN, WIDTH), shape(8, WIDTH), shape(2, 64, WIDTH), shape(2, 16, WIDTH)),
-        (VMEM,) * 5,
+        [VMEM, VMEM, VMEM, VMEM, VMEM, ANY, ANY],
+        (shape(5, WIN, WIDTH), shape(NB, WIN, WIDTH), shape(8, WIDTH), shape(2, 64, WIDTH)),
+        (VMEM,) * 4,
         [vmem(in_rows, WIDTH), vmem(2 * TILE_ROWS, WIDTH)] + work + [dma(3)],
         1 << 24, 6 << 20,
-    )(arrived, added_before, beside_small, own, own_blocks, on_chip, across, y_before, y_after)
+    )(arrived, added_before, beside_small, own, own_blocks, on_chip, across)
     swapped = lax.ppermute(swap, "gx", outside_pairs)
     inside = call(
         wall_inner_kernel, 12,
@@ -477,21 +474,11 @@
         [vmem(2 * TILE_ROWS, WIDTH)] + work + [dma()],
         1 << 23, 3 << 20,
     )(state, pats, inside, swapped, own, own_blocks, across)
-    sent_back, z_faces = lax.optimization_barrier((sent_back, z_faces))
-    z_before = lax.ppermute(z_faces[1], "gz", up)
-    z_after = lax.ppermute(z_faces[0], "gz", down)
     returned = lax.all_to_all(sent_back, "gx", split_axis=0, concat_axis=0, tiled=True)
 
-    base = call(
-        stencil_kernel, 12,
-        [HBM, HBM, VMEM, VMEM, VMEM, VMEM],
-        shape(ROWS, WIDTH), VMEM,
-        [vmem(ROWS, WIDTH), vmem(ROWS, WIDTH, kind=I32), dma(2)],
-        1 << 22, 1 << 21,
-    )(fluid, liquid.reshape(ROWS, WIDTH), x_faces, y_faces, z_before, z_after)
     fluid_new = call(
-        final_kernel, 16, [VMEM] * 4, shape(ROWS, WIDTH), VMEM, [], 2 * 256 * 1024 * 4096, 1 << 20
-    )(base, src, outgoing, returned)
+        final_kernel, 16, [VMEM] * 7, shape(ROWS, WIDTH), VMEM, [], 2 * 256 * 1024 * 4096, 1 << 20
+    )(fluid, liquid.reshape(ROWS, WIDTH), x_faces, faces, src, outgoing, returned)
     return fluid_new.reshape(fluid_temp.shape), solid[None]
 
 

time: 77 us -> 74.1 us (0.962)
  starting transfers between devices: 52.4 us -> 34.2 us
  blocking collectives: 0 us -> 17.8 us
  Pallas kernels: 15.1 us -> 13.5 us
    all_to_all x0 -> x1, blocking collectives: none -> 17.8 us  [per_device(): lax.all_to_all(sent_back, 'gx', split_axis=0, concat_axis=0, tiled=True)]
    ppermute x4 -> x0, starting transfers between devices: 12.8 us -> none  [the longest x1 4.63 us: per_device(): z_after = lax.ppermute(z_faces[0], 'gz', down)]
    ppermute x4 -> x0, waiting for transfers between devices: 5.88 us -> none  [the longest x1 3.92 us: per_device(): z_before = lax.ppermute(z_faces[1], 'gz', up)]
    all_to_all x1, starting transfers between devices: 12.4 us -> 6.76 us  [per_device(): lax.all_to_all(faces, ('gy', 'gz'), split_axis=0, concat_axis=0, tiled=True)]
    all_to_all x1, waiting for transfers between devices: 0.01 us -> 5.62 us  [per_device(): lax.all_to_all(sent, 'gx', split_axis=0, concat_axis=0, tiled=True)]
    pallas_call x3 -> x2, Pallas kernels: 6.19 us -> 5.18 us  [the longest x1 3.26 us: per_device(): call(final_kernel, 16, [VMEM] * 7, shape(ROWS, WIDTH), VMEM, [], 2 * 256...]
  transfers between devices with their start and end apart: 9 -> 5, of which waited for: 4 -> 2; matrix products, arithmetic and copies ran while one was open for 1% -> 0% of each run, Pallas kernels for 4% -> 7%
where the time goes in v5:
time: 74.1 us; the launch traced here: 73.8 us
  starting transfers between devices  34.2 us (46%)
  blocking collectives  17.8 us (24%)
  Pallas kernels  13.5 us (18%)
  waiting for transfers between devices  6.21 us (8%)
  local copies, waits for them, and re-layouts  1.23 us (2%)
  between operations  0.8 us (1%)
    all_to_all x1, blocking collectives, per_device(): lax.all_to_all(sent_back, 'gx', split_axis=0, concat_axis=0, tiled=True)  17.8 us
    all_to_all x1, starting transfers between devices, per_device(): lax.all_to_all(sent, 'gx', split_axis=0, concat_axis=0, tiled=True)  16.8 us
    all_to_all x1, starting transfers between devices, per_device(): lax.all_to_all(faces, ('gy', 'gz'), split_axis=0, concat_axis=0, tiled=True)  6.76 us
    all_to_all x1, waiting for transfers between devices, per_device(): lax.all_to_all(sent, 'gx', split_axis=0, concat_axis=0, tiled=True)  5.62 us
    pallas_call x1, Pallas kernels, per_device(): call(pick_kernel, 60, [HBM] * 7, (shape(RUNS, 1, 384), shape(RUNS, WIDTH)...  5.4 us
    ppermute x1, starting transfers between devices, per_device(): swapped = lax.ppermute(swap, 'gx', outside_pairs)  3.8 us
    ppermute x1, starting transfers between devices, per_device(): across = lax.ppermute(across, 'gx', outside_pairs)  3.54 us
    ppermute x1, starting transfers between devices, per_device(): on_chip = lax.ppermute(on_chip, 'gx', inside_pairs)  3.35 us
  transfers between devices with their start and end apart: 5, of which 2 were waited for; matrix products, arithmetic and copies ran while one was open for 0% of the time, Pallas kernels for 7%

profile of v5, /device:TPU:1, one launch (start us, length us, event | category | flops | bytes accessed | tf_op | source)
XLA Modules:
  0.0 73.8 jit_solution(9088987953997404421)
XLA Ops:
  0.6 0.0 copy-start.4
  0.6 5.4 %shard_map.95 = (f32[32,1,384]{2,1,0:T(1,128)}, f32[32,128]{1,0:T(8,128)}, f32[56,128]{1,0:T(8,128)}, f32[16,1,2048]{2,1,0:T(1,128)}, f32[3960,128]{1,0:T(8,128)}, /*index=5*/f32[1400,128]{1,0:T(8,128)}) custom-call(f32[1024,128]{1,0:T(8,128)} %bitcast.14, s32[32,128]{1,0:T(8,128)} %bitcast.19, s32[32,128]{1,0:T(8,128)} %bitcast.17, f32[8,128]{1,0:T(8,128)} %bitcast.21, ...), custom_call_target="tpu_custom_call" | custom-call | flops 2147483648 | bytes 4194304 | tf_op jit(solution)/shard_map/pallas_call | solution.py:426
  6.0 16.8 %all-to-all-start = ((f32[32,1,384]{2,1,0:T(1,128)}), f32[32,1,384]{2,1,0:T(1,128)S(1)}, u32[]{:S(2)}, u32[]{:S(2)}) async-start(f32[32,1,384]{2,1,0:T(1,128)} %get-tuple-element.16), calls=%async_computation | async-start | bytes 98304 | tf_op jit(solution)/shard_map/all_to_all | solution.py:441
  22.8 3.5 %collective-permute-start = (f32[1400,128]{1,0:T(8,128)}, f32[1400,128]{1,0:T(8,128)S(1)}, u32[]{:S(2)}, u32[]{:S(2)}) collective-permute-start(f32[1400,128]{1,0:T(8,128)} %get-tuple-element.17), channel_id=1, source_target_pairs={{0,496},{16,32},{32,16},{48,64},{64,48},{80,96},{96,80},{112,128},... | collective-permute-start | bytes 2150408 | tf_op jit(solution)/shard_map/ppermute | solution.py:443
  26.4 3.4 %collective-permute-start.1 = (f32[3960,128]{1,0:T(8,128)}, f32[3960,128]{1,0:T(8,128)S(1)}, u32[]{:S(2)}, u32[]{:S(2)}) collective-permute-start(f32[3960,128]{1,0:T(8,128)} %get-tuple-element.21), channel_id=1, source_target_pairs={{0,16},{16,0},{32,48},{48,32},{64,80},{80,64},{96,112},{112,96},{1... | collective-permute-start | bytes 6082568 | tf_op jit(solution)/shard_map/ppermute | solution.py:442
  29.7 5.6 %all-to-all-done.arrived = f32[32,1,384]{2,1,0:T(1,128)S(1)} async-done(((f32[32,1,384]{2,1,0:T(1,128)}), f32[32,1,384]{2,1,0:T(1,128)S(1)}, u32[]{:S(2)}, u32[]{:S(2)}) %all-to-all-start) | async-done | bytes 49184 | tf_op jit(solution)/shard_map/all_to_all | solution.py:441
  35.3 6.8 %all-to-all-start.1 = ((f32[16,1,2048]{2,1,0:T(1,128)}), f32[16,1,2048]{2,1,0:T(1,128)S(1)}, u32[]{:S(2)}, u32[]{:S(2)}) async-start(f32[16,1,2048]{2,1,0:T(1,128)} %get-tuple-element.23), calls=%async_computation.1 | async-start | bytes 262144 | tf_op jit(solution)/shard_map/all_to_all | solution.py:444
  42.1 0.4 shard_map.96.added_own
  42.5 0.0 collective-permute-done.across_hbm
  42.5 0.5 shard_map.97
  43.1 0.0 collective-permute-done.1.on_chip_hbm
  43.1 1.2 %copy-done = f32[1,8,5,128,128]{4,3,2,1,0:T(8,128)S(1)} copy-done((f32[1,8,5,128,128]{4,3,2,1,0:T(8,128)S(1)}, f32[1,8,5,128,128]{4,3,2,1,0:T(8,128)}, u32[]{:S(2)}) %copy-start) | copy-done | bytes 2621464
  44.3 1.9 %shard_map.98 = (f32[5,24,128]{2,1,0:T(8,128)S(1)}, f32[5,24,128]{2,1,0:T(8,128)S(1)}, f32[8,128]{1,0:T(8,128)S(1)}, f32[2,64,128]{2,1,0:T(8,128)S(1)}) custom-call(f32[32,1,384]{2,1,0:T(1,128)S(1)} %all-to-all-done.arrived, f32[16,128]{1,0:T(8,128)S(1)} %get-tuple-element.18.added_before, f32[120,128]{1,0:T(8,128)S(1)} %get-tuple-element.19.beside_small, ...), custom_call_target="tpu_custom_call" | custom-call | flops 16777216 | bytes 6291456 | tf_op jit(solution)/shard_map/pallas_call | solution.py:454
  46.2 3.8 %collective-permute-start.2 = (f32[8,128]{1,0:T(8,128)S(1)}, f32[8,128]{1,0:T(8,128)S(1)}, u32[]{:S(2)}, u32[]{:S(2)}) collective-permute-start(f32[8,128]{1,0:T(8,128)S(1)} %get-tuple-element.27), channel_id=1, source_target_pairs={{0,496},{16,32},{32,16},{48,64},{64,48},{80,96},{96,80},{112,128},... | collective-permute-start | bytes 12296 | tf_op jit(solution)/shard_map/ppermute | solution.py:462
  50.0 0.8 %shard_map.99.inside = f32[3,24,128]{2,1,0:T(8,128)S(1)} custom-call(f32[5,24,128]{2,1,0:T(8,128)S(1)} %get-tuple-element.25.state, f32[5,24,128]{2,1,0:T(8,128)S(1)} %get-tuple-element.26.pats, f32[5120,128]{1,0:T(8,128)S(1)} %bitcast.12, f32[3960,128]{1,0:T(8,128)S(1)} %collective-permute-done.1.on_chip_hbm), custom_call_target="tpu_custom_call" | custom-call | flops 4194304 | bytes 3145728 | tf_op jit(solution)/shard_map/pallas_call | solution.py:463
  50.8 0.0 copy-start.2
  50.8 0.0 copy-start.3
  50.8 0.0 copy-start.5
  50.8 0.6 collective-permute-done.2.swapped
  51.4 1.3 %shard_map.100 = (f32[8,128]{1,0:T(8,128)}, f32[32,1,128]{2,1,0:T(1,128)S(1)}) custom-call(f32[5,24,128]{2,1,0:T(8,128)S(1)} %get-tuple-element.25.state, f32[5,24,128]{2,1,0:T(8,128)S(1)} %get-tuple-element.26.pats, f32[3,24,128]{2,1,0:T(8,128)S(1)} %shard_map.99.inside, f32[8,128]{1,0:T(8,128)S(1)} %collective-permute-done.2.swapped, ...), custom_call_target="tpu_custom_call" | custom-call | flops 8388608 | bytes 3145728 | tf_op jit(solution)/shard_map/pallas_call | solution.py:470
  52.7 0.0 all-to-all-done.1.faces
  52.7 17.8 %all_to_all.15.returned = f32[32,1,128]{2,1,0:T(1,128)S(1)} all-to-all(f32[32,1,128]{2,1,0:T(1,128)S(1)} %get-tuple-element.28), channel_id=1, replica_groups=mesh['gx'=32,'gy'=4,'gz'=4] {'gx'}, dimensions={0} | all-to-all | bytes 32768 | tf_op jit(solution)/shard_map/all_to_all | solution.py:477
  70.5 0.0 copy-done.3
  70.5 3.3 %shard_map.101 = f32[1024,128]{1,0:T(8,128)} custom-call(f32[1024,128]{1,0:T(8,128)S(1)} %bitcast.15, s32[1024,128]{1,0:T(8,128)S(1)} %bitcast.16, f32[2,64,128]{2,1,0:T(8,128)S(1)} %get-tuple-element.22.x_faces, f32[16,1,2048]{2,1,0:T(1,128)S(1)} %all-to-all-done.1.faces, s32[32,128]{1,0:T(8,128)S(1)} %bitcast.20, f32[32,128]{1,0:T(8,128)S(1)} %copy-done.6, ...), custom_call_target="tpu_custom_call" | custom-call | flops 2147483648 | bytes 1048576 | tf_op jit(solution)/shard_map/pallas_call | solution.py:479
  (8 shorter events, 0.0 us)
Async XLA Ops:
  0.6 41.5 %copy-start.4 = (s32[32,1,1,128]{3,2,1,0:T(1,128)S(1)}, s32[32,1,1,128]{3,2,1,0:T(1,128)}, u32[]{:S(2)}) copy-start(s32[32,1,1,128]{3,2,1,0:T(1,128)} %param.11) | copy-start | bytes 49156
  6.0 29.3 %all-to-all-start = ((f32[32,1,384]{2,1,0:T(1,128)}), f32[32,1,384]{2,1,0:T(1,128)S(1)}, u32[]{:S(2)}, u32[]{:S(2)}) async-start(f32[32,1,384]{2,1,0:T(1,128)} %get-tuple-element.16), calls=%async_computation | async-start | bytes 98304 | tf_op jit(solution)/shard_map/all_to_all | solution.py:441
  22.8 19.7 %collective-permute-start = (f32[1400,128]{1,0:T(8,128)}, f32[1400,128]{1,0:T(8,128)S(1)}, u32[]{:S(2)}, u32[]{:S(2)}) collective-permute-start(f32[1400,128]{1,0:T(8,128)} %get-tuple-element.17), channel_id=1, source_target_pairs={{0,496},{16,32},{32,16},{48,64},{64,48},{80,96},{96,80},{112,128},... | collective-permute-start | bytes 2150408 | tf_op jit(solution)/shard_map/ppermute | solution.py:443
  26.4 16.7 %collective-permute-start.1 = (f32[3960,128]{1,0:T(8,128)}, f32[3960,128]{1,0:T(8,128)S(1)}, u32[]{:S(2)}, u32[]{:S(2)}) collective-permute-start(f32[3960,128]{1,0:T(8,128)} %get-tuple-element.21), channel_id=1, source_target_pairs={{0,16},{16,0},{32,48},{48,32},{64,80},{80,64},{96,112},{112,96},{1... | collective-permute-start | bytes 6082568 | tf_op jit(solution)/shard_map/ppermute | solution.py:442
  35.3 17.3 %all-to-all-start.1 = ((f32[16,1,2048]{2,1,0:T(1,128)}), f32[16,1,2048]{2,1,0:T(1,128)S(1)}, u32[]{:S(2)}, u32[]{:S(2)}) async-start(f32[16,1,2048]{2,1,0:T(1,128)} %get-tuple-element.23), calls=%async_computation.1 | async-start | bytes 262144 | tf_op jit(solution)/shard_map/all_to_all | solution.py:444
  42.5 1.8 %copy-start = (f32[1,8,5,128,128]{4,3,2,1,0:T(8,128)S(1)}, f32[1,8,5,128,128]{4,3,2,1,0:T(8,128)}, u32[]{:S(2)}) copy-start(f32[1,8,5,128,128]{4,3,2,1,0:T(8,128)} %param.14) | copy-start | bytes 7864324
  42.5 1.8 %copy-start.1 = (f32[56,128]{1,0:T(8,128)S(1)}, f32[56,128]{1,0:T(8,128)}, u32[]{:S(2)}) copy-start(f32[56,128]{1,0:T(8,128)} %get-tuple-element.20.own) | copy-start | bytes 86020
  46.2 5.2 %collective-permute-start.2 = (f32[8,128]{1,0:T(8,128)S(1)}, f32[8,128]{1,0:T(8,128)S(1)}, u32[]{:S(2)}, u32[]{:S(2)}) collective-permute-start(f32[8,128]{1,0:T(8,128)S(1)} %get-tuple-element.27), channel_id=1, source_target_pairs={{0,496},{16,32},{32,16},{48,64},{64,48},{80,96},{96,80},{112,128},... | collective-permute-start | bytes 12296 | tf_op jit(solution)/shard_map/ppermute | solution.py:462
  50.8 19.7 %copy-start.2 = (f32[16,64,128]{2,1,0:T(8,128)S(1)}, f32[16,64,128]{2,1,0:T(8,128)}, u32[]{:S(2)}) copy-start(f32[16,64,128]{2,1,0:T(8,128)} %param.8) | copy-start | bytes 1572868
  50.8 19.7 %copy-start.3 = (s32[16,64,128]{2,1,0:T(8,128)S(1)}, s32[16,64,128]{2,1,0:T(8,128)}, u32[]{:S(2)}) copy-start(s32[16,64,128]{2,1,0:T(8,128)} %param.9) | copy-start | bytes 1572868
  50.8 19.7 %copy-start.5 = (s32[32,1,1,128]{3,2,1,0:T(1,128)S(1)}, s32[32,1,1,128]{3,2,1,0:T(1,128)}, u32[]{:S(2)}) copy-start(s32[32,1,1,128]{3,2,1,0:T(1,128)} %param.10) | copy-start | bytes 49156
  50.8 19.7 %copy-start.6 = (f32[32,128]{1,0:T(8,128)S(1)}, f32[32,128]{1,0:T(8,128)}, u32[]{:S(2)}) copy-start(f32[32,128]{1,0:T(8,128)} %get-tuple-element.24.outgoing) | copy-start | bytes 49156

commit v6 on v5

--- a/solution.py
+++ b/solution.py
@@ -205,23 +205,71 @@
     )
 
 
-def wall_first_kernel(
-    arrived, added_before, beside_small, own, own_blocks, on_chip_hbm, across_hbm,
-    state, pats, swap, faces,
-    inner, outer, iterate, shifted, coupled, sems,
+def windows(parity, keep, own, partner, beside, added):
+    holders = [own, partner, beside]
+    diagonals = [each[40:48] for each in holders]
+    rights = [d * each[32:40] + a for d, each, a in zip(diagonals, holders, added)]
+    inverses = [1.0 / d for d in diagonals]
+    rights[2], inverses[2] = rights[2] * keep, inverses[2] * keep
+    present = window(parity, *[each[48:56].T[0:TILES] for each in holders])
+    return window(parity, *rights), window(parity, *inverses), window(parity, *diagonals), present
+
+
+def wall_edge_kernel(
+    added_before, beside_small, own, own_blocks, across_hbm,
+    products, swap,
+    outer, pats, iterate, shifted, coupled, sem,
 ):
+    load = pltpu.make_async_copy(across_hbm.at[0 : 2 * TILE_ROWS], outer, sem)
+    load.start()
     me = lax.axis_index("gx")
     parity = lax.rem(me, 2)
     keep = jnp.where((me == 0) | (me == RUNS - 1), 0.0, 1.0)
-    loads = []
+    mine = own[...]
+    added = [added_before[0:TILES, :], jnp.zeros((TILES, WIDTH), F32), added_before[TILES : 2 * TILES, :]]
+    right, inverse, diagonal, present = windows(parity, keep, mine, mine, beside_small[...], added)
+    for offset in range(NB):
+        pats[offset] = jnp.broadcast_to(present[:, offset : offset + 1], (WIN, WIDTH))
+    value = inverse * right
+    iterate[...] = value
+    shifted[...] = jnp.zeros((NB, WIN, WIDTH), F32)
+    coupled[...] = jnp.zeros((WIN, WIDTH), F32)
+    own_at = 4 + 4 * parity
+    neighbours(iterate, pats, 2, 16, shifted)
+    for index in range(6):
+        tile = index + 2 * parity
+        apply_tile(own_blocks, tile, shifted, own_at + tile, coupled)
+    load.wait()
+    for index in range(2):
+        apply_tile(outer, index, shifted, 2 + 14 * parity + index, coupled)
+    products[0] = coupled[...]
+    value, update = stepped(0, value, None, right, inverse, diagonal, coupled[...])
+    iterate[...] = value
+    neighbours(iterate, pats, 4, 12, shifted)
+    for index in range(4):
+        tile = index + 4 * parity
+        apply_tile(own_blocks, tile, shifted, own_at + tile, coupled)
+    products[1] = coupled[...]
+    value, update = stepped(1, value, update, right, inverse, diagonal, coupled[...])
+    swap[0:4, :] = jnp.where(parity == 0, value[4:8], value[12:16])
+    swap[4:8, :] = jnp.where(parity == 0, update[4:8], update[12:16])
+
+
+def wall_inner_kernel(
+    arrived, added_before, beside_small, own, products, own_blocks, on_chip_hbm,
+    state, pats, inside, faces,
+    inner, iterate, shifted, coupled, sems,
+):
     at_in = 6 * TILE_ROWS
-    for index, (source, target, low, high) in enumerate((
-        (on_chip_hbm, inner, at_in, at_in + SMALL),
-        (on_chip_hbm, inner, 0, at_in),
-        (across_hbm, outer, 0, 2 * TILE_ROWS),
-    )):
-        loads.append(pltpu.make_async_copy(source.at[low:high], target.at[low:high], sems.at[index]))
-        loads[-1].start()
+    loads = [
+        pltpu.make_async_copy(on_chip_hbm.at[low:high], inner.at[low:high], sems.at[index])
+        for index, (low, high) in enumerate(((at_in, at_in + SMALL), (0, at_in)))
+    ]
+    for each in loads:
+        each.start()
+    me = lax.axis_index("gx")
+    parity = lax.rem(me, 2)
+    keep = jnp.where((me == 0) | (me == RUNS - 1), 0.0, 1.0)
     loads[0].wait()
     partner, beside = inner[at_in : at_in + SMALL, :], beside_small[...]
     added = [
@@ -229,19 +277,12 @@
         spread_run(lambda r: inner[at_in + r : at_in + r + 1, :].astype(I32), lambda r: arrived[r, :, 128:256]),
         added_before[TILES : 2 * TILES, :],
     ]
-    holders = [own[...], partner, beside]
-    diagonals = [each[40:48] for each in holders]
-    rights = [d * each[32:40] + a for d, each, a in zip(diagonals, holders, added)]
-    inverses = [1.0 / d for d in diagonals]
-    rights[2], inverses[2] = rights[2] * keep, inverses[2] * keep
-    present = window(parity, *[each[48:56].T[0:TILES] for each in holders])
+    right, inverse, diagonal, present = windows(parity, keep, own[...], partner, beside, added)
     for offset in range(NB):
         pats[offset] = jnp.broadcast_to(present[:, offset : offset + 1], (WIN, WIDTH))
-    right = window(parity, *rights)
-    inverse = window(parity, *inverses)
-    diagonal = window(parity, *diagonals)
     faces[0] = jnp.where(parity == 0, beside[56:120], partner[56:120])
     faces[1] = jnp.where(parity == 0, partner[56:120], beside[56:120])
+    place = lax.broadcasted_iota(I32, (WIN, WIDTH), 0)
     value = inverse * right
     iterate[...] = value
     shifted[...] = jnp.zeros((NB, WIN, WIDTH), F32)
@@ -249,44 +290,35 @@
     own_at = 4 + 4 * parity
 
     neighbours(iterate, pats, 2, 16, shifted)
-    for tile in range(TILES):
+    for index in range(2):
+        tile = index + 6 - 6 * parity
         apply_tile(own_blocks, tile, shifted, own_at + tile, coupled)
     loads[1].wait()
-    loads[2].wait()
-    for tile in range(6):
-        apply_tile(inner, tile, shifted, 12 - 10 * parity + tile, coupled)
-    for tile in range(2):
-        apply_tile(outer, tile, shifted, 2 + 14 * parity + tile, coupled)
-    value, update = stepped(0, value, None, right, inverse, diagonal, coupled[...])
+    for index in range(6):
+        apply_tile(inner, index, shifted, 12 - 10 * parity + index, coupled)
+    low = 2 + 8 * parity
+    product = jnp.where((place >= low) & (place < low + 8), products[0], coupled[...])
+    value, update = stepped(0, value, None, right, inverse, diagonal, product)
     iterate[...] = value
 
     neighbours(iterate, pats, 4, 12, shifted)
-    for tile in range(TILES):
-        apply_tile(own_blocks, tile, shifted, own_at + tile, coupled)
-    for tile in range(4):
-        apply_tile(inner, tile + 2 * parity, shifted, 12 - 8 * parity + tile, coupled)
-    value, update = stepped(1, value, update, right, inverse, diagonal, coupled[...])
+    for index in range(4):
+        tile = index + 4 - 4 * parity
+        apply_tile(own_blocks, tile, shifted, own_at + tile, coupled)
+    for index in range(4):
+        apply_tile(inner, index + 2 * parity, shifted, 12 - 8 * parity + index, coupled)
+    low = 4 + 8 * parity
+    product = jnp.where((place >= low) & (place < low + 4), products[1], coupled[...])
+    value, update = stepped(1, value, update, right, inverse, diagonal, product)
     state[0], state[1], state[2], state[3], state[4] = value, update, right, inverse, diagonal
-    swap[0:4, :] = jnp.where(parity == 0, value[4:8], value[12:16])
-    swap[4:8, :] = jnp.where(parity == 0, update[4:8], update[12:16])
-
-
-def wall_inner_kernel(state, pats, own_blocks, on_chip_hbm, inside, inner, iterate, shifted, coupled, sem):
-    parity = lax.rem(lax.axis_index("gx"), 2)
-    load = pltpu.make_async_copy(on_chip_hbm.at[pl.ds(parity * 4 * TILE_ROWS, 2 * TILE_ROWS)], inner, sem)
-    load.start()
-    value, update, right, inverse, diagonal = (state[i] for i in range(5))
-    iterate[...] = value
-    shifted[...] = jnp.zeros((NB, WIN, WIDTH), F32)
-    coupled[...] = jnp.zeros((WIN, WIDTH), F32)
-    own_at = 4 + 4 * parity
+    iterate[...] = value
+
     neighbours(iterate, pats, 6, 8, shifted)
     for index in range(6):
         tile = index + 2 - 2 * parity
         apply_tile(own_blocks, tile, shifted, own_at + tile, coupled)
-    load.wait()
     for index in range(2):
-        apply_tile(inner, index, shifted, 12 - 6 * parity + index, coupled)
+        apply_tile(inner, index + 4 * parity, shifted, 12 - 6 * parity + index, coupled)
     value, update = stepped(2, value, update, right, inverse, diagonal, coupled[...])
     inside[0], inside[1] = value, update
     iterate[...] = value
@@ -451,22 +483,21 @@
         beside_run_kernel, 12, [VMEM, ANY, VMEM], (shape(2 * TILES, WIDTH), shape(SMALL, WIDTH)), (VMEM, VMEM), [dma()],
         14 * 10**9, 1 << 16,
     )(arrived, across, added_own)
-    state, pats, swap, x_faces = call(
-        wall_first_kernel, 16,
-        [VMEM, VMEM, VMEM, VMEM, VMEM, ANY, ANY],
-        (shape(5, WIN, WIDTH), shape(NB, WIN, WIDTH), shape(8, WIDTH), shape(2, 64, WIDTH)),
-        (VMEM,) * 4,
-        [vmem(in_rows, WIDTH), vmem(2 * TILE_ROWS, WIDTH)] + work + [dma(3)],
+    products, swap = call(
+        wall_edge_kernel, 12,
+        [VMEM] * 4 + [ANY],
+        (shape(2, WIN, WIDTH), shape(8, WIDTH)), (VMEM, VMEM),
+        [vmem(2 * TILE_ROWS, WIDTH), vmem(NB, WIN, WIDTH)] + work + [dma()],
+        1 << 23, 4 << 20,
+    )(added_before, beside_small, own, own_blocks, across)
+    swapped = lax.ppermute(swap, "gx", outside_pairs)
+    state, pats, inside, x_faces = call(
+        wall_inner_kernel, 16,
+        [VMEM] * 6 + [ANY],
+        (shape(5, WIN, WIDTH), shape(NB, WIN, WIDTH), shape(3, WIN, WIDTH), shape(2, 64, WIDTH)), (VMEM,) * 4,
+        [vmem(in_rows, WIDTH)] + work + [dma(2)],
         1 << 24, 6 << 20,
-    )(arrived, added_before, beside_small, own, own_blocks, on_chip, across)
-    swapped = lax.ppermute(swap, "gx", outside_pairs)
-    inside = call(
-        wall_inner_kernel, 12,
-        [VMEM, VMEM, VMEM, ANY],
-        shape(3, WIN, WIDTH), VMEM,
-        [vmem(2 * TILE_ROWS, WIDTH)] + work + [dma()],
-        1 << 22, 3 << 20,
-    )(state, pats, own_blocks, on_chip)
+    )(arrived, added_before, beside_small, own, products, own_blocks, on_chip)
     solid, sent_back = call(
         wall_last_kernel, 12,
         [VMEM] * 6 + [ANY],

time: 74.1 us -> 73.1 us (0.987)
  transfers between devices with their start and end apart: 5 -> 5, of which waited for: 2 -> 1; matrix products, arithmetic and copies ran while one was open for 0% -> 0% of each run, Pallas kernels for 7% -> 7%
where the time goes in v6:
time: 73.1 us; the launch traced here: 72.7 us
  starting transfers between devices  34.3 us (47%)
  blocking collectives  17.1 us (23%)
  Pallas kernels  13.7 us (19%)
  waiting for transfers between devices  5.6 us (8%)
  local copies, waits for them, and re-layouts  1.24 us (2%)
  between operations  0.8 us (1%)
    all_to_all x1, blocking collectives, per_device(): lax.all_to_all(sent_back, 'gx', split_axis=0, concat_axis=0, tiled=True)  17.1 us
    all_to_all x1, starting transfers between devices, per_device(): lax.all_to_all(sent, 'gx', split_axis=0, concat_axis=0, tiled=True)  16.8 us
    all_to_all x1, starting transfers between devices, per_device(): lax.all_to_all(faces, ('gy', 'gz'), split_axis=0, concat_axis=0, tiled=True)  6.76 us
    all_to_all x1, waiting for transfers between devices, per_device(): lax.all_to_all(sent, 'gx', split_axis=0, concat_axis=0, tiled=True)  5.57 us
    pallas_call x1, Pallas kernels, per_device(): call(pick_kernel, 60, [HBM] * 7, (shape(RUNS, 1, 384), shape(RUNS, WIDTH)...  5.39 us
    ppermute x1, starting transfers between devices, per_device(): swapped = lax.ppermute(swap, 'gx', outside_pairs)  3.86 us
    ppermute x1, starting transfers between devices, per_device(): across = lax.ppermute(across, 'gx', outside_pairs)  3.54 us
    ppermute x1, starting transfers between devices, per_device(): on_chip = lax.ppermute(on_chip, 'gx', inside_pairs)  3.35 us
  transfers between devices with their start and end apart: 5, of which 1 were waited for; matrix products, arithmetic and copies ran while one was open for 0% of the time, Pallas kernels for 7%

profile of v6, /device:TPU:1, one launch (start us, length us, event | category | flops | bytes accessed | tf_op | source)
XLA Modules:
  0.0 72.7 jit_solution(3110284933230992264)
XLA Ops:
  0.6 5.4 %shard_map.95 = (f32[32,1,384]{2,1,0:T(1,128)}, f32[32,128]{1,0:T(8,128)}, f32[56,128]{1,0:T(8,128)}, f32[16,1,2048]{2,1,0:T(1,128)}, f32[3960,128]{1,0:T(8,128)}, /*index=5*/f32[1400,128]{1,0:T(8,128)}) custom-call(f32[1024,128]{1,0:T(8,128)} %bitcast.14, s32[32,128]{1,0:T(8,128)} %bitcast.19, s32[32,128]{1,0:T(8,128)} %bitcast.17, f32[8,128]{1,0:T(8,128)} %bitcast.21, ...), custom_call_target="tpu_custom_call" | custom-call | flops 2147483648 | bytes 4194304 | tf_op jit(solution)/shard_map/pallas_call | solution.py:458
  6.0 16.8 %all-to-all-start = ((f32[32,1,384]{2,1,0:T(1,128)}), f32[32,1,384]{2,1,0:T(1,128)S(1)}, u32[]{:S(2)}, u32[]{:S(2)}) async-start(f32[32,1,384]{2,1,0:T(1,128)} %get-tuple-element.18), calls=%async_computation | async-start | bytes 98304 | tf_op jit(solution)/shard_map/all_to_all | solution.py:473
  22.8 3.5 %collective-permute-start = (f32[1400,128]{1,0:T(8,128)}, f32[1400,128]{1,0:T(8,128)S(1)}, u32[]{:S(2)}, u32[]{:S(2)}) collective-permute-start(f32[1400,128]{1,0:T(8,128)} %get-tuple-element.19), channel_id=1, source_target_pairs={{0,496},{16,32},{32,16},{48,64},{64,48},{80,96},{96,80},{112,128},... | collective-permute-start | bytes 2150408 | tf_op jit(solution)/shard_map/ppermute | solution.py:475
  26.4 3.4 %collective-permute-start.1 = (f32[3960,128]{1,0:T(8,128)}, f32[3960,128]{1,0:T(8,128)S(1)}, u32[]{:S(2)}, u32[]{:S(2)}) collective-permute-start(f32[3960,128]{1,0:T(8,128)} %get-tuple-element.24), channel_id=1, source_target_pairs={{0,16},{16,0},{32,48},{48,32},{64,80},{80,64},{96,112},{112,96},{1... | collective-permute-start | bytes 6082568 | tf_op jit(solution)/shard_map/ppermute | solution.py:474
  29.7 5.6 %all-to-all-done.arrived = f32[32,1,384]{2,1,0:T(1,128)S(1)} async-done(((f32[32,1,384]{2,1,0:T(1,128)}), f32[32,1,384]{2,1,0:T(1,128)S(1)}, u32[]{:S(2)}, u32[]{:S(2)}) %all-to-all-start) | async-done | bytes 49184 | tf_op jit(solution)/shard_map/all_to_all | solution.py:473
  35.3 6.8 %all-to-all-start.1 = ((f32[16,1,2048]{2,1,0:T(1,128)}), f32[16,1,2048]{2,1,0:T(1,128)S(1)}, u32[]{:S(2)}, u32[]{:S(2)}) async-start(f32[16,1,2048]{2,1,0:T(1,128)} %get-tuple-element.26), calls=%async_computation.1 | async-start | bytes 262144 | tf_op jit(solution)/shard_map/all_to_all | solution.py:476
  42.1 0.4 shard_map.96.added_own
  42.5 0.0 collective-permute-done.across_hbm
  42.5 0.5 shard_map.97
  43.0 1.2 %copy-done = f32[1,8,5,128,128]{4,3,2,1,0:T(8,128)S(1)} copy-done((f32[1,8,5,128,128]{4,3,2,1,0:T(8,128)S(1)}, f32[1,8,5,128,128]{4,3,2,1,0:T(8,128)}, u32[]{:S(2)}) %copy-start) | copy-done | bytes 2621464
  44.2 0.0 copy-done.1
  44.2 0.9 %shard_map.98 = (f32[2,24,128]{2,1,0:T(8,128)S(1)}, f32[8,128]{1,0:T(8,128)S(1)}) custom-call(f32[16,128]{1,0:T(8,128)S(1)} %get-tuple-element.20.added_before, f32[120,128]{1,0:T(8,128)S(1)} %get-tuple-element.21.beside_small, f32[56,128]{1,0:T(8,128)S(1)} %copy-done.1, f32[5120,128]{1,0:T(8,128)S(1)} %bitcast.11, ...), custom_call_target="tpu_custom_call" | custom-call | flops 8388608 | bytes 4194304 | tf_op jit(solution)/shard_map/pallas_call | solution.py:486
  45.1 3.9 %collective-permute-start.2 = (f32[8,128]{1,0:T(8,128)S(1)}, f32[8,128]{1,0:T(8,128)S(1)}, u32[]{:S(2)}, u32[]{:S(2)}) collective-permute-start(f32[8,128]{1,0:T(8,128)S(1)} %get-tuple-element.31), channel_id=1, source_target_pairs={{0,496},{16,32},{32,16},{48,64},{64,48},{80,96},{96,80},{112,128},... | collective-permute-start | bytes 12296 | tf_op jit(solution)/shard_map/ppermute | solution.py:493
  49.0 0.0 collective-permute-done.1.on_chip_hbm
  49.0 2.0 %shard_map.99 = (f32[5,24,128]{2,1,0:T(8,128)S(1)}, f32[5,24,128]{2,1,0:T(8,128)S(1)}, f32[3,24,128]{2,1,0:T(8,128)S(1)}, f32[2,64,128]{2,1,0:T(8,128)S(1)}) custom-call(f32[32,1,384]{2,1,0:T(1,128)S(1)} %all-to-all-done.arrived, f32[16,128]{1,0:T(8,128)S(1)} %get-tuple-element.20.added_before, f32[120,128]{1,0:T(8,128)S(1)} %get-tuple-element.21.beside_small, ...), custom_call_target="tpu_custom_call" | custom-call | flops 16777216 | bytes 6291456 | tf_op jit(solution)/shard_map/pallas_call | solution.py:494
  51.0 0.0 copy-start.2
  51.0 0.0 copy-start.3
  51.0 0.0 copy-start.5
  51.0 0.0 copy-start.6
  51.0 0.0 collective-permute-done.2.swapped
  51.1 1.3 %shard_map.100 = (f32[8,128]{1,0:T(8,128)}, f32[32,1,128]{2,1,0:T(1,128)S(1)}) custom-call(f32[5,24,128]{2,1,0:T(8,128)S(1)} %get-tuple-element.28.state, f32[5,24,128]{2,1,0:T(8,128)S(1)} %get-tuple-element.29.pats, f32[3,24,128]{2,1,0:T(8,128)S(1)} %get-tuple-element.30.inside, f32[8,128]{1,0:T(8,128)S(1)} %collective-permute-done.2.swapped, ...), custom_call_target="tpu_custom_call" | custom-call | flops 8388608 | bytes 3145728 | tf_op jit(solution)/shard_map/pallas_call | solution.py:501
  52.3 0.0 all-to-all-done.1.faces
  52.4 17.1 %all_to_all.15.returned = f32[32,1,128]{2,1,0:T(1,128)S(1)} all-to-all(f32[32,1,128]{2,1,0:T(1,128)S(1)} %get-tuple-element.32), channel_id=1, replica_groups=mesh['gx'=32,'gy'=4,'gz'=4] {'gx'}, dimensions={0} | all-to-all | bytes 32768 | tf_op jit(solution)/shard_map/all_to_all | solution.py:508
  69.5 3.3 %shard_map.101 = f32[1024,128]{1,0:T(8,128)} custom-call(f32[1024,128]{1,0:T(8,128)S(1)} %bitcast.15, s32[1024,128]{1,0:T(8,128)S(1)} %bitcast.16, f32[2,64,128]{2,1,0:T(8,128)S(1)} %get-tuple-element.25.x_faces, f32[16,1,2048]{2,1,0:T(1,128)S(1)} %all-to-all-done.1.faces, s32[32,128]{1,0:T(8,128)S(1)} %bitcast.20, f32[32,128]{1,0:T(8,128)S(1)} %copy-done.6, ...), custom_call_target="tpu_custom_call" | custom-call | flops 2147483648 | bytes 1048576 | tf_op jit(solution)/shard_map/pallas_call | solution.py:510
  (8 shorter events, 0.0 us)
Async XLA Ops:
  0.6 41.4 %copy-start.4 = (s32[32,1,1,128]{3,2,1,0:T(1,128)S(1)}, s32[32,1,1,128]{3,2,1,0:T(1,128)}, u32[]{:S(2)}) copy-start(s32[32,1,1,128]{3,2,1,0:T(1,128)} %param.11) | copy-start | bytes 49156
  6.0 29.2 %all-to-all-start = ((f32[32,1,384]{2,1,0:T(1,128)}), f32[32,1,384]{2,1,0:T(1,128)S(1)}, u32[]{:S(2)}, u32[]{:S(2)}) async-start(f32[32,1,384]{2,1,0:T(1,128)} %get-tuple-element.18), calls=%async_computation | async-start | bytes 98304 | tf_op jit(solution)/shard_map/all_to_all | solution.py:473
  22.8 19.7 %collective-permute-start = (f32[1400,128]{1,0:T(8,128)}, f32[1400,128]{1,0:T(8,128)S(1)}, u32[]{:S(2)}, u32[]{:S(2)}) collective-permute-start(f32[1400,128]{1,0:T(8,128)} %get-tuple-element.19), channel_id=1, source_target_pairs={{0,496},{16,32},{32,16},{48,64},{64,48},{80,96},{96,80},{112,128},... | collective-permute-start | bytes 2150408 | tf_op jit(solution)/shard_map/ppermute | solution.py:475
  26.4 22.7 %collective-permute-start.1 = (f32[3960,128]{1,0:T(8,128)}, f32[3960,128]{1,0:T(8,128)S(1)}, u32[]{:S(2)}, u32[]{:S(2)}) collective-permute-start(f32[3960,128]{1,0:T(8,128)} %get-tuple-element.24), channel_id=1, source_target_pairs={{0,16},{16,0},{32,48},{48,32},{64,80},{80,64},{96,112},{112,96},{1... | collective-permute-start | bytes 6082568 | tf_op jit(solution)/shard_map/ppermute | solution.py:474
  35.3 17.1 %all-to-all-start.1 = ((f32[16,1,2048]{2,1,0:T(1,128)}), f32[16,1,2048]{2,1,0:T(1,128)S(1)}, u32[]{:S(2)}, u32[]{:S(2)}) async-start(f32[16,1,2048]{2,1,0:T(1,128)} %get-tuple-element.26), calls=%async_computation.1 | async-start | bytes 262144 | tf_op jit(solution)/shard_map/all_to_all | solution.py:476
  42.5 1.8 %copy-start = (f32[1,8,5,128,128]{4,3,2,1,0:T(8,128)S(1)}, f32[1,8,5,128,128]{4,3,2,1,0:T(8,128)}, u32[]{:S(2)}) copy-start(f32[1,8,5,128,128]{4,3,2,1,0:T(8,128)} %param.14) | copy-start | bytes 7864324
  42.5 1.8 %copy-start.1 = (f32[56,128]{1,0:T(8,128)S(1)}, f32[56,128]{1,0:T(8,128)}, u32[]{:S(2)}) copy-start(f32[56,128]{1,0:T(8,128)} %get-tuple-element.22.own) | copy-start | bytes 86020
  45.1 5.9 %collective-permute-start.2 = (f32[8,128]{1,0:T(8,128)S(1)}, f32[8,128]{1,0:T(8,128)S(1)}, u32[]{:S(2)}, u32[]{:S(2)}) collective-permute-start(f32[8,128]{1,0:T(8,128)S(1)} %get-tuple-element.31), channel_id=1, source_target_pairs={{0,496},{16,32},{32,16},{48,64},{64,48},{80,96},{96,80},{112,128},... | collective-permute-start | bytes 12296 | tf_op jit(solution)/shard_map/ppermute | solution.py:493
  51.0 18.4 %copy-start.2 = (f32[16,64,128]{2,1,0:T(8,128)S(1)}, f32[16,64,128]{2,1,0:T(8,128)}, u32[]{:S(2)}) copy-start(f32[16,64,128]{2,1,0:T(8,128)} %param.8) | copy-start | bytes 1572868
  51.0 18.4 %copy-start.3 = (s32[16,64,128]{2,1,0:T(8,128)S(1)}, s32[16,64,128]{2,1,0:T(8,128)}, u32[]{:S(2)}) copy-start(s32[16,64,128]{2,1,0:T(8,128)} %param.9) | copy-start | bytes 1572868
  51.0 18.4 %copy-start.5 = (s32[32,1,1,128]{3,2,1,0:T(1,128)S(1)}, s32[32,1,1,128]{3,2,1,0:T(1,128)}, u32[]{:S(2)}) copy-start(s32[32,1,1,128]{3,2,1,0:T(1,128)} %param.10) | copy-start | bytes 49156
  51.0 18.4 %copy-start.6 = (f32[32,128]{1,0:T(8,128)S(1)}, f32[32,128]{1,0:T(8,128)}, u32[]{:S(2)}) copy-start(f32[32,128]{1,0:T(8,128)} %get-tuple-element.27.outgoing) | copy-start | bytes 49156

commit v7 on v6

--- a/solution.py
+++ b/solution.py
@@ -67,7 +67,7 @@
 def pick_kernel(
     fluid_hbm, src_hbm, dst_hbm, old_hbm, diag_hbm, pattern_hbm, blocks_hbm,
     sent, outgoing, own, faces, on_chip_hbm, across_hbm,
-    fluid, src, dst, pattern, table, packed, staged_in, staged_out, sems,
+    fluid, src, dst, pattern, table, staged_in, staged_out, sems,
 ):
     me = lax.axis_index("gx")
     parity = lax.rem(me, 2)
@@ -77,7 +77,7 @@
         started.start()
         return started
 
-    loads = [copy(fluid_hbm.at[128 * i : 128 * i + 128], fluid.at[128 * i : 128 * i + 128], i) for i in range(8)]
+    load_fluid = copy(fluid_hbm, fluid, 0)
     load_src = copy(src_hbm, src, 8)
     small = [
         copy(dst_hbm, dst, 9),
@@ -85,12 +85,12 @@
         copy(diag_hbm, own.at[40:48], 11),
         copy(pattern_hbm, pattern, 16),
     ]
-    inside = copy(blocks_hbm.at[pl.ds((1 - parity) * 2 * TILE_ROWS, 6 * TILE_ROWS)], staged_in, 12)
-    outside = copy(blocks_hbm.at[pl.ds(parity * 6 * TILE_ROWS, 2 * TILE_ROWS)], staged_out, 13)
+    inside = copy(blocks_hbm.at[pl.ds((1 - parity) * 2 * TILE_ROWS, 6 * TILE_ROWS)], staged_in.at[0 : 6 * TILE_ROWS], 12)
+    outside = copy(blocks_hbm.at[pl.ds(parity * 6 * TILE_ROWS, 2 * TILE_ROWS)], staged_out.at[0 : 2 * TILE_ROWS], 13)
     before_z = lax.axis_index("gy") * 4 + lax.rem(lax.axis_index("gz") + 3, 4)
     after_z = lax.axis_index("gy") * 4 + lax.rem(lax.axis_index("gz") + 1, 4)
+    load_fluid.wait()
     for block in range(8):
-        loads[block].wait()
         turned = fluid[128 * block : 128 * block + 128, :].T
         high, low = two_parts(turned)
         table[0:128, 128 * block : 128 * block + 128] = high
@@ -105,11 +105,12 @@
     for offset in range(NB):
         own[48 + offset : 49 + offset, 0:TILES] = pattern[offset].astype(F32)
     first, last = fluid[0:64, :], fluid[960:1024, :]
-    for index, face in ((0, jnp.where(parity == 0, last, first)), (1, jnp.where(parity == 0, first, last))):
-        packed[index, 0:56, :] = own[...]
-        packed[index, 56:120, :] = face
-    tail_in = copy(packed.at[0], on_chip_hbm.at[6 * TILE_ROWS : 6 * TILE_ROWS + SMALL], 14)
-    tail_out = copy(packed.at[1], across_hbm.at[2 * TILE_ROWS : 2 * TILE_ROWS + SMALL], 15)
+    for packed, start, face in (
+        (staged_in, 6 * TILE_ROWS, jnp.where(parity == 0, last, first)),
+        (staged_out, 2 * TILE_ROWS, jnp.where(parity == 0, first, last)),
+    ):
+        packed[start : start + 56, :] = own[...]
+        packed[start + 56 : start + SMALL, :] = face
     y, z = lax.axis_index("gy"), lax.axis_index("gz")
     after_y, before_y = lax.rem(y + 1, 4) * 4 + z, lax.rem(y + 3, 4) * 4 + z
     for slab in range(16):
@@ -122,8 +123,8 @@
         if start == RUNS // 2:
             inside.wait()
             outside.wait()
-            inside = copy(staged_in, on_chip_hbm.at[0 : 6 * TILE_ROWS], 17)
-            outside = copy(staged_out, across_hbm.at[0 : 2 * TILE_ROWS], 18)
+            inside = copy(staged_in, on_chip_hbm, 17)
+            outside = copy(staged_out, across_hbm, 18)
         ids = lanes([src[r : r + 1, :] for r in range(start, start + group)])
         picked = jnp.dot(table[...], row_hots(ids >> 7, ROWS), preferred_element_type=F32)
         both = picked[0:128] + picked[128:256]
@@ -136,7 +137,7 @@
             sent[r ^ 1, :, 128:256] = mine
             beside = (r + 1) % RUNS if r % 2 else (r - 1) % RUNS
             sent[beside, :, 256:384] = mine
-    for each in (inside, outside, tail_in, tail_out):
+    for each in (inside, outside):
         each.wait()
 
 
@@ -203,6 +204,12 @@
     added[TILES : 2 * TILES, :] = spread_run(
         lambda r: small[r : r + 1, :].astype(I32), lambda r: arrived[r, :, 256:384]
     )
+
+
+def load_kernel(after, blocks_hbm, blocks, sem):
+    load = pltpu.make_async_copy(blocks_hbm, blocks, sem)
+    load.start()
+    load.wait()
 
 
 def windows(parity, keep, own, partner, beside, added):
@@ -382,7 +389,18 @@
             returned[8 * block + r] = found[r : r + 1, :]
 
 
-def final_kernel(fluid, liquid, x_faces, faces, src, outgoing, returned, fluid_new):
+def final_kernel(
+    fluid_hbm, liquid_hbm, x_faces_hbm, faces, src, outgoing, returned,
+    fluid_new,
+    fluid, liquid, x_faces, sems,
+):
+    loads = [
+        pltpu.make_async_copy(fluid_hbm, fluid, sems.at[0]),
+        pltpu.make_async_copy(liquid_hbm, liquid, sems.at[1]),
+        pltpu.make_async_copy(x_faces_hbm, x_faces, sems.at[2]),
+    ]
+    for each in loads:
+        each.start()
     group = 4
     total = None
     for start in range(0, RUNS, group):
@@ -393,6 +411,8 @@
         added = lax.dot_general(row_hots(ids >> 7, ROWS), placed, CONTRACT_LAST, preferred_element_type=F32)
         total = added if total is None else total + added
     wall = total[:, 0:128] + total[:, 128:256]
+    for each in loads:
+        each.wait()
     y, z = lax.axis_index("gy"), lax.axis_index("gz")
     after_y, before_y = lax.rem(y + 1, 4) * 4 + z, lax.rem(y + 3, 4) * 4 + z
     after_z, before_z = y * 4 + lax.rem(z + 1, 4), y * 4 + lax.rem(z + 3, 4)
@@ -446,6 +466,10 @@
     return pltpu.SemaphoreType.DMA(dims) if dims else pltpu.SemaphoreType.DMA
 
 
+def in_hbm(array):
+    return pltpu.with_memory_space_constraint(array, pltpu.HBM)
+
+
 def per_device(fluid_temp, liquid, face_src, face_dst, solid_old, solid_diag, blocks, pattern):
     inside_pairs = [(i, i ^ 1) for i in range(RUNS)]
     outside_pairs = [(i, (i - 1) % RUNS if i % 2 == 0 else (i + 1) % RUNS) for i in range(RUNS)]
@@ -465,7 +489,7 @@
         (VMEM, VMEM, VMEM, VMEM, HBM, HBM),
         [
             vmem(ROWS, WIDTH), vmem(RUNS, WIDTH, kind=I32), vmem(RUNS, WIDTH, kind=I32), vmem(NB, 1, TILES, kind=I32),
-            vmem(256, ROWS, kind=BF16), vmem(2, SMALL, WIDTH), vmem(6 * TILE_ROWS, WIDTH), vmem(2 * TILE_ROWS, WIDTH), dma(19),
+            vmem(256, ROWS, kind=BF16), vmem(in_rows, WIDTH), vmem(out_rows, WIDTH), dma(19),
         ],
         2 * 256 * 1024 * 4096, 1 << 22,
     )(fluid, src, dst, solid_old[0], solid_diag[0], jnp.transpose(pattern, (2, 0, 1)), own_blocks)
@@ -483,13 +507,16 @@
         beside_run_kernel, 12, [VMEM, ANY, VMEM], (shape(2 * TILES, WIDTH), shape(SMALL, WIDTH)), (VMEM, VMEM), [dma()],
         14 * 10**9, 1 << 16,
     )(arrived, across, added_own)
+    held_blocks = call(
+        load_kernel, 12, [ANY, HBM], shape(TILES * TILE_ROWS, WIDTH), VMEM, [dma()], 1 << 10, 6 << 20
+    )(own, in_hbm(own_blocks))
     products, swap = call(
         wall_edge_kernel, 12,
         [VMEM] * 4 + [ANY],
         (shape(2, WIN, WIDTH), shape(8, WIDTH)), (VMEM, VMEM),
         [vmem(2 * TILE_ROWS, WIDTH), vmem(NB, WIN, WIDTH)] + work + [dma()],
         1 << 23, 4 << 20,
-    )(added_before, beside_small, own, own_blocks, across)
+    )(added_before, beside_small, own, held_blocks, across)
     swapped = lax.ppermute(swap, "gx", outside_pairs)
     state, pats, inside, x_faces = call(
         wall_inner_kernel, 16,
@@ -497,19 +524,20 @@
         (shape(5, WIN, WIDTH), shape(NB, WIN, WIDTH), shape(3, WIN, WIDTH), shape(2, 64, WIDTH)), (VMEM,) * 4,
         [vmem(in_rows, WIDTH)] + work + [dma(2)],
         1 << 24, 6 << 20,
-    )(arrived, added_before, beside_small, own, products, own_blocks, on_chip)
+    )(arrived, added_before, beside_small, own, products, held_blocks, on_chip)
     solid, sent_back = call(
         wall_last_kernel, 12,
         [VMEM] * 6 + [ANY],
         (shape(TILES, WIDTH), shape(RUNS, 1, WIDTH)), (VMEM, VMEM),
         [vmem(2 * TILE_ROWS, WIDTH)] + work + [dma()],
         1 << 23, 3 << 20,
-    )(state, pats, inside, swapped, own, own_blocks, across)
+    )(state, pats, inside, swapped, own, held_blocks, across)
     returned = lax.all_to_all(sent_back, "gx", split_axis=0, concat_axis=0, tiled=True)
 
     fluid_new = call(
-        final_kernel, 16, [VMEM] * 7, shape(ROWS, WIDTH), VMEM, [], 2 * 256 * 1024 * 4096, 1 << 20
-    )(fluid, liquid.reshape(ROWS, WIDTH), x_faces, faces, src, outgoing, returned)
+        final_kernel, 16, [HBM] * 3 + [VMEM] * 4, shape(ROWS, WIDTH), VMEM,
+        [vmem(ROWS, WIDTH), vmem(ROWS, WIDTH, kind=I32), vmem(2, 64, WIDTH), dma(3)], 2 * 256 * 1024 * 4096, 1 << 20,
+    )(in_hbm(fluid), in_hbm(liquid.reshape(ROWS, WIDTH)), in_hbm(x_faces), faces, src, outgoing, returned)
     return fluid_new.reshape(fluid_temp.shape), solid[None]
 
 

time: 73.1 us -> 76.3 us (1.044)
  Pallas kernels: 13.7 us -> 17.3 us
  waiting for transfers between devices: 5.6 us -> 3.07 us
  blocking collectives: 17.1 us -> 18.7 us
    pallas_call x1 -> x2, Pallas kernels: 3.26 us -> 6.72 us  [the longest x1 4.96 us: per_device(): call(final_kernel, 16, [HBM] * 3 + [VMEM] * 4, shape(ROWS, WIDTH), VMEM,...]
    all_to_all x1, waiting for transfers between devices: 5.57 us -> 3.06 us  [per_device(): lax.all_to_all(sent, 'gx', split_axis=0, concat_axis=0, tiled=True)]
    all_to_all x1, blocking collectives: 17.1 us -> 18.7 us  [per_device(): lax.all_to_all(sent_back, 'gx', split_axis=0, concat_axis=0, tiled=True)]
    unnamed x14 -> x12, local copies, waits for them, and re-layouts: 1.24 us -> 1.61 us
  transfers between devices with their start and end apart: 5 -> 5, of which waited for: 1 -> 1; matrix products, arithmetic and copies ran while one was open for 0% -> 0% of each run, Pallas kernels for 7% -> 10%
where the time goes in v7:
time: 76.3 us; the launch traced here: 75.7 us
  starting transfers between devices  34.3 us (45%)
  blocking collectives  18.7 us (25%)
  Pallas kernels  17.3 us (23%)
  waiting for transfers between devices  3.07 us (4%)
  local copies, waits for them, and re-layouts  1.61 us (2%)
    all_to_all x1, blocking collectives, per_device(): lax.all_to_all(sent_back, 'gx', split_axis=0, concat_axis=0, tiled=True)  18.7 us
    all_to_all x1, starting transfers between devices, per_device(): lax.all_to_all(sent, 'gx', split_axis=0, concat_axis=0, tiled=True)  16.8 us
    all_to_all x1, starting transfers between devices, per_device(): lax.all_to_all(faces, ('gy', 'gz'), split_axis=0, concat_axis=0, tiled=True)  6.75 us
    pallas_call x1, Pallas kernels, per_device(): call(pick_kernel, 60, [HBM] * 7, (shape(RUNS, 1, 384), shape(RUNS, WIDTH)...  4.97 us
    pallas_call x1, Pallas kernels, per_device(): call(final_kernel, 16, [HBM] * 3 + [VMEM] * 4, shape(ROWS, WIDTH), VMEM,...  4.96 us
    ppermute x1, starting transfers between devices, per_device(): swapped = lax.ppermute(swap, 'gx', outside_pairs)  3.86 us
    ppermute x1, starting transfers between devices, per_device(): across = lax.ppermute(across, 'gx', outside_pairs)  3.54 us
    ppermute x1, starting transfers between devices, per_device(): on_chip = lax.ppermute(on_chip, 'gx', inside_pairs)  3.35 us
  transfers between devices with their start and end apart: 5, of which 1 were waited for; matrix products, arithmetic and copies ran while one was open for 0% of the time, Pallas kernels for 10%

profile of v7, /device:TPU:1, one launch (start us, length us, event | category | flops | bytes accessed | tf_op | source)
XLA Modules:
  0.0 75.7 jit_solution(17959139496911267297)
XLA Ops:
  0.6 5.0 %shard_map.95 = (f32[32,1,384]{2,1,0:T(1,128)}, f32[32,128]{1,0:T(8,128)}, f32[56,128]{1,0:T(8,128)}, f32[16,1,2048]{2,1,0:T(1,128)}, f32[3960,128]{1,0:T(8,128)}, /*index=5*/f32[1400,128]{1,0:T(8,128)}) custom-call(f32[1024,128]{1,0:T(8,128)} %bitcast.16, s32[32,128]{1,0:T(8,128)} %bitcast.12, s32[32,128]{1,0:T(8,128)} %bitcast.10, f32[8,128]{1,0:T(8,128)} %bitcast.19, ...), custom_call_target="tpu_custom_call" | custom-call | flops 2147483648 | bytes 4194304 | tf_op jit(solution)/shard_map/pallas_call | solution.py:482
  5.6 16.8 %all-to-all-start = ((f32[32,1,384]{2,1,0:T(1,128)}), f32[32,1,384]{2,1,0:T(1,128)S(1)}, u32[]{:S(2)}, u32[]{:S(2)}) async-start(f32[32,1,384]{2,1,0:T(1,128)} %get-tuple-element.18), calls=%async_computation | async-start | bytes 98304 | tf_op jit(solution)/shard_map/all_to_all | solution.py:497
  22.4 3.5 %collective-permute-start = (f32[1400,128]{1,0:T(8,128)}, f32[1400,128]{1,0:T(8,128)S(1)}, u32[]{:S(2)}, u32[]{:S(2)}) collective-permute-start(f32[1400,128]{1,0:T(8,128)} %get-tuple-element.19), channel_id=1, source_target_pairs={{0,496},{16,32},{32,16},{48,64},{64,48},{80,96},{96,80},{112,128},... | collective-permute-start | bytes 2150408 | tf_op jit(solution)/shard_map/ppermute | solution.py:499
  25.9 3.4 %collective-permute-start.1 = (f32[3960,128]{1,0:T(8,128)}, f32[3960,128]{1,0:T(8,128)}, u32[]{:S(2)}, u32[]{:S(2)}) collective-permute-start(f32[3960,128]{1,0:T(8,128)} %get-tuple-element.24), channel_id=1, source_target_pairs={{0,16},{16,0},{32,48},{48,32},{64,80},{80,64},{96,112},{112,96},{1... | collective-permute-start | bytes 6082568 | tf_op jit(solution)/shard_map/ppermute | solution.py:498
  29.3 0.0 copy-start
  29.3 0.7 copy-done
  30.0 1.8 %shard_map.98.own_blocks = f32[5120,128]{1,0:T(8,128)S(1)} custom-call(f32[56,128]{1,0:T(8,128)S(1)} %copy-done, f32[5120,128]{1,0:T(8,128)} %bitcast.15), custom_call_target="tpu_custom_call" | custom-call | flops 1024 | bytes 6291456 | tf_op jit(solution)/shard_map/pallas_call | solution.py:510
  31.8 3.1 %all-to-all-done.arrived = f32[32,1,384]{2,1,0:T(1,128)S(1)} async-done(((f32[32,1,384]{2,1,0:T(1,128)}), f32[32,1,384]{2,1,0:T(1,128)S(1)}, u32[]{:S(2)}, u32[]{:S(2)}) %all-to-all-start) | async-done | bytes 49184 | tf_op jit(solution)/shard_map/all_to_all | solution.py:497
  34.9 6.8 %all-to-all-start.1 = ((f32[16,1,2048]{2,1,0:T(1,128)}), f32[16,1,2048]{2,1,0:T(1,128)S(1)}, u32[]{:S(2)}, u32[]{:S(2)}) async-start(f32[16,1,2048]{2,1,0:T(1,128)} %get-tuple-element.26), calls=%async_computation.1 | async-start | bytes 262144 | tf_op jit(solution)/shard_map/all_to_all | solution.py:500
  41.6 0.0 copy-done.3
  41.6 0.4 shard_map.96.added_own
  42.0 0.0 collective-permute-done.across_hbm
  42.0 0.5 shard_map.97
  42.6 0.2 copy-done.1
  42.8 0.9 %shard_map.99 = (f32[2,24,128]{2,1,0:T(8,128)S(1)}, f32[8,128]{1,0:T(8,128)S(1)}) custom-call(f32[16,128]{1,0:T(8,128)S(1)} %get-tuple-element.20.added_before, f32[120,128]{1,0:T(8,128)S(1)} %get-tuple-element.21.beside_small, f32[56,128]{1,0:T(8,128)S(1)} %copy-done.1, f32[5120,128]{1,0:T(8,128)S(1)} %shard_map.98.own_blocks, ...), custom_call_target="tpu_custom_call" | custom-call | flops 8388608 | bytes 4194304 | tf_op jit(solution)/shard_map/pallas_call | solution.py:513
  43.7 3.9 %collective-permute-start.2 = (f32[8,128]{1,0:T(8,128)S(1)}, f32[8,128]{1,0:T(8,128)S(1)}, u32[]{:S(2)}, u32[]{:S(2)}) collective-permute-start(f32[8,128]{1,0:T(8,128)S(1)} %get-tuple-element.31), channel_id=1, source_target_pairs={{0,496},{16,32},{32,16},{48,64},{64,48},{80,96},{96,80},{112,128},... | collective-permute-start | bytes 12296 | tf_op jit(solution)/shard_map/ppermute | solution.py:520
  47.6 0.0 collective-permute-done.1.on_chip_hbm
  47.6 2.6 %shard_map.100 = (f32[5,24,128]{2,1,0:T(8,128)S(1)}, f32[5,24,128]{2,1,0:T(8,128)S(1)}, f32[3,24,128]{2,1,0:T(8,128)S(1)}, f32[2,64,128]{2,1,0:T(8,128)S(1)}) custom-call(f32[32,1,384]{2,1,0:T(1,128)S(1)} %all-to-all-done.arrived, f32[16,128]{1,0:T(8,128)S(1)} %get-tuple-element.20.added_before, f32[120,128]{1,0:T(8,128)S(1)} %get-tuple-element.21.beside_small, ...), custom_call_target="tpu_custom_call" | custom-call | flops 16777216 | bytes 6291456 | tf_op jit(solution)/shard_map/pallas_call | solution.py:521
  50.2 0.6 copy-done.2
  50.8 0.0 collective-permute-done.2.swapped
  50.8 1.3 %shard_map.101 = (f32[8,128]{1,0:T(8,128)}, f32[32,1,128]{2,1,0:T(1,128)S(1)}) custom-call(f32[5,24,128]{2,1,0:T(8,128)S(1)} %get-tuple-element.28.state, f32[5,24,128]{2,1,0:T(8,128)S(1)} %get-tuple-element.29.pats, f32[3,24,128]{2,1,0:T(8,128)S(1)} %get-tuple-element.30.inside, f32[8,128]{1,0:T(8,128)S(1)} %collective-permute-done.2.swapped, ...), custom_call_target="tpu_custom_call" | custom-call | flops 8388608 | bytes 3145728 | tf_op jit(solution)/shard_map/pallas_call | solution.py:528
  52.1 0.0 all-to-all-done.1.faces
  52.1 18.7 %all_to_all.15.returned = f32[32,1,128]{2,1,0:T(1,128)S(1)} all-to-all(f32[32,1,128]{2,1,0:T(1,128)S(1)} %get-tuple-element.32), channel_id=1, replica_groups=mesh['gx'=32,'gy'=4,'gz'=4] {'gx'}, dimensions={0} | all-to-all | bytes 32768 | tf_op jit(solution)/shard_map/all_to_all | solution.py:535
  70.8 5.0 %shard_map.102 = f32[1024,128]{1,0:T(8,128)} custom-call(f32[1024,128]{1,0:T(8,128)} %bitcast.17, s32[1024,128]{1,0:T(8,128)} %bitcast.18, f32[2,64,128]{2,1,0:T(8,128)} %copy-done.2, f32[16,1,2048]{2,1,0:T(1,128)S(1)} %all-to-all-done.1.faces, s32[32,128]{1,0:T(8,128)S(1)} %bitcast.13, f32[32,128]{1,0:T(8,128)S(1)} %copy-done.5, ...), custom_call_target="tpu_custom_call" | custom-call | flops 2147483648 | bytes 1048576 | tf_op jit(solution)/shard_map/pallas_call | solution.py:537
  (7 shorter events, 0.0 us)
Async XLA Ops:
  5.6 29.3 %all-to-all-start = ((f32[32,1,384]{2,1,0:T(1,128)}), f32[32,1,384]{2,1,0:T(1,128)S(1)}, u32[]{:S(2)}, u32[]{:S(2)}) async-start(f32[32,1,384]{2,1,0:T(1,128)} %get-tuple-element.18), calls=%async_computation | async-start | bytes 98304 | tf_op jit(solution)/shard_map/all_to_all | solution.py:497
  22.4 19.7 %collective-permute-start = (f32[1400,128]{1,0:T(8,128)}, f32[1400,128]{1,0:T(8,128)S(1)}, u32[]{:S(2)}, u32[]{:S(2)}) collective-permute-start(f32[1400,128]{1,0:T(8,128)} %get-tuple-element.19), channel_id=1, source_target_pairs={{0,496},{16,32},{32,16},{48,64},{64,48},{80,96},{96,80},{112,128},... | collective-permute-start | bytes 2150408 | tf_op jit(solution)/shard_map/ppermute | solution.py:499
  25.9 21.7 %collective-permute-start.1 = (f32[3960,128]{1,0:T(8,128)}, f32[3960,128]{1,0:T(8,128)}, u32[]{:S(2)}, u32[]{:S(2)}) collective-permute-start(f32[3960,128]{1,0:T(8,128)} %get-tuple-element.24), channel_id=1, source_target_pairs={{0,16},{16,0},{32,48},{48,32},{64,80},{80,64},{96,112},{112,96},{1... | collective-permute-start | bytes 6082568 | tf_op jit(solution)/shard_map/ppermute | solution.py:498
  29.3 0.7 copy-start
  30.0 11.6 %copy-start.3 = (s32[32,1,1,128]{3,2,1,0:T(1,128)S(1)}, s32[32,1,1,128]{3,2,1,0:T(1,128)}, u32[]{:S(2)}) copy-start(s32[32,1,1,128]{3,2,1,0:T(1,128)} %param.11) | copy-start | bytes 49156
  34.9 17.2 %all-to-all-start.1 = ((f32[16,1,2048]{2,1,0:T(1,128)}), f32[16,1,2048]{2,1,0:T(1,128)S(1)}, u32[]{:S(2)}, u32[]{:S(2)}) async-start(f32[16,1,2048]{2,1,0:T(1,128)} %get-tuple-element.26), calls=%async_computation.1 | async-start | bytes 262144 | tf_op jit(solution)/shard_map/all_to_all | solution.py:500
  42.0 0.8 %copy-start.1 = (f32[56,128]{1,0:T(8,128)S(1)}, f32[56,128]{1,0:T(8,128)}, u32[]{:S(2)}) copy-start(f32[56,128]{1,0:T(8,128)} %get-tuple-element.22.after.own) | copy-start | bytes 86020
  43.7 7.1 %collective-permute-start.2 = (f32[8,128]{1,0:T(8,128)S(1)}, f32[8,128]{1,0:T(8,128)S(1)}, u32[]{:S(2)}, u32[]{:S(2)}) collective-permute-start(f32[8,128]{1,0:T(8,128)S(1)} %get-tuple-element.31), channel_id=1, source_target_pairs={{0,496},{16,32},{32,16},{48,64},{64,48},{80,96},{96,80},{112,128},... | collective-permute-start | bytes 12296 | tf_op jit(solution)/shard_map/ppermute | solution.py:520
  50.2 0.6 copy-start.2
  50.8 20.0 %copy-start.4 = (s32[32,1,1,128]{3,2,1,0:T(1,128)S(1)}, s32[32,1,1,128]{3,2,1,0:T(1,128)}, u32[]{:S(2)}) copy-start(s32[32,1,1,128]{3,2,1,0:T(1,128)} %param.10) | copy-start | bytes 49156
  50.8 20.0 %copy-start.5 = (f32[32,128]{1,0:T(8,128)S(1)}, f32[32,128]{1,0:T(8,128)}, u32[]{:S(2)}) copy-start(f32[32,128]{1,0:T(8,128)} %get-tuple-element.27.outgoing) | copy-start | bytes 49156

commit v8 on v6

--- a/solution.py
+++ b/solution.py
@@ -67,7 +67,7 @@
 def pick_kernel(
     fluid_hbm, src_hbm, dst_hbm, old_hbm, diag_hbm, pattern_hbm, blocks_hbm,
     sent, outgoing, own, faces, on_chip_hbm, across_hbm,
-    fluid, src, dst, pattern, table, packed, staged_in, staged_out, sems,
+    fluid, src, dst, pattern, table, staged_in, staged_out, sems,
 ):
     me = lax.axis_index("gx")
     parity = lax.rem(me, 2)
@@ -77,7 +77,7 @@
         started.start()
         return started
 
-    loads = [copy(fluid_hbm.at[128 * i : 128 * i + 128], fluid.at[128 * i : 128 * i + 128], i) for i in range(8)]
+    load_fluid = copy(fluid_hbm, fluid, 0)
     load_src = copy(src_hbm, src, 8)
     small = [
         copy(dst_hbm, dst, 9),
@@ -85,12 +85,12 @@
         copy(diag_hbm, own.at[40:48], 11),
         copy(pattern_hbm, pattern, 16),
     ]
-    inside = copy(blocks_hbm.at[pl.ds((1 - parity) * 2 * TILE_ROWS, 6 * TILE_ROWS)], staged_in, 12)
-    outside = copy(blocks_hbm.at[pl.ds(parity * 6 * TILE_ROWS, 2 * TILE_ROWS)], staged_out, 13)
+    inside = copy(blocks_hbm.at[pl.ds((1 - parity) * 2 * TILE_ROWS, 6 * TILE_ROWS)], staged_in.at[0 : 6 * TILE_ROWS], 12)
+    outside = copy(blocks_hbm.at[pl.ds(parity * 6 * TILE_ROWS, 2 * TILE_ROWS)], staged_out.at[0 : 2 * TILE_ROWS], 13)
     before_z = lax.axis_index("gy") * 4 + lax.rem(lax.axis_index("gz") + 3, 4)
     after_z = lax.axis_index("gy") * 4 + lax.rem(lax.axis_index("gz") + 1, 4)
+    load_fluid.wait()
     for block in range(8):
-        loads[block].wait()
         turned = fluid[128 * block : 128 * block + 128, :].T
         high, low = two_parts(turned)
         table[0:128, 128 * block : 128 * block + 128] = high
@@ -105,11 +105,12 @@
     for offset in range(NB):
         own[48 + offset : 49 + offset, 0:TILES] = pattern[offset].astype(F32)
     first, last = fluid[0:64, :], fluid[960:1024, :]
-    for index, face in ((0, jnp.where(parity == 0, last, first)), (1, jnp.where(parity == 0, first, last))):
-        packed[index, 0:56, :] = own[...]
-        packed[index, 56:120, :] = face
-    tail_in = copy(packed.at[0], on_chip_hbm.at[6 * TILE_ROWS : 6 * TILE_ROWS + SMALL], 14)
-    tail_out = copy(packed.at[1], across_hbm.at[2 * TILE_ROWS : 2 * TILE_ROWS + SMALL], 15)
+    for packed, start, face in (
+        (staged_in, 6 * TILE_ROWS, jnp.where(parity == 0, last, first)),
+        (staged_out, 2 * TILE_ROWS, jnp.where(parity == 0, first, last)),
+    ):
+        packed[start : start + 56, :] = own[...]
+        packed[start + 56 : start + SMALL, :] = face
     y, z = lax.axis_index("gy"), lax.axis_index("gz")
     after_y, before_y = lax.rem(y + 1, 4) * 4 + z, lax.rem(y + 3, 4) * 4 + z
     for slab in range(16):
@@ -122,8 +123,8 @@
         if start == RUNS // 2:
             inside.wait()
             outside.wait()
-            inside = copy(staged_in, on_chip_hbm.at[0 : 6 * TILE_ROWS], 17)
-            outside = copy(staged_out, across_hbm.at[0 : 2 * TILE_ROWS], 18)
+            inside = copy(staged_in, on_chip_hbm, 17)
+            outside = copy(staged_out, across_hbm, 18)
         ids = lanes([src[r : r + 1, :] for r in range(start, start + group)])
         picked = jnp.dot(table[...], row_hots(ids >> 7, ROWS), preferred_element_type=F32)
         both = picked[0:128] + picked[128:256]
@@ -136,7 +137,7 @@
             sent[r ^ 1, :, 128:256] = mine
             beside = (r + 1) % RUNS if r % 2 else (r - 1) % RUNS
             sent[beside, :, 256:384] = mine
-    for each in (inside, outside, tail_in, tail_out):
+    for each in (inside, outside):
         each.wait()
 
 
@@ -465,7 +466,7 @@
         (VMEM, VMEM, VMEM, VMEM, HBM, HBM),
         [
             vmem(ROWS, WIDTH), vmem(RUNS, WIDTH, kind=I32), vmem(RUNS, WIDTH, kind=I32), vmem(NB, 1, TILES, kind=I32),
-            vmem(256, ROWS, kind=BF16), vmem(2, SMALL, WIDTH), vmem(6 * TILE_ROWS, WIDTH), vmem(2 * TILE_ROWS, WIDTH), dma(19),
+            vmem(256, ROWS, kind=BF16), vmem(in_rows, WIDTH), vmem(out_rows, WIDTH), dma(19),
         ],
         2 * 256 * 1024 * 4096, 1 << 22,
     )(fluid, src, dst, solid_old[0], solid_diag[0], jnp.transpose(pattern, (2, 0, 1)), own_blocks)
@@ -477,11 +478,11 @@
 
     work = [vmem(WIN, WIDTH), vmem(NB, WIN, WIDTH), vmem(WIN, WIDTH)]
     added_own = call(
-        own_run_kernel, 12, [VMEM, VMEM], shape(TILES, WIDTH), VMEM, [], 65 * 10**8, 1 << 16
+        own_run_kernel, 12, [VMEM, VMEM], shape(TILES, WIDTH), VMEM, [], 20 * 10**9, 1 << 16
     )(arrived, dst)
     added_before, beside_small = call(
         beside_run_kernel, 12, [VMEM, ANY, VMEM], (shape(2 * TILES, WIDTH), shape(SMALL, WIDTH)), (VMEM, VMEM), [dma()],
-        14 * 10**9, 1 << 16,
+        10**9, 1 << 16,
     )(arrived, across, added_own)
     products, swap = call(
         wall_edge_kernel, 12,

time: 73.1 us -> 74.8 us (1.023)
  blocking collectives: 17.1 us -> 19.2 us
  starting transfers between devices: 34.3 us -> 33 us
  waiting for transfers between devices: 5.6 us -> 6.88 us
    all_to_all x1, blocking collectives: 17.1 us -> 19.2 us  [per_device(): lax.all_to_all(sent_back, 'gx', split_axis=0, concat_axis=0, tiled=True)]
    all_to_all x1, waiting for transfers between devices: 5.57 us -> 6.86 us  [per_device(): lax.all_to_all(sent, 'gx', split_axis=0, concat_axis=0, tiled=True)]
    ppermute x1, starting transfers between devices: 3.35 us -> 2.14 us  [per_device(): on_chip = lax.ppermute(on_chip, 'gx', inside_pairs)]
where the time goes in v8:
time: 74.8 us; the launch traced here: 74.4 us
  starting transfers between devices  33 us (44%)
  blocking collectives  19.2 us (26%)
  Pallas kernels  13.3 us (18%)
  waiting for transfers between devices  6.88 us (9%)
  local copies, waits for them, and re-layouts  1.24 us (2%)
  between operations  0.8 us (1%)
    all_to_all x1, blocking collectives, per_device(): lax.all_to_all(sent_back, 'gx', split_axis=0, concat_axis=0, tiled=True)  19.2 us
    all_to_all x1, starting transfers between devices, per_device(): lax.all_to_all(sent, 'gx', split_axis=0, concat_axis=0, tiled=True)  16.8 us
    all_to_all x1, waiting for transfers between devices, per_device(): lax.all_to_all(sent, 'gx', split_axis=0, concat_axis=0, tiled=True)  6.86 us
    all_to_all x1, starting transfers between devices, per_device(): lax.all_to_all(faces, ('gy', 'gz'), split_axis=0, concat_axis=0, tiled=True)  6.75 us
    pallas_call x1, Pallas kernels, per_device(): call(pick_kernel, 60, [HBM] * 7, (shape(RUNS, 1, 384), shape(RUNS, WIDTH)...  4.98 us
    ppermute x1, starting transfers between devices, per_device(): swapped = lax.ppermute(swap, 'gx', outside_pairs)  3.86 us
    ppermute x1, starting transfers between devices, per_device(): across = lax.ppermute(across, 'gx', outside_pairs)  3.45 us
    pallas_call x1, Pallas kernels, per_device(): call(final_kernel, 16, [VMEM] * 7, shape(ROWS, WIDTH), VMEM, [], 2 * 256...  3.26 us
  transfers between devices with their start and end apart: 5, of which 1 were waited for; matrix products, arithmetic and copies ran while one was open for 0% of the time, Pallas kernels for 7%

profile of v8, /device:TPU:1, one launch (start us, length us, event | category | flops | bytes accessed | tf_op | source)
XLA Modules:
  0.0 74.4 jit_solution(1352203119238511665)
XLA Ops:
  0.6 5.0 %shard_map.95 = (f32[32,1,384]{2,1,0:T(1,128)}, f32[32,128]{1,0:T(8,128)}, f32[56,128]{1,0:T(8,128)}, f32[16,1,2048]{2,1,0:T(1,128)}, f32[3960,128]{1,0:T(8,128)}, /*index=5*/f32[1400,128]{1,0:T(8,128)}) custom-call(f32[1024,128]{1,0:T(8,128)} %bitcast.14, s32[32,128]{1,0:T(8,128)} %bitcast.19, s32[32,128]{1,0:T(8,128)} %bitcast.17, f32[8,128]{1,0:T(8,128)} %bitcast.21, ...), custom_call_target="tpu_custom_call" | custom-call | flops 2147483648 | bytes 4194304 | tf_op jit(solution)/shard_map/pallas_call | solution.py:459
  5.6 16.8 %all-to-all-start = ((f32[32,1,384]{2,1,0:T(1,128)}), f32[32,1,384]{2,1,0:T(1,128)S(1)}, u32[]{:S(2)}, u32[]{:S(2)}) async-start(f32[32,1,384]{2,1,0:T(1,128)} %get-tuple-element.18), calls=%async_computation | async-start | bytes 98304 | tf_op jit(solution)/shard_map/all_to_all | solution.py:474
  22.4 2.1 %collective-permute-start.1 = (f32[3960,128]{1,0:T(8,128)}, f32[3960,128]{1,0:T(8,128)S(1)}, u32[]{:S(2)}, u32[]{:S(2)}) collective-permute-start(f32[3960,128]{1,0:T(8,128)} %get-tuple-element.24), channel_id=1, source_target_pairs={{0,16},{16,0},{32,48},{48,32},{64,80},{80,64},{96,112},{112,96},{1... | collective-permute-start | bytes 6082568 | tf_op jit(solution)/shard_map/ppermute | solution.py:475
  24.5 3.5 %collective-permute-start = (f32[1400,128]{1,0:T(8,128)}, f32[1400,128]{1,0:T(8,128)S(1)}, u32[]{:S(2)}, u32[]{:S(2)}) collective-permute-start(f32[1400,128]{1,0:T(8,128)} %get-tuple-element.19), channel_id=1, source_target_pairs={{0,496},{16,32},{32,16},{48,64},{64,48},{80,96},{96,80},{112,128},... | collective-permute-start | bytes 2150408 | tf_op jit(solution)/shard_map/ppermute | solution.py:476
  28.0 6.9 %all-to-all-done.arrived = f32[32,1,384]{2,1,0:T(1,128)S(1)} async-done(((f32[32,1,384]{2,1,0:T(1,128)}), f32[32,1,384]{2,1,0:T(1,128)S(1)}, u32[]{:S(2)}, u32[]{:S(2)}) %all-to-all-start) | async-done | bytes 49184 | tf_op jit(solution)/shard_map/all_to_all | solution.py:474
  34.9 6.8 %all-to-all-start.1 = ((f32[16,1,2048]{2,1,0:T(1,128)}), f32[16,1,2048]{2,1,0:T(1,128)S(1)}, u32[]{:S(2)}, u32[]{:S(2)}) async-start(f32[16,1,2048]{2,1,0:T(1,128)} %get-tuple-element.26), calls=%async_computation.1 | async-start | bytes 262144 | tf_op jit(solution)/shard_map/all_to_all | solution.py:477
  41.6 0.4 shard_map.96.added_own
  42.0 0.0 collective-permute-done.across_hbm
  42.1 0.5 shard_map.97
  42.6 1.2 %copy-done = f32[1,8,5,128,128]{4,3,2,1,0:T(8,128)S(1)} copy-done((f32[1,8,5,128,128]{4,3,2,1,0:T(8,128)S(1)}, f32[1,8,5,128,128]{4,3,2,1,0:T(8,128)}, u32[]{:S(2)}) %copy-start) | copy-done | bytes 2621464
  43.8 0.0 copy-done.1
  43.8 0.9 %shard_map.98 = (f32[2,24,128]{2,1,0:T(8,128)S(1)}, f32[8,128]{1,0:T(8,128)S(1)}) custom-call(f32[16,128]{1,0:T(8,128)S(1)} %get-tuple-element.20.added_before, f32[120,128]{1,0:T(8,128)S(1)} %get-tuple-element.21.beside_small, f32[56,128]{1,0:T(8,128)S(1)} %copy-done.1, f32[5120,128]{1,0:T(8,128)S(1)} %bitcast.11, ...), custom_call_target="tpu_custom_call" | custom-call | flops 8388608 | bytes 4194304 | tf_op jit(solution)/shard_map/pallas_call | solution.py:487
  44.7 3.9 %collective-permute-start.2 = (f32[8,128]{1,0:T(8,128)S(1)}, f32[8,128]{1,0:T(8,128)S(1)}, u32[]{:S(2)}, u32[]{:S(2)}) collective-permute-start(f32[8,128]{1,0:T(8,128)S(1)} %get-tuple-element.31), channel_id=1, source_target_pairs={{0,496},{16,32},{32,16},{48,64},{64,48},{80,96},{96,80},{112,128},... | collective-permute-start | bytes 12296 | tf_op jit(solution)/shard_map/ppermute | solution.py:494
  48.6 0.0 collective-permute-done.1.on_chip_hbm
  48.6 2.0 %shard_map.99 = (f32[5,24,128]{2,1,0:T(8,128)S(1)}, f32[5,24,128]{2,1,0:T(8,128)S(1)}, f32[3,24,128]{2,1,0:T(8,128)S(1)}, f32[2,64,128]{2,1,0:T(8,128)S(1)}) custom-call(f32[32,1,384]{2,1,0:T(1,128)S(1)} %all-to-all-done.arrived, f32[16,128]{1,0:T(8,128)S(1)} %get-tuple-element.20.added_before, f32[120,128]{1,0:T(8,128)S(1)} %get-tuple-element.21.beside_small, ...), custom_call_target="tpu_custom_call" | custom-call | flops 16777216 | bytes 6291456 | tf_op jit(solution)/shard_map/pallas_call | solution.py:495
  50.6 0.0 copy-start.2
  50.6 0.0 copy-start.3
  50.6 0.0 copy-start.5
  50.6 0.0 copy-start.6
  50.6 0.0 collective-permute-done.2.swapped
  50.6 1.3 %shard_map.100 = (f32[8,128]{1,0:T(8,128)}, f32[32,1,128]{2,1,0:T(1,128)S(1)}) custom-call(f32[5,24,128]{2,1,0:T(8,128)S(1)} %get-tuple-element.28.state, f32[5,24,128]{2,1,0:T(8,128)S(1)} %get-tuple-element.29.pats, f32[3,24,128]{2,1,0:T(8,128)S(1)} %get-tuple-element.30.inside, f32[8,128]{1,0:T(8,128)S(1)} %collective-permute-done.2.swapped, ...), custom_call_target="tpu_custom_call" | custom-call | flops 8388608 | bytes 3145728 | tf_op jit(solution)/shard_map/pallas_call | solution.py:502
  51.9 0.0 all-to-all-done.1.faces
  51.9 19.2 %all_to_all.15.returned = f32[32,1,128]{2,1,0:T(1,128)S(1)} all-to-all(f32[32,1,128]{2,1,0:T(1,128)S(1)} %get-tuple-element.32), channel_id=1, replica_groups=mesh['gx'=32,'gy'=4,'gz'=4] {'gx'}, dimensions={0} | all-to-all | bytes 32768 | tf_op jit(solution)/shard_map/all_to_all | solution.py:509
  71.1 3.3 %shard_map.101 = f32[1024,128]{1,0:T(8,128)} custom-call(f32[1024,128]{1,0:T(8,128)S(1)} %bitcast.15, s32[1024,128]{1,0:T(8,128)S(1)} %bitcast.16, f32[2,64,128]{2,1,0:T(8,128)S(1)} %get-tuple-element.25.x_faces, f32[16,1,2048]{2,1,0:T(1,128)S(1)} %all-to-all-done.1.faces, s32[32,128]{1,0:T(8,128)S(1)} %bitcast.20, f32[32,128]{1,0:T(8,128)S(1)} %copy-done.6, ...), custom_call_target="tpu_custom_call" | custom-call | flops 2147483648 | bytes 1048576 | tf_op jit(solution)/shard_map/pallas_call | solution.py:511
  (8 shorter events, 0.0 us)
Async XLA Ops:
  0.6 41.0 %copy-start.4 = (s32[32,1,1,128]{3,2,1,0:T(1,128)S(1)}, s32[32,1,1,128]{3,2,1,0:T(1,128)}, u32[]{:S(2)}) copy-start(s32[32,1,1,128]{3,2,1,0:T(1,128)} %param.11) | copy-start | bytes 49156
  5.6 29.2 %all-to-all-start = ((f32[32,1,384]{2,1,0:T(1,128)}), f32[32,1,384]{2,1,0:T(1,128)S(1)}, u32[]{:S(2)}, u32[]{:S(2)}) async-start(f32[32,1,384]{2,1,0:T(1,128)} %get-tuple-element.18), calls=%async_computation | async-start | bytes 98304 | tf_op jit(solution)/shard_map/all_to_all | solution.py:474
  22.4 26.2 %collective-permute-start.1 = (f32[3960,128]{1,0:T(8,128)}, f32[3960,128]{1,0:T(8,128)S(1)}, u32[]{:S(2)}, u32[]{:S(2)}) collective-permute-start(f32[3960,128]{1,0:T(8,128)} %get-tuple-element.24), channel_id=1, source_target_pairs={{0,16},{16,0},{32,48},{48,32},{64,80},{80,64},{96,112},{112,96},{1... | collective-permute-start | bytes 6082568 | tf_op jit(solution)/shard_map/ppermute | solution.py:475
  24.5 17.5 %collective-permute-start = (f32[1400,128]{1,0:T(8,128)}, f32[1400,128]{1,0:T(8,128)S(1)}, u32[]{:S(2)}, u32[]{:S(2)}) collective-permute-start(f32[1400,128]{1,0:T(8,128)} %get-tuple-element.19), channel_id=1, source_target_pairs={{0,496},{16,32},{32,16},{48,64},{64,48},{80,96},{96,80},{112,128},... | collective-permute-start | bytes 2150408 | tf_op jit(solution)/shard_map/ppermute | solution.py:476
  34.9 17.0 %all-to-all-start.1 = ((f32[16,1,2048]{2,1,0:T(1,128)}), f32[16,1,2048]{2,1,0:T(1,128)S(1)}, u32[]{:S(2)}, u32[]{:S(2)}) async-start(f32[16,1,2048]{2,1,0:T(1,128)} %get-tuple-element.26), calls=%async_computation.1 | async-start | bytes 262144 | tf_op jit(solution)/shard_map/all_to_all | solution.py:477
  42.0 1.8 %copy-start = (f32[1,8,5,128,128]{4,3,2,1,0:T(8,128)S(1)}, f32[1,8,5,128,128]{4,3,2,1,0:T(8,128)}, u32[]{:S(2)}) copy-start(f32[1,8,5,128,128]{4,3,2,1,0:T(8,128)} %param.14) | copy-start | bytes 7864324
  42.0 1.8 %copy-start.1 = (f32[56,128]{1,0:T(8,128)S(1)}, f32[56,128]{1,0:T(8,128)}, u32[]{:S(2)}) copy-start(f32[56,128]{1,0:T(8,128)} %get-tuple-element.22.own) | copy-start | bytes 86020
  44.7 5.9 %collective-permute-start.2 = (f32[8,128]{1,0:T(8,128)S(1)}, f32[8,128]{1,0:T(8,128)S(1)}, u32[]{:S(2)}, u32[]{:S(2)}) collective-permute-start(f32[8,128]{1,0:T(8,128)S(1)} %get-tuple-element.31), channel_id=1, source_target_pairs={{0,496},{16,32},{32,16},{48,64},{64,48},{80,96},{96,80},{112,128},... | collective-permute-start | bytes 12296 | tf_op jit(solution)/shard_map/ppermute | solution.py:494
  50.6 20.5 %copy-start.2 = (f32[16,64,128]{2,1,0:T(8,128)S(1)}, f32[16,64,128]{2,1,0:T(8,128)}, u32[]{:S(2)}) copy-start(f32[16,64,128]{2,1,0:T(8,128)} %param.8) | copy-start | bytes 1572868
  50.6 20.5 %copy-start.3 = (s32[16,64,128]{2,1,0:T(8,128)S(1)}, s32[16,64,128]{2,1,0:T(8,128)}, u32[]{:S(2)}) copy-start(s32[16,64,128]{2,1,0:T(8,128)} %param.9) | copy-start | bytes 1572868
  50.6 20.5 %copy-start.5 = (s32[32,1,1,128]{3,2,1,0:T(1,128)S(1)}, s32[32,1,1,128]{3,2,1,0:T(1,128)}, u32[]{:S(2)}) copy-start(s32[32,1,1,128]{3,2,1,0:T(1,128)} %param.10) | copy-start | bytes 49156
  50.6 20.5 %copy-start.6 = (f32[32,128]{1,0:T(8,128)S(1)}, f32[32,128]{1,0:T(8,128)}, u32[]{:S(2)}) copy-start(f32[32,128]{1,0:T(8,128)} %get-tuple-element.27.outgoing) | copy-start | bytes 49156

commit v9 on v8

--- a/solution.py
+++ b/solution.py
@@ -478,11 +478,11 @@
 
     work = [vmem(WIN, WIDTH), vmem(NB, WIN, WIDTH), vmem(WIN, WIDTH)]
     added_own = call(
-        own_run_kernel, 12, [VMEM, VMEM], shape(TILES, WIDTH), VMEM, [], 20 * 10**9, 1 << 16
+        own_run_kernel, 12, [VMEM, VMEM], shape(TILES, WIDTH), VMEM, [], 65 * 10**8, 1 << 16
     )(arrived, dst)
     added_before, beside_small = call(
         beside_run_kernel, 12, [VMEM, ANY, VMEM], (shape(2 * TILES, WIDTH), shape(SMALL, WIDTH)), (VMEM, VMEM), [dma()],
-        10**9, 1 << 16,
+        14 * 10**9, 1 << 16,
     )(arrived, across, added_own)
     products, swap = call(
         wall_edge_kernel, 12,

time: 74.8 us -> 72.7 us (0.972)
  blocking collectives: 19.2 us -> 17.1 us
  starting transfers between devices: 33 us -> 34.3 us
  waiting for transfers between devices: 6.88 us -> 5.6 us
    all_to_all x1, blocking collectives: 19.2 us -> 17.1 us  [per_device(): lax.all_to_all(sent_back, 'gx', split_axis=0, concat_axis=0, tiled=True)]
    all_to_all x1, waiting for transfers between devices: 6.86 us -> 5.57 us  [per_device(): lax.all_to_all(sent, 'gx', split_axis=0, concat_axis=0, tiled=True)]
    ppermute x1, starting transfers between devices: 2.14 us -> 3.35 us  [per_device(): on_chip = lax.ppermute(on_chip, 'gx', inside_pairs)]
where the time goes in v9:
time: 72.7 us; the launch traced here: 72.3 us
  starting transfers between devices  34.3 us (47%)
  blocking collectives  17.1 us (24%)
  Pallas kernels  13.3 us (18%)
  waiting for transfers between devices  5.6 us (8%)
  local copies, waits for them, and re-layouts  1.24 us (2%)
  between operations  0.8 us (1%)
    all_to_all x1, blocking collectives, per_device(): lax.all_to_all(sent_back, 'gx', split_axis=0, concat_axis=0, tiled=True)  17.1 us
    all_to_all x1, starting transfers between devices, per_device(): lax.all_to_all(sent, 'gx', split_axis=0, concat_axis=0, tiled=True)  16.8 us
    all_to_all x1, starting transfers between devices, per_device(): lax.all_to_all(faces, ('gy', 'gz'), split_axis=0, concat_axis=0, tiled=True)  6.75 us
    all_to_all x1, waiting for transfers between devices, per_device(): lax.all_to_all(sent, 'gx', split_axis=0, concat_axis=0, tiled=True)  5.57 us
    pallas_call x1, Pallas kernels, per_device(): call(pick_kernel, 60, [HBM] * 7, (shape(RUNS, 1, 384), shape(RUNS, WIDTH)...  4.98 us
    ppermute x1, starting transfers between devices, per_device(): swapped = lax.ppermute(swap, 'gx', outside_pairs)  3.86 us
    ppermute x1, starting transfers between devices, per_device(): across = lax.ppermute(across, 'gx', outside_pairs)  3.54 us
    ppermute x1, starting transfers between devices, per_device(): on_chip = lax.ppermute(on_chip, 'gx', inside_pairs)  3.35 us
  transfers between devices with their start and end apart: 5, of which 1 were waited for; matrix products, arithmetic and copies ran while one was open for 0% of the time, Pallas kernels for 7%

profile of v9, /device:TPU:1, one launch (start us, length us, event | category | flops | bytes accessed | tf_op | source)
XLA Modules:
  0.0 72.3 jit_solution(6543826824977640702)
XLA Ops:
  0.6 5.0 %shard_map.95 = (f32[32,1,384]{2,1,0:T(1,128)}, f32[32,128]{1,0:T(8,128)}, f32[56,128]{1,0:T(8,128)}, f32[16,1,2048]{2,1,0:T(1,128)}, f32[3960,128]{1,0:T(8,128)}, /*index=5*/f32[1400,128]{1,0:T(8,128)}) custom-call(f32[1024,128]{1,0:T(8,128)} %bitcast.14, s32[32,128]{1,0:T(8,128)} %bitcast.19, s32[32,128]{1,0:T(8,128)} %bitcast.17, f32[8,128]{1,0:T(8,128)} %bitcast.21, ...), custom_call_target="tpu_custom_call" | custom-call | flops 2147483648 | bytes 4194304 | tf_op jit(solution)/shard_map/pallas_call | solution.py:459
  5.6 16.8 %all-to-all-start = ((f32[32,1,384]{2,1,0:T(1,128)}), f32[32,1,384]{2,1,0:T(1,128)S(1)}, u32[]{:S(2)}, u32[]{:S(2)}) async-start(f32[32,1,384]{2,1,0:T(1,128)} %get-tuple-element.18), calls=%async_computation | async-start | bytes 98304 | tf_op jit(solution)/shard_map/all_to_all | solution.py:474
  22.4 3.5 %collective-permute-start = (f32[1400,128]{1,0:T(8,128)}, f32[1400,128]{1,0:T(8,128)S(1)}, u32[]{:S(2)}, u32[]{:S(2)}) collective-permute-start(f32[1400,128]{1,0:T(8,128)} %get-tuple-element.19), channel_id=1, source_target_pairs={{0,496},{16,32},{32,16},{48,64},{64,48},{80,96},{96,80},{112,128},... | collective-permute-start | bytes 2150408 | tf_op jit(solution)/shard_map/ppermute | solution.py:476
  25.9 3.4 %collective-permute-start.1 = (f32[3960,128]{1,0:T(8,128)}, f32[3960,128]{1,0:T(8,128)S(1)}, u32[]{:S(2)}, u32[]{:S(2)}) collective-permute-start(f32[3960,128]{1,0:T(8,128)} %get-tuple-element.24), channel_id=1, source_target_pairs={{0,16},{16,0},{32,48},{48,32},{64,80},{80,64},{96,112},{112,96},{1... | collective-permute-start | bytes 6082568 | tf_op jit(solution)/shard_map/ppermute | solution.py:475
  29.3 5.6 %all-to-all-done.arrived = f32[32,1,384]{2,1,0:T(1,128)S(1)} async-done(((f32[32,1,384]{2,1,0:T(1,128)}), f32[32,1,384]{2,1,0:T(1,128)S(1)}, u32[]{:S(2)}, u32[]{:S(2)}) %all-to-all-start) | async-done | bytes 49184 | tf_op jit(solution)/shard_map/all_to_all | solution.py:474
  34.9 6.8 %all-to-all-start.1 = ((f32[16,1,2048]{2,1,0:T(1,128)}), f32[16,1,2048]{2,1,0:T(1,128)S(1)}, u32[]{:S(2)}, u32[]{:S(2)}) async-start(f32[16,1,2048]{2,1,0:T(1,128)} %get-tuple-element.26), calls=%async_computation.1 | async-start | bytes 262144 | tf_op jit(solution)/shard_map/all_to_all | solution.py:477
  41.6 0.4 shard_map.96.added_own
  42.0 0.0 collective-permute-done.across_hbm
  42.1 0.5 shard_map.97
  42.6 1.2 %copy-done = f32[1,8,5,128,128]{4,3,2,1,0:T(8,128)S(1)} copy-done((f32[1,8,5,128,128]{4,3,2,1,0:T(8,128)S(1)}, f32[1,8,5,128,128]{4,3,2,1,0:T(8,128)}, u32[]{:S(2)}) %copy-start) | copy-done | bytes 2621464
  43.8 0.0 copy-done.1
  43.8 0.9 %shard_map.98 = (f32[2,24,128]{2,1,0:T(8,128)S(1)}, f32[8,128]{1,0:T(8,128)S(1)}) custom-call(f32[16,128]{1,0:T(8,128)S(1)} %get-tuple-element.20.added_before, f32[120,128]{1,0:T(8,128)S(1)} %get-tuple-element.21.beside_small, f32[56,128]{1,0:T(8,128)S(1)} %copy-done.1, f32[5120,128]{1,0:T(8,128)S(1)} %bitcast.11, ...), custom_call_target="tpu_custom_call" | custom-call | flops 8388608 | bytes 4194304 | tf_op jit(solution)/shard_map/pallas_call | solution.py:487
  44.7 3.9 %collective-permute-start.2 = (f32[8,128]{1,0:T(8,128)S(1)}, f32[8,128]{1,0:T(8,128)S(1)}, u32[]{:S(2)}, u32[]{:S(2)}) collective-permute-start(f32[8,128]{1,0:T(8,128)S(1)} %get-tuple-element.31), channel_id=1, source_target_pairs={{0,496},{16,32},{32,16},{48,64},{64,48},{80,96},{96,80},{112,128},... | collective-permute-start | bytes 12296 | tf_op jit(solution)/shard_map/ppermute | solution.py:494
  48.6 0.0 collective-permute-done.1.on_chip_hbm
  48.6 2.0 %shard_map.99 = (f32[5,24,128]{2,1,0:T(8,128)S(1)}, f32[5,24,128]{2,1,0:T(8,128)S(1)}, f32[3,24,128]{2,1,0:T(8,128)S(1)}, f32[2,64,128]{2,1,0:T(8,128)S(1)}) custom-call(f32[32,1,384]{2,1,0:T(1,128)S(1)} %all-to-all-done.arrived, f32[16,128]{1,0:T(8,128)S(1)} %get-tuple-element.20.added_before, f32[120,128]{1,0:T(8,128)S(1)} %get-tuple-element.21.beside_small, ...), custom_call_target="tpu_custom_call" | custom-call | flops 16777216 | bytes 6291456 | tf_op jit(solution)/shard_map/pallas_call | solution.py:495
  50.6 0.0 copy-start.2
  50.6 0.0 copy-start.3
  50.6 0.0 copy-start.5
  50.6 0.0 collective-permute-done.2.swapped
  50.6 1.3 %shard_map.100 = (f32[8,128]{1,0:T(8,128)}, f32[32,1,128]{2,1,0:T(1,128)S(1)}) custom-call(f32[5,24,128]{2,1,0:T(8,128)S(1)} %get-tuple-element.28.state, f32[5,24,128]{2,1,0:T(8,128)S(1)} %get-tuple-element.29.pats, f32[3,24,128]{2,1,0:T(8,128)S(1)} %get-tuple-element.30.inside, f32[8,128]{1,0:T(8,128)S(1)} %collective-permute-done.2.swapped, ...), custom_call_target="tpu_custom_call" | custom-call | flops 8388608 | bytes 3145728 | tf_op jit(solution)/shard_map/pallas_call | solution.py:502
  51.9 0.0 all-to-all-done.1.faces
  51.9 17.1 %all_to_all.15.returned = f32[32,1,128]{2,1,0:T(1,128)S(1)} all-to-all(f32[32,1,128]{2,1,0:T(1,128)S(1)} %get-tuple-element.32), channel_id=1, replica_groups=mesh['gx'=32,'gy'=4,'gz'=4] {'gx'}, dimensions={0} | all-to-all | bytes 32768 | tf_op jit(solution)/shard_map/all_to_all | solution.py:509
  69.0 0.0 copy-done.6
  69.0 3.3 %shard_map.101 = f32[1024,128]{1,0:T(8,128)} custom-call(f32[1024,128]{1,0:T(8,128)S(1)} %bitcast.15, s32[1024,128]{1,0:T(8,128)S(1)} %bitcast.16, f32[2,64,128]{2,1,0:T(8,128)S(1)} %get-tuple-element.25.x_faces, f32[16,1,2048]{2,1,0:T(1,128)S(1)} %all-to-all-done.1.faces, s32[32,128]{1,0:T(8,128)S(1)} %bitcast.20, f32[32,128]{1,0:T(8,128)S(1)} %copy-done.6, ...), custom_call_target="tpu_custom_call" | custom-call | flops 2147483648 | bytes 1048576 | tf_op jit(solution)/shard_map/pallas_call | solution.py:511
  (8 shorter events, 0.0 us)
Async XLA Ops:
  0.6 41.0 %copy-start.4 = (s32[32,1,1,128]{3,2,1,0:T(1,128)S(1)}, s32[32,1,1,128]{3,2,1,0:T(1,128)}, u32[]{:S(2)}) copy-start(s32[32,1,1,128]{3,2,1,0:T(1,128)} %param.11) | copy-start | bytes 49156
  5.6 29.2 %all-to-all-start = ((f32[32,1,384]{2,1,0:T(1,128)}), f32[32,1,384]{2,1,0:T(1,128)S(1)}, u32[]{:S(2)}, u32[]{:S(2)}) async-start(f32[32,1,384]{2,1,0:T(1,128)} %get-tuple-element.18), calls=%async_computation | async-start | bytes 98304 | tf_op jit(solution)/shard_map/all_to_all | solution.py:474
  22.4 19.7 %collective-permute-start = (f32[1400,128]{1,0:T(8,128)}, f32[1400,128]{1,0:T(8,128)S(1)}, u32[]{:S(2)}, u32[]{:S(2)}) collective-permute-start(f32[1400,128]{1,0:T(8,128)} %get-tuple-element.19), channel_id=1, source_target_pairs={{0,496},{16,32},{32,16},{48,64},{64,48},{80,96},{96,80},{112,128},... | collective-permute-start | bytes 2150408 | tf_op jit(solution)/shard_map/ppermute | solution.py:476
  25.9 22.7 %collective-permute-start.1 = (f32[3960,128]{1,0:T(8,128)}, f32[3960,128]{1,0:T(8,128)S(1)}, u32[]{:S(2)}, u32[]{:S(2)}) collective-permute-start(f32[3960,128]{1,0:T(8,128)} %get-tuple-element.24), channel_id=1, source_target_pairs={{0,16},{16,0},{32,48},{48,32},{64,80},{80,64},{96,112},{112,96},{1... | collective-permute-start | bytes 6082568 | tf_op jit(solution)/shard_map/ppermute | solution.py:475
  34.9 17.1 %all-to-all-start.1 = ((f32[16,1,2048]{2,1,0:T(1,128)}), f32[16,1,2048]{2,1,0:T(1,128)S(1)}, u32[]{:S(2)}, u32[]{:S(2)}) async-start(f32[16,1,2048]{2,1,0:T(1,128)} %get-tuple-element.26), calls=%async_computation.1 | async-start | bytes 262144 | tf_op jit(solution)/shard_map/all_to_all | solution.py:477
  42.0 1.8 %copy-start = (f32[1,8,5,128,128]{4,3,2,1,0:T(8,128)S(1)}, f32[1,8,5,128,128]{4,3,2,1,0:T(8,128)}, u32[]{:S(2)}) copy-start(f32[1,8,5,128,128]{4,3,2,1,0:T(8,128)} %param.14) | copy-start | bytes 7864324
  42.0 1.8 %copy-start.1 = (f32[56,128]{1,0:T(8,128)S(1)}, f32[56,128]{1,0:T(8,128)}, u32[]{:S(2)}) copy-start(f32[56,128]{1,0:T(8,128)} %get-tuple-element.22.own) | copy-start | bytes 86020
  44.7 5.9 %collective-permute-start.2 = (f32[8,128]{1,0:T(8,128)S(1)}, f32[8,128]{1,0:T(8,128)S(1)}, u32[]{:S(2)}, u32[]{:S(2)}) collective-permute-start(f32[8,128]{1,0:T(8,128)S(1)} %get-tuple-element.31), channel_id=1, source_target_pairs={{0,496},{16,32},{32,16},{48,64},{64,48},{80,96},{96,80},{112,128},... | collective-permute-start | bytes 12296 | tf_op jit(solution)/shard_map/ppermute | solution.py:494
  50.6 18.5 %copy-start.2 = (f32[16,64,128]{2,1,0:T(8,128)S(1)}, f32[16,64,128]{2,1,0:T(8,128)}, u32[]{:S(2)}) copy-start(f32[16,64,128]{2,1,0:T(8,128)} %param.8) | copy-start | bytes 1572868
  50.6 18.4 %copy-start.3 = (s32[16,64,128]{2,1,0:T(8,128)S(1)}, s32[16,64,128]{2,1,0:T(8,128)}, u32[]{:S(2)}) copy-start(s32[16,64,128]{2,1,0:T(8,128)} %param.9) | copy-start | bytes 1572868
  50.6 18.4 %copy-start.5 = (s32[32,1,1,128]{3,2,1,0:T(1,128)S(1)}, s32[32,1,1,128]{3,2,1,0:T(1,128)}, u32[]{:S(2)}) copy-start(s32[32,1,1,128]{3,2,1,0:T(1,128)} %param.10) | copy-start | bytes 49156
  50.6 18.4 %copy-start.6 = (f32[32,128]{1,0:T(8,128)S(1)}, f32[32,128]{1,0:T(8,128)}, u32[]{:S(2)}) copy-start(f32[32,128]{1,0:T(8,128)} %get-tuple-element.27.outgoing) | copy-start | bytes 49156

commit v10 on v9

--- a/solution.py
+++ b/solution.py
@@ -66,8 +66,8 @@
 
 def pick_kernel(
     fluid_hbm, src_hbm, dst_hbm, old_hbm, diag_hbm, pattern_hbm, blocks_hbm,
-    sent, outgoing, own, faces, on_chip_hbm, across_hbm,
-    fluid, src, dst, pattern, table, staged_in, staged_out, sems,
+    sent, outgoing, own, faces_hbm, on_chip_hbm, across_hbm,
+    fluid, src, dst, pattern, table, staged_in, staged_out, faces, sems,
 ):
     me = lax.axis_index("gx")
     parity = lax.rem(me, 2)
@@ -96,8 +96,8 @@
         table[0:128, 128 * block : 128 * block + 128] = high
         table[128:256, 128 * block : 128 * block + 128] = low
         at = slice(128 * block, 128 * block + 128)
-        faces[before_z, :, at] = turned[0:1, :]
-        faces[after_z, :, at] = turned[127:128, :]
+        faces[2, :, at] = turned[0:1, :]
+        faces[3, :, at] = turned[127:128, :]
     for each in small:
         each.wait()
     own[0:32, :] = dst[...].astype(F32)
@@ -115,8 +115,12 @@
     after_y, before_y = lax.rem(y + 1, 4) * 4 + z, lax.rem(y + 3, 4) * 4 + z
     for slab in range(16):
         at = slice(128 * slab, 128 * slab + 128)
-        faces[before_y, :, at] = fluid[64 * slab : 64 * slab + 1, :]
-        faces[after_y, :, at] = fluid[64 * slab + 63 : 64 * slab + 64, :]
+        faces[0, :, at] = fluid[64 * slab : 64 * slab + 1, :]
+        faces[1, :, at] = fluid[64 * slab + 63 : 64 * slab + 64, :]
+    saves = [
+        copy(faces.at[index], faces_hbm.at[place], 19 + index)
+        for index, place in enumerate((before_y, after_y, before_z, after_z))
+    ]
     load_src.wait()
     group = 4
     for start in range(0, RUNS, group):
@@ -137,7 +141,7 @@
             sent[r ^ 1, :, 128:256] = mine
             beside = (r + 1) % RUNS if r % 2 else (r - 1) % RUNS
             sent[beside, :, 256:384] = mine
-    for each in (inside, outside):
+    for each in (inside, outside, *saves):
         each.wait()
 
 
@@ -463,10 +467,10 @@
             shape(RUNS, 1, 384), shape(RUNS, WIDTH), shape(56, WIDTH), shape(16, 1, 2048),
             shape(in_rows, WIDTH), shape(out_rows, WIDTH),
         ),
-        (VMEM, VMEM, VMEM, VMEM, HBM, HBM),
+        (VMEM, VMEM, VMEM, HBM, HBM, HBM),
         [
             vmem(ROWS, WIDTH), vmem(RUNS, WIDTH, kind=I32), vmem(RUNS, WIDTH, kind=I32), vmem(NB, 1, TILES, kind=I32),
-            vmem(256, ROWS, kind=BF16), vmem(in_rows, WIDTH), vmem(out_rows, WIDTH), dma(19),
+            vmem(256, ROWS, kind=BF16), vmem(in_rows, WIDTH), vmem(out_rows, WIDTH), vmem(4, 1, 2048), dma(23),
         ],
         2 * 256 * 1024 * 4096, 1 << 22,
     )(fluid, src, dst, solid_old[0], solid_diag[0], jnp.transpose(pattern, (2, 0, 1)), own_blocks)

time: 72.7 us -> 72.7 us (level)
  no operation moved by 1% of the time
where the time goes in v10:
time: 72.7 us; the launch traced here: 72.3 us
  starting transfers between devices  34.3 us (47%)
  blocking collectives  17.1 us (24%)
  Pallas kernels  13.3 us (18%)
  waiting for transfers between devices  5.6 us (8%)
  local copies, waits for them, and re-layouts  1.24 us (2%)
  between operations  0.8 us (1%)
    all_to_all x1, blocking collectives, per_device(): lax.all_to_all(sent_back, 'gx', split_axis=0, concat_axis=0, tiled=True)  17.1 us
    all_to_all x1, starting transfers between devices, per_device(): lax.all_to_all(sent, 'gx', split_axis=0, concat_axis=0, tiled=True)  16.8 us
    all_to_all x1, starting transfers between devices, per_device(): lax.all_to_all(faces, ('gy', 'gz'), split_axis=0, concat_axis=0, tiled=True)  6.76 us
    all_to_all x1, waiting for transfers between devices, per_device(): lax.all_to_all(sent, 'gx', split_axis=0, concat_axis=0, tiled=True)  5.57 us
    pallas_call x1, Pallas kernels, per_device(): call(pick_kernel, 60, [HBM] * 7, (shape(RUNS, 1, 384), shape(RUNS, WIDTH)...  4.98 us
    ppermute x1, starting transfers between devices, per_device(): swapped = lax.ppermute(swap, 'gx', outside_pairs)  3.86 us
    ppermute x1, starting transfers between devices, per_device(): across = lax.ppermute(across, 'gx', outside_pairs)  3.54 us
    ppermute x1, starting transfers between devices, per_device(): on_chip = lax.ppermute(on_chip, 'gx', inside_pairs)  3.35 us
  transfers between devices with their start and end apart: 5, of which 1 were waited for; matrix products, arithmetic and copies ran while one was open for 0% of the time, Pallas kernels for 7%

profile of v10, /device:TPU:1, one launch (start us, length us, event | category | flops | bytes accessed | tf_op | source)
XLA Modules:
  0.0 72.3 jit_solution(3967174676908127184)
XLA Ops:
  0.6 0.0 copy-start.4
  0.6 5.0 %shard_map.95 = (f32[32,1,384]{2,1,0:T(1,128)}, f32[32,128]{1,0:T(8,128)}, f32[56,128]{1,0:T(8,128)}, f32[16,1,2048]{2,1,0:T(1,128)}, f32[3960,128]{1,0:T(8,128)}, /*index=5*/f32[1400,128]{1,0:T(8,128)}) custom-call(f32[1024,128]{1,0:T(8,128)} %bitcast.14, s32[32,128]{1,0:T(8,128)} %bitcast.19, s32[32,128]{1,0:T(8,128)} %bitcast.17, f32[8,128]{1,0:T(8,128)} %bitcast.21, ...), custom_call_target="tpu_custom_call" | custom-call | flops 2147483648 | bytes 4194304 | tf_op jit(solution)/shard_map/pallas_call | solution.py:463
  5.6 16.8 %all-to-all-start = ((f32[32,1,384]{2,1,0:T(1,128)}), f32[32,1,384]{2,1,0:T(1,128)S(1)}, u32[]{:S(2)}, u32[]{:S(2)}) async-start(f32[32,1,384]{2,1,0:T(1,128)} %get-tuple-element.18), calls=%async_computation | async-start | bytes 98304 | tf_op jit(solution)/shard_map/all_to_all | solution.py:478
  22.4 3.5 %collective-permute-start = (f32[1400,128]{1,0:T(8,128)}, f32[1400,128]{1,0:T(8,128)S(1)}, u32[]{:S(2)}, u32[]{:S(2)}) collective-permute-start(f32[1400,128]{1,0:T(8,128)} %get-tuple-element.19), channel_id=1, source_target_pairs={{0,496},{16,32},{32,16},{48,64},{64,48},{80,96},{96,80},{112,128},... | collective-permute-start | bytes 2150408 | tf_op jit(solution)/shard_map/ppermute | solution.py:480
  25.9 3.4 %collective-permute-start.1 = (f32[3960,128]{1,0:T(8,128)}, f32[3960,128]{1,0:T(8,128)S(1)}, u32[]{:S(2)}, u32[]{:S(2)}) collective-permute-start(f32[3960,128]{1,0:T(8,128)} %get-tuple-element.24), channel_id=1, source_target_pairs={{0,16},{16,0},{32,48},{48,32},{64,80},{80,64},{96,112},{112,96},{1... | collective-permute-start | bytes 6082568 | tf_op jit(solution)/shard_map/ppermute | solution.py:479
  29.3 5.6 %all-to-all-done.arrived = f32[32,1,384]{2,1,0:T(1,128)S(1)} async-done(((f32[32,1,384]{2,1,0:T(1,128)}), f32[32,1,384]{2,1,0:T(1,128)S(1)}, u32[]{:S(2)}, u32[]{:S(2)}) %all-to-all-start) | async-done | bytes 49184 | tf_op jit(solution)/shard_map/all_to_all | solution.py:478
  34.9 6.8 %all-to-all-start.1 = ((f32[16,1,2048]{2,1,0:T(1,128)}), f32[16,1,2048]{2,1,0:T(1,128)S(1)}, u32[]{:S(2)}, u32[]{:S(2)}) async-start(f32[16,1,2048]{2,1,0:T(1,128)} %get-tuple-element.26), calls=%async_computation.1 | async-start | bytes 262144 | tf_op jit(solution)/shard_map/all_to_all | solution.py:481
  41.6 0.4 shard_map.96.added_own
  42.0 0.0 collective-permute-done.across_hbm
  42.1 0.5 shard_map.97
  42.6 1.2 %copy-done = f32[1,8,5,128,128]{4,3,2,1,0:T(8,128)S(1)} copy-done((f32[1,8,5,128,128]{4,3,2,1,0:T(8,128)S(1)}, f32[1,8,5,128,128]{4,3,2,1,0:T(8,128)}, u32[]{:S(2)}) %copy-start) | copy-done | bytes 2621464
  43.8 0.9 %shard_map.98 = (f32[2,24,128]{2,1,0:T(8,128)S(1)}, f32[8,128]{1,0:T(8,128)S(1)}) custom-call(f32[16,128]{1,0:T(8,128)S(1)} %get-tuple-element.20.added_before, f32[120,128]{1,0:T(8,128)S(1)} %get-tuple-element.21.beside_small, f32[56,128]{1,0:T(8,128)S(1)} %copy-done.1, f32[5120,128]{1,0:T(8,128)S(1)} %bitcast.11, ...), custom_call_target="tpu_custom_call" | custom-call | flops 8388608 | bytes 4194304 | tf_op jit(solution)/shard_map/pallas_call | solution.py:491
  44.7 3.9 %collective-permute-start.2 = (f32[8,128]{1,0:T(8,128)S(1)}, f32[8,128]{1,0:T(8,128)S(1)}, u32[]{:S(2)}, u32[]{:S(2)}) collective-permute-start(f32[8,128]{1,0:T(8,128)S(1)} %get-tuple-element.31), channel_id=1, source_target_pairs={{0,496},{16,32},{32,16},{48,64},{64,48},{80,96},{96,80},{112,128},... | collective-permute-start | bytes 12296 | tf_op jit(solution)/shard_map/ppermute | solution.py:498
  48.6 0.0 collective-permute-done.1.on_chip_hbm
  48.6 2.0 %shard_map.99 = (f32[5,24,128]{2,1,0:T(8,128)S(1)}, f32[5,24,128]{2,1,0:T(8,128)S(1)}, f32[3,24,128]{2,1,0:T(8,128)S(1)}, f32[2,64,128]{2,1,0:T(8,128)S(1)}) custom-call(f32[32,1,384]{2,1,0:T(1,128)S(1)} %all-to-all-done.arrived, f32[16,128]{1,0:T(8,128)S(1)} %get-tuple-element.20.added_before, f32[120,128]{1,0:T(8,128)S(1)} %get-tuple-element.21.beside_small, ...), custom_call_target="tpu_custom_call" | custom-call | flops 16777216 | bytes 6291456 | tf_op jit(solution)/shard_map/pallas_call | solution.py:499
  50.6 0.0 copy-start.2
  50.6 0.0 copy-start.3
  50.6 0.0 copy-start.5
  50.6 0.0 collective-permute-done.2.swapped
  50.6 1.3 %shard_map.100 = (f32[8,128]{1,0:T(8,128)}, f32[32,1,128]{2,1,0:T(1,128)S(1)}) custom-call(f32[5,24,128]{2,1,0:T(8,128)S(1)} %get-tuple-element.28.state, f32[5,24,128]{2,1,0:T(8,128)S(1)} %get-tuple-element.29.pats, f32[3,24,128]{2,1,0:T(8,128)S(1)} %get-tuple-element.30.inside, f32[8,128]{1,0:T(8,128)S(1)} %collective-permute-done.2.swapped, ...), custom_call_target="tpu_custom_call" | custom-call | flops 8388608 | bytes 3145728 | tf_op jit(solution)/shard_map/pallas_call | solution.py:506
  51.9 0.0 all-to-all-done.1.faces
  51.9 17.1 %all_to_all.15.returned = f32[32,1,128]{2,1,0:T(1,128)S(1)} all-to-all(f32[32,1,128]{2,1,0:T(1,128)S(1)} %get-tuple-element.32), channel_id=1, replica_groups=mesh['gx'=32,'gy'=4,'gz'=4] {'gx'}, dimensions={0} | all-to-all | bytes 32768 | tf_op jit(solution)/shard_map/all_to_all | solution.py:513
  69.0 0.0 copy-done.6
  69.0 3.3 %shard_map.101 = f32[1024,128]{1,0:T(8,128)} custom-call(f32[1024,128]{1,0:T(8,128)S(1)} %bitcast.15, s32[1024,128]{1,0:T(8,128)S(1)} %bitcast.16, f32[2,64,128]{2,1,0:T(8,128)S(1)} %get-tuple-element.25.x_faces, f32[16,1,2048]{2,1,0:T(1,128)S(1)} %all-to-all-done.1.faces, s32[32,128]{1,0:T(8,128)S(1)} %bitcast.20, f32[32,128]{1,0:T(8,128)S(1)} %copy-done.6, ...), custom_call_target="tpu_custom_call" | custom-call | flops 2147483648 | bytes 1048576 | tf_op jit(solution)/shard_map/pallas_call | solution.py:515
  (8 shorter events, 0.0 us)
Async XLA Ops:
  0.6 41.0 %copy-start.4 = (s32[32,1,1,128]{3,2,1,0:T(1,128)S(1)}, s32[32,1,1,128]{3,2,1,0:T(1,128)}, u32[]{:S(2)}) copy-start(s32[32,1,1,128]{3,2,1,0:T(1,128)} %param.11) | copy-start | bytes 49156
  5.6 29.2 %all-to-all-start = ((f32[32,1,384]{2,1,0:T(1,128)}), f32[32,1,384]{2,1,0:T(1,128)S(1)}, u32[]{:S(2)}, u32[]{:S(2)}) async-start(f32[32,1,384]{2,1,0:T(1,128)} %get-tuple-element.18), calls=%async_computation | async-start | bytes 98304 | tf_op jit(solution)/shard_map/all_to_all | solution.py:478
  22.4 19.7 %collective-permute-start = (f32[1400,128]{1,0:T(8,128)}, f32[1400,128]{1,0:T(8,128)S(1)}, u32[]{:S(2)}, u32[]{:S(2)}) collective-permute-start(f32[1400,128]{1,0:T(8,128)} %get-tuple-element.19), channel_id=1, source_target_pairs={{0,496},{16,32},{32,16},{48,64},{64,48},{80,96},{96,80},{112,128},... | collective-permute-start | bytes 2150408 | tf_op jit(solution)/shard_map/ppermute | solution.py:480
  25.9 22.7 %collective-permute-start.1 = (f32[3960,128]{1,0:T(8,128)}, f32[3960,128]{1,0:T(8,128)S(1)}, u32[]{:S(2)}, u32[]{:S(2)}) collective-permute-start(f32[3960,128]{1,0:T(8,128)} %get-tuple-element.24), channel_id=1, source_target_pairs={{0,16},{16,0},{32,48},{48,32},{64,80},{80,64},{96,112},{112,96},{1... | collective-permute-start | bytes 6082568 | tf_op jit(solution)/shard_map/ppermute | solution.py:479
  34.9 17.1 %all-to-all-start.1 = ((f32[16,1,2048]{2,1,0:T(1,128)}), f32[16,1,2048]{2,1,0:T(1,128)S(1)}, u32[]{:S(2)}, u32[]{:S(2)}) async-start(f32[16,1,2048]{2,1,0:T(1,128)} %get-tuple-element.26), calls=%async_computation.1 | async-start | bytes 262144 | tf_op jit(solution)/shard_map/all_to_all | solution.py:481
  42.0 1.8 %copy-start = (f32[1,8,5,128,128]{4,3,2,1,0:T(8,128)S(1)}, f32[1,8,5,128,128]{4,3,2,1,0:T(8,128)}, u32[]{:S(2)}) copy-start(f32[1,8,5,128,128]{4,3,2,1,0:T(8,128)} %param.14) | copy-start | bytes 7864324
  42.0 1.8 %copy-start.1 = (f32[56,128]{1,0:T(8,128)S(1)}, f32[56,128]{1,0:T(8,128)}, u32[]{:S(2)}) copy-start(f32[56,128]{1,0:T(8,128)} %get-tuple-element.22.own) | copy-start | bytes 86020
  44.7 5.9 %collective-permute-start.2 = (f32[8,128]{1,0:T(8,128)S(1)}, f32[8,128]{1,0:T(8,128)S(1)}, u32[]{:S(2)}, u32[]{:S(2)}) collective-permute-start(f32[8,128]{1,0:T(8,128)S(1)} %get-tuple-element.31), channel_id=1, source_target_pairs={{0,496},{16,32},{32,16},{48,64},{64,48},{80,96},{96,80},{112,128},... | collective-permute-start | bytes 12296 | tf_op jit(solution)/shard_map/ppermute | solution.py:498
  50.6 18.4 %copy-start.2 = (f32[16,64,128]{2,1,0:T(8,128)S(1)}, f32[16,64,128]{2,1,0:T(8,128)}, u32[]{:S(2)}) copy-start(f32[16,64,128]{2,1,0:T(8,128)} %param.8) | copy-start | bytes 1572868
  50.6 18.4 %copy-start.3 = (s32[16,64,128]{2,1,0:T(8,128)S(1)}, s32[16,64,128]{2,1,0:T(8,128)}, u32[]{:S(2)}) copy-start(s32[16,64,128]{2,1,0:T(8,128)} %param.9) | copy-start | bytes 1572868
  50.6 18.4 %copy-start.5 = (s32[32,1,1,128]{3,2,1,0:T(1,128)S(1)}, s32[32,1,1,128]{3,2,1,0:T(1,128)}, u32[]{:S(2)}) copy-start(s32[32,1,1,128]{3,2,1,0:T(1,128)} %param.10) | copy-start | bytes 49156
  50.6 18.4 %copy-start.6 = (f32[32,128]{1,0:T(8,128)S(1)}, f32[32,128]{1,0:T(8,128)}, u32[]{:S(2)}) copy-start(f32[32,128]{1,0:T(8,128)} %get-tuple-element.27.outgoing) | copy-start | bytes 49156
